TPU v7x, 32 devices: a whole 2x2x4 slice. The times are simulated.
32 devices in a mesh: parts: 2 (over y), row: 4 (over z), col: 2 (over core), dp: 2 (over x).
Axes of the slice: x: 2, y: 2, z: 4, core: 2. Of those that a mesh axis runs over, the one named last changes fastest.
Arguments:
- activations: bfloat16 [1280, 4096], P(('parts', 'dp'), ('row', 'col')), parts along dimension 0, may hold values from -6 to 6
- gradients: bfloat16 [1280, 14336], P(('parts', 'dp'), ('row', 'col')), parts along dimension 0, may hold values from -0.59765625 to 0.59765625
- q_act: bfloat16 [4096, 4096], P(None, ('row', 'col')), may hold values from -0.09375 to 0.09375
- q_grad: bfloat16 [14336, 2, 3584], P(None, 'col', 'row'), may hold values from -0.046875 to 0.046875
- lengths: int32 [4, 3], P(('parts', 'dp')), parts along dimension 0, may hold values from 1 to 160, 320 in all within a row
Outputs:
- correction: float32 [8192, 7168], P(('parts', 'row'), ('col', 'dp')), parts along dimension 0
There are 2 independent parts, one for each index of `parts`. A program takes and returns all parts, laid end to end along the dimension named above; an argument that names none is the same for every part. Nothing has to cross between parts.
Inputs may be any that keep to these rules, and one draw needn't show every extreme that they name: Each row holds the lengths of 3 examples that fill one index of dp's 320 tokens; the longest in each row is 160.
All inputs are finite; a program needn't handle non-finite values.
Results may differ from a plain program's by a relative error of at most 0.0033.
Values may be sent and summed in bfloat16 or wider, within the bound.
No kernel may reach another device: no remote copies, remote signals or barrier semaphores. Data moves between devices by JAX's collectives and lax.ppermute only.
A program may use at most 128 MiB of HBM per device.

v0:
```python
import jax
import jax.numpy as jnp
from jax import lax
from jax.sharding import PartitionSpec as P


def fold_with(basis, section):
    return jnp.dot(section, basis, preferred_element_type=jnp.float32)


def on_device(activations, gradients, q_act, q_grad, lengths):
    tokens_here = activations.shape[0]
    basis_grad = q_grad.reshape(q_grad.shape[0], q_grad.shape[2])
    examples_all = lengths.shape[1] * lax.axis_size("dp")
    rotated = fold_with(
        q_act, lax.all_gather(activations, ("row", "col"), axis=1, tiled=True)
    ).astype(jnp.bfloat16)
    rotated = lax.all_gather(rotated, "col", axis=1, tiled=True)
    rotated_g = fold_with(basis_grad, lax.all_gather(gradients, ("row", "col"), axis=1, tiled=True))
    rotated_g = lax.all_gather(rotated_g.astype(jnp.bfloat16), "row", axis=1, tiled=True)
    lengths_row = lengths[0]
    endings = jnp.cumsum(lengths_row)
    beginnings = endings - lengths_row
    positions = jnp.arange(tokens_here, dtype=jnp.int32)
    member = (
        (positions[:, None] >= beginnings[None, :]) & (positions[:, None] < endings[None, :])
    ).astype(jnp.bfloat16)
    masked = rotated[None, :, :] * member.T[:, :, None]
    products = jnp.einsum("etk,tj->ekj", masked, rotated_g, preferred_element_type=jnp.float32)
    partial_sum = jnp.sum(products * products, axis=0) / examples_all
    return lax.psum_scatter(partial_sum, "dp", scatter_dimension=1, tiled=True)


def solution(mesh):
    return jax.shard_map(
        on_device,
        mesh=mesh,
        in_specs=(
            P(("parts", "dp"), ("row", "col")),
            P(("parts", "dp"), ("row", "col")),
            P(None, ("row", "col")),
            P(None, "col", "row"),
            P(("parts", "dp"), None),
        ),
        out_specs=P(("parts", "row"), ("col", "dp")),
        check_vma=False,
    )
```

profile of v0, /device:TPU:0, one launch (start us, length us, event | category | flops | bytes accessed | tf_op | source)
XLA Modules:
  0.0 389.4 jit_solution(17217954655340704916)
XLA Ops:
  6.5 0.0 all-gather.6.cloned.1.call-start
  6.5 0.7 all-gather.6.cloned.1.call-update
  7.3 0.0 all-gather.4.cloned.1.call-start
  7.3 0.7 all-gather.4.cloned.1.call-update
  8.0 0.0 copy-start
  8.0 0.0 all-gather.8.cloned.1.call-start
  8.1 92.2 %all-gather.6.cloned.1.call-done = bf16[320,14336]{1,0:T(8,128)(2,1)} async-done(((bf16[320,1792]{1,0:T(8,128)(2,1)}), bf16[320,14336]{1,0:T(8,128)(2,1)}) %all-gather.6.cloned.1.call-update) | async-done | bytes 9175056 | tf_op jit(solution)/shard_map/all_gather | solution.py:19
  100.3 17.2 %fusion.4 = bf16[320,896]{1,0:T(8,128)(2,1)} fusion(bf16[320,14336]{1,0:T(8,128)(2,1)} %all-gather.6.cloned.1.call-done, bf16[14336,1,896]{2,0,1:T(8,128)(2,1)} %param.8), kind=kOutput, calls=%fused_computation.6 | convolution fusion | flops 8221122560 | bytes 35438592 | tf_op jit(solution)/shard_map/dot_general | solution.py:8
  117.5 0.0 all-gather.8.cloned.1.call-update
  117.5 0.0 reduce-scatter.2.cloned.1.call-start
  117.5 0.0 copy-done
  117.5 0.2 reduce-window.4
  117.7 0.1 fusion.10
  117.8 16.4 %all-gather.4.cloned.1.call-done = bf16[320,4096]{1,0:T(8,128)(2,1)} async-done(((bf16[320,512]{1,0:T(8,128)(2,1)}), bf16[320,4096]{1,0:T(8,128)(2,1)}) %all-gather.4.cloned.1.call-update) | async-done | bytes 2621456 | tf_op jit(solution)/shard_map/all_gather | solution.py:16
  134.2 4.5 %convolution_convert_fusion = bf16[320,512]{1,0:T(8,128)(2,1)S(1)} fusion(bf16[320,4096]{1,0:T(8,128)(2,1)} %all-gather.4.cloned.1.call-done, bf16[4096,512]{1,0:T(8,128)(2,1)} %param.7), kind=kOutput, calls=%fused_computation.7 | convolution fusion | flops 1342341120 | bytes 7143424 | tf_op jit(solution)/shard_map/dot_general | solution.py:8
  138.7 2.3 all_gather.13
  141.0 43.1 %all-gather.8.cloned.1.call-done = bf16[320,3584]{1,0:T(8,128)(2,1)} async-done(((bf16[320,896]{1,0:T(8,128)(2,1)}), bf16[320,3584]{1,0:T(8,128)(2,1)}) %all-gather.8.cloned.1.call-update) | async-done | bytes 2293776 | tf_op jit(solution)/shard_map/all_gather | solution.py:20
  184.1 20.8 %multiply_reduce_fusion = f32[1024,3584]{1,0:T(8,128)} fusion(bf16[320,3584]{1,0:T(8,128)(2,1)} %all-gather.8.cloned.1.call-done, bf16[3,320]{1,0:T(4,128)(2,1)S(1)} %fusion.10, bf16[320,1024]{1,0:T(8,128)(2,1)S(1)} %all_gather.13), kind=kOutput, calls=%fused_computation | convolution fusion | flops 7065763840 | bytes 17631104 | tf_op jit(solution)/shard_map/etk,tj->ekj/dot_general | solution.py:29
  204.9 12.0 %broadcast_multiply_fusion = f32[1024,3584]{1,0:T(8,128)} fusion(f32[1024,3584]{1,0:T(8,128)} %multiply_reduce_fusion), kind=kLoop, calls=%fused_computation.3 | loop fusion | flops 3670016 | bytes 29360128 | tf_op jit(solution)/shard_map/div | solution.py:30
  216.9 0.0 reduce-scatter.2.cloned.1.call-update
  216.9 166.0 %reduce-scatter.2.cloned.1.call-done = f32[1024,1792]{1,0:T(8,128)} async-done(((f32[1024,3584]{1,0:T(8,128)}), f32[1024,1792]{1,0:T(8,128)}) %reduce-scatter.2.cloned.1.call-update) | async-done | bytes 7340048 | tf_op jit(solution)/shard_map/reduce_scatter | solution.py:31
  (1 shorter events, 0.0 us)
Async XLA Ops:
  6.5 93.7 %all-gather.6.cloned.1.call-start = ((), (), s32[]{:S(2)}) async-start(), calls=%async_computation.2 | async-start | bytes 10321920 | tf_op jit(solution)/shard_map/all_gather | solution.py:19
  7.3 127.0 %all-gather.4.cloned.1.call-start = ((), (), s32[]{:S(2)}) async-start(), calls=%async_computation.1 | async-start | bytes 2949120 | tf_op jit(solution)/shard_map/all_gather | solution.py:16
  8.0 109.5 %copy-start = (s32[1,3]{1,0:T(1,128)S(1)}, s32[1,3]{1,0:T(1,128)}, u32[]{:S(2)}) copy-start(s32[1,3]{1,0:T(1,128)} %param.9) | copy-start | bytes 40
  8.0 176.0 %all-gather.8.cloned.1.call-start = ((), (), s32[]{:S(2)}) async-start(), calls=%async_computation.3 | async-start | bytes 2867200 | tf_op jit(solution)/shard_map/all_gather | solution.py:20
  117.5 265.4 %reduce-scatter.2.cloned.1.call-start = ((), (), s32[]{:S(2)}) async-start(), calls=%async_computation.4 | async-start | bytes 22020096 | tf_op jit(solution)/shard_map/reduce_scatter | solution.py:31
Sparse Core Ops, SparseCore 0:
  9.0 91.2 all-gather.5
  101.9 32.2 all-gather.3
  135.8 48.2 all-gather.7
  217.0 165.7 reduce-scatter.1
where the time goes:
time: 390 us; the launch traced here: 389 us
  waiting for transfers between devices  319 us (82%)
  matrix products  42.5 us (11%)
  between operations  13.1 us (3%)
  other arithmetic  12.3 us (3%)
    reduce_scatter x1, waiting for transfers between devices, on_device(): return lax.psum_scatter(partial_sum, 'dp', scatter_dimension=1, tiled=True)  166 us
    all_gather x1, waiting for transfers between devices, on_device(): lax.all_gather(gradients, ('row', 'col'), axis=1, tiled=True)  92.2 us
    all_gather x1, waiting for transfers between devices, on_device(): lax.all_gather(rotated_g.astype(jnp.bfloat16), 'row', axis=1, tiled=True)  43.1 us
    dot_general x2, matrix products, fold_with(): return jnp.dot(section, basis, preferred_element_type=jnp.float32)  21.7 us
    dot_general x1, matrix products, on_device(): jnp.einsum('etk,tj->ekj', masked, rotated_g, preferred_element_type=jnp.f...  20.8 us
    all_gather x1, waiting for transfers between devices, on_device(): lax.all_gather(activations, ('row', 'col'), axis=1, tiled=True)  16.4 us
    div x1, other arithmetic, on_device(): partial_sum = jnp.sum(products * products, axis=0) / examples_all  12 us
  transfers between devices with their start and end apart: 4, of which 4 were waited for; matrix products, arithmetic and copies ran while one was open for 6% of the time, Pallas kernels for 0%

commit v1 on v0

v1 whole, which is shorter than its diff:
```python
import functools

import jax
import jax.numpy as jnp
from jax import lax
from jax.experimental import pallas as pl
from jax.experimental.pallas import tpu as pltpu
from jax.sharding import PartitionSpec as P

STEP = 64
VMEM_BYTES = 56 * 1024 * 1024


def span_of(lengths_ref, example):
    begin = 0
    for before in range(example):
        begin = begin + lengths_ref[0, before]
    return begin, begin + lengths_ref[0, example]


def window_start(begin, slack):
    return pl.multiple_of(jnp.minimum(begin // STEP * STEP, slack), STEP)


def mask_kernel(examples, window, lengths_ref, act_ref, out_ref):
    slack = act_ref.shape[0] - window
    for example in range(examples):
        begin, end = span_of(lengths_ref, example)
        start = window_start(begin, slack)
        rows = act_ref[pl.ds(start, window), :]
        token = start + lax.broadcasted_iota(jnp.int32, (window, 1), 0)
        inside = (token >= begin) & (token < end)
        kept = jnp.where(inside, rows.astype(jnp.float32), 0.0)
        out_ref[example] = kept.T.astype(out_ref.dtype)


def masked_windows(rotated, lengths, window):
    tokens, directions = rotated.shape
    examples = lengths.shape[1]
    return pl.pallas_call(
        functools.partial(mask_kernel, examples, window),
        out_shape=jax.ShapeDtypeStruct((examples, directions, window), rotated.dtype),
        in_specs=[
            pl.BlockSpec(memory_space=pltpu.SMEM),
            pl.BlockSpec(memory_space=pltpu.VMEM),
        ],
        out_specs=pl.BlockSpec(memory_space=pltpu.VMEM),
        compiler_params=pltpu.CompilerParams(vmem_limit_bytes=VMEM_BYTES),
        cost_estimate=pl.CostEstimate(
            flops=0, bytes_accessed=2 * tokens * directions * (1 + examples), transcendentals=0
        ),
    )(lengths, rotated)


def square_kernel(blocks, examples, window, total, *refs):
    lengths_refs, act_refs, grad_refs = refs[:blocks], refs[blocks : 2 * blocks], refs[2 * blocks : 3 * blocks]
    out_ref = refs[3 * blocks]
    directions = out_ref.shape[0]
    piece = min(directions, 256)
    for top in range(0, directions, piece):
        acc = None
        for block in range(blocks):
            slack = grad_refs[block].shape[0] - window
            for example in range(examples):
                begin, _ = span_of(lengths_refs[block], example)
                start = window_start(begin, slack)
                product = jnp.dot(
                    act_refs[block][example, top : top + piece, :],
                    grad_refs[block][pl.ds(start, window), :],
                    preferred_element_type=jnp.float32,
                )
                acc = product * product if acc is None else acc + product * product
        out_ref[top : top + piece, :] = acc / total


def squared_sums(lengths, acts, grads, window, total):
    blocks = len(acts)
    examples, directions, _ = acts[0].shape
    tokens, columns = grads[0].shape
    wide = 256 if columns % 256 == 0 else 128
    return pl.pallas_call(
        functools.partial(square_kernel, blocks, examples, window, total),
        out_shape=jax.ShapeDtypeStruct((directions, columns), jnp.float32),
        grid=(columns // wide,),
        in_specs=[pl.BlockSpec(memory_space=pltpu.SMEM)] * blocks
        + [pl.BlockSpec((examples, directions, window), lambda j: (0, 0, 0))] * blocks
        + [pl.BlockSpec((tokens, wide), lambda j: (0, j))] * blocks,
        out_specs=pl.BlockSpec((directions, wide), lambda j: (0, j)),
        compiler_params=pltpu.CompilerParams(vmem_limit_bytes=VMEM_BYTES),
        cost_estimate=pl.CostEstimate(
            flops=2 * blocks * examples * directions * columns * window,
            bytes_accessed=4 * directions * columns + 2 * blocks * tokens * columns,
            transcendentals=0,
        ),
    )(*lengths, *acts, *grads)


def fold_with(basis, section):
    return jnp.dot(section, basis, preferred_element_type=jnp.float32).astype(jnp.bfloat16)


def on_device(activations, gradients, q_act, q_grad, lengths):
    tokens = activations.shape[0]
    n_dp = lax.axis_size("dp")
    total = lengths.shape[1] * n_dp
    window = min(tokens, 256)
    basis_grad = q_grad.reshape(q_grad.shape[0], q_grad.shape[2])

    def shifted(x, k):
        return lax.ppermute(x, "dp", [(i, (i + k) % n_dp) for i in range(n_dp)])

    rotated_g = fold_with(basis_grad, lax.all_gather(gradients, ("row", "col"), axis=1, tiled=True))
    rotated = fold_with(q_act, lax.all_gather(activations, ("row", "col"), axis=1, tiled=True))
    acts, spans = [rotated], [lengths]
    for k in range(1, n_dp):
        acts.append(shifted(rotated, k))
        spans.append(shifted(lengths, k))
    acts = [lax.all_gather(x, "col", axis=1, tiled=True) for x in acts]
    acts = [masked_windows(x, s, window) for x, s in zip(acts, spans)]

    rotated_g = lax.all_gather(rotated_g, "row", axis=1, tiled=True)
    columns = rotated_g.shape[1] // n_dp
    me = lax.axis_index("dp")

    def columns_of(d):
        return lax.dynamic_slice_in_dim(rotated_g, d % n_dp * columns, columns, axis=1)

    grads = [columns_of(me)]
    for k in range(1, n_dp):
        grads.append(shifted(columns_of(me + k), k))
    return squared_sums(spans, acts, grads, window, total)


def solution(mesh):
    return jax.shard_map(
        on_device,
        mesh=mesh,
        in_specs=(
            P(("parts", "dp"), ("row", "col")),
            P(("parts", "dp"), ("row", "col")),
            P(None, ("row", "col")),
            P(None, "col", "row"),
            P(("parts", "dp"), None),
        ),
        out_specs=P(("parts", "row"), ("col", "dp")),
        check_vma=False,
    )
```

time: 390 us -> 238 us (0.61)
  waiting for transfers between devices: 319 us -> 174 us
  matrix products: 42.5 us -> 21.2 us
  Pallas kernels: 0 us -> 16.9 us
  other arithmetic: 12.3 us -> 0 us
  local copies, waits for them, and re-layouts: 0.01 us -> 4.39 us
    reduce_scatter x1 -> x0, waiting for transfers between devices: 166 us -> none  [on_device(): return lax.psum_scatter(partial_sum, 'dp', scatter_dimension=1, tiled=True)]
    dot_general x3 -> x2, matrix products: 42.5 us -> 21.2 us  [fold_with(): jnp.dot(section, basis, preferred_element_type=jnp.float32)]
    pallas_call x0 -> x3, Pallas kernels: none -> 16.9 us  [the longest x1 11.3 us: squared_sums(): pl.pallas_call(functools.partial(square_kernel, blocks, examples, window,...]
    all_gather x1, waiting for transfers between devices: 16.4 us -> 30 us  [on_device(): lax.all_gather(activations, ('row', 'col'), axis=1, tiled=True)]
    div x1 -> x0, other arithmetic: 12 us -> none  [on_device(): partial_sum = jnp.sum(products * products, axis=0) / examples_all]
    all_gather x1, waiting for transfers between devices: 43.1 us -> 47.1 us  [on_device(): rotated_g = lax.all_gather(rotated_g, 'row', axis=1, tiled=True)]
  transfers between devices with their start and end apart: 4 -> 6, of which waited for: 4 -> 4; matrix products, arithmetic and copies ran while one was open for 6% -> 3% of each run, Pallas kernels for 0% -> 2%
where the time goes in v1:
time: 238 us
  waiting for transfers between devices  174 us (73%)
  matrix products  21.2 us (9%)
  Pallas kernels  16.9 us (7%)
  between operations  13.1 us (6%)
  blocking collectives  4.79 us (2%)
  local copies, waits for them, and re-layouts  4.39 us (2%)
  starting transfers between devices  3.66 us (2%)
    all_gather x1, waiting for transfers between devices, on_device(): lax.all_gather(gradients, ('row', 'col'), axis=1, tiled=True)  93 us
    all_gather x1, waiting for transfers between devices, on_device(): rotated_g = lax.all_gather(rotated_g, 'row', axis=1, tiled=True)  47.1 us
    all_gather x1, waiting for transfers between devices, on_device(): lax.all_gather(activations, ('row', 'col'), axis=1, tiled=True)  30 us
    dot_general x2, matrix products, fold_with(): jnp.dot(section, basis, preferred_element_type=jnp.float32)  21.2 us
    pallas_call x1, Pallas kernels, squared_sums(): pl.pallas_call(functools.partial(square_kernel, blocks, examples, window,...  11.3 us
    pallas_call x2, Pallas kernels, masked_windows(): pl.pallas_call(functools.partial(mask_kernel, examples, window), out_shap...  5.64 us
    all_gather x2, blocking collectives, on_device(): acts = [lax.all_gather(x, 'col', axis=1, tiled=True) for x in acts]  4.79 us
  transfers between devices with their start and end apart: 6, of which 4 were waited for; matrix products, arithmetic and copies ran while one was open for 3% of the time, Pallas kernels for 2%

profile of v1, /device:TPU:0, one launch (start us, length us, event | category | flops | bytes accessed | tf_op | source)
XLA Modules:
  0.0 238.1 jit_solution(14925829331257325435)
XLA Ops:
  6.5 0.0 all-gather.6.cloned.1.call-start
  6.5 0.7 all-gather.6.cloned.1.call-update
  7.3 0.0 all-gather.8.cloned.1.call-start
  7.3 93.0 %all-gather.6.cloned.1.call-done = bf16[320,14336]{1,0:T(8,128)(2,1)} async-done(((bf16[320,1792]{1,0:T(8,128)(2,1)}), bf16[320,14336]{1,0:T(8,128)(2,1)}) %all-gather.6.cloned.1.call-update) | async-done | bytes 9175056 | tf_op jit(solution)/shard_map/all_gather | solution.py:112
  100.3 16.8 %fusion.2 = bf16[320,896]{1,0:T(8,128)(2,1)} fusion(bf16[320,14336]{1,0:T(8,128)(2,1)} %all-gather.6.cloned.1.call-done, bf16[14336,1,896]{2,0,1:T(8,128)(2,1)} %param.8), kind=kOutput, calls=%fused_computation.2 | convolution fusion | flops 8221122560 | bytes 35438592 | tf_op jit(solution)/shard_map/dot_general | solution.py:99
  117.0 0.0 all-gather.8.cloned.1.call-update
  117.0 0.0 all-gather.4.cloned.1.call-start
  117.1 0.7 all-gather.4.cloned.1.call-update
  117.8 47.1 %all-gather.8.cloned.1.call-done = bf16[320,3584]{1,0:T(8,128)(2,1)} async-done(((bf16[320,896]{1,0:T(8,128)(2,1)}), bf16[320,3584]{1,0:T(8,128)(2,1)}) %all-gather.8.cloned.1.call-update) | async-done | bytes 2293776 | tf_op jit(solution)/shard_map/all_gather | solution.py:121
  164.9 2.8 %constant_dynamic-slice_fusion = (bf16[320,1792]{1,0:T(8,128)(2,1)S(1)}, bf16[320,1792]{1,0:T(8,128)(2,1)}) fusion(bf16[320,3584]{1,0:T(8,128)(2,1)} %all-gather.8.cloned.1.call-done, s32[]{:T(128)S(6)} %select_n.20, s32[]{:T(128)S(6)} %select_n.18), kind=kLoop, calls=%fused_computation.4 | loop fusion | bytes 4587528 | tf_op jit(solution)/shard_map/dynamic_slice | solution.py:126
  167.6 0.0 copy-start
  167.6 1.5 collective-permute-start.2
  169.1 30.0 %all-gather.4.cloned.1.call-done = bf16[320,4096]{1,0:T(8,128)(2,1)} async-done(((bf16[320,512]{1,0:T(8,128)(2,1)}), bf16[320,4096]{1,0:T(8,128)(2,1)}) %all-gather.4.cloned.1.call-update) | async-done | bytes 2621456 | tf_op jit(solution)/shard_map/all_gather | solution.py:113
  199.1 4.5 %convolution_convert_fusion = bf16[320,512]{1,0:T(8,128)(2,1)S(1)} fusion(bf16[320,4096]{1,0:T(8,128)(2,1)} %all-gather.4.cloned.1.call-done, bf16[4096,512]{1,0:T(8,128)(2,1)} %param.7), kind=kOutput, calls=%fused_computation.3 | convolution fusion | flops 1342341120 | bytes 7143424 | tf_op jit(solution)/shard_map/dot_general | solution.py:99
  203.6 1.5 collective-permute-start.1
  205.1 0.0 copy-done
  205.1 0.6 collective-permute-start
  205.7 2.4 %all_gather.16.act_ref = bf16[320,1024]{1,0:T(8,128)(2,1)} all-gather(bf16[320,512]{1,0:T(8,128)(2,1)S(1)} %convolution_convert_fusion), channel_id=1, replica_groups=mesh['parts'=2,'row'=4,'col'=2,'dp'=2] {'col'}, dimensions={1}, use_global_device_ids=true | all-gather | bytes 983040 | tf_op jit(solution)/shard_map/all_gather | solution.py:118
  208.1 2.8 %shard_map.55.refs_2_ = bf16[3,1024,256]{2,1,0:T(8,128)(2,1)} custom-call(s32[1,3]{1,0:T(1,128)} %refs_0_.1, bf16[320,1024]{1,0:T(8,128)(2,1)} %all_gather.16.act_ref), custom_call_target="tpu_custom_call" | custom-call | bytes 2621440 | tf_op jit(solution)/shard_map/pallas_call | solution.py:40
  210.9 2.6 %collective-permute-done.1 = bf16[320,512]{1,0:T(8,128)(2,1)S(1)} collective-permute-done((bf16[320,512]{1,0:T(8,128)(2,1)S(1)}, bf16[320,512]{1,0:T(8,128)(2,1)S(1)}, u32[]{:S(2)}, u32[]{:S(2)}) %collective-permute-start.1) | collective-permute-done | bytes 327712 | tf_op jit(solution)/shard_map/ppermute | solution.py:110
  213.5 2.4 %all_gather.17.act_ref = bf16[320,1024]{1,0:T(8,128)(2,1)} all-gather(bf16[320,512]{1,0:T(8,128)(2,1)S(1)} %collective-permute-done.1), channel_id=1, replica_groups=mesh['parts'=2,'row'=4,'col'=2,'dp'=2] {'col'}, dimensions={1}, use_global_device_ids=true | all-gather | bytes 983040 | tf_op jit(solution)/shard_map/all_gather | solution.py:118
  215.9 0.0 collective-permute-done.lengths_ref.refs_1_
  215.9 0.0 copy-start.1
  215.9 0.6 copy-done.1
  216.5 2.8 %shard_map.56.refs_3_ = bf16[3,1024,256]{2,1,0:T(8,128)(2,1)} custom-call(s32[1,3]{1,0:T(1,128)} %copy-done.1, bf16[320,1024]{1,0:T(8,128)(2,1)} %all_gather.17.act_ref), custom_call_target="tpu_custom_call" | custom-call | bytes 2621440 | tf_op jit(solution)/shard_map/pallas_call | solution.py:40
  219.3 0.0 collective-permute-done.2.refs_5_
  219.3 0.0 copy-start.2
  219.3 1.0 copy-done.2
  220.3 11.3 %shard_map.57 = f32[1024,1792]{1,0:T(8,128)} custom-call(s32[1,3]{1,0:T(1,128)} %refs_0_.1, s32[1,3]{1,0:T(1,128)} %copy-done.1, bf16[3,1024,256]{2,1,0:T(8,128)(2,1)} %shard_map.55.refs_2_, bf16[3,1024,256]{2,1,0:T(8,128)(2,1)} %shard_map.56.refs_3_, bf16[320,1792]{1,0:T(8,128)(2,1)} %get-tuple-element.6.refs_4_, bf16[320,1792]{1,0:T(8,128)(2,1)} %copy-done.2), custom_call_target="tpu_custom_call" | custom-call | flops 5637144576 | bytes 9633792 | tf_op jit(solution)/shard_map/pallas_call | solution.py:81
Async XLA Ops:
  6.5 93.7 %all-gather.6.cloned.1.call-start = ((), (), s32[]{:S(2)}) async-start(), calls=%async_computation.1 | async-start | bytes 10321920 | tf_op jit(solution)/shard_map/all_gather | solution.py:112
  7.3 157.6 %all-gather.8.cloned.1.call-start = ((), (), s32[]{:S(2)}) async-start(), calls=%async_computation.2 | async-start | bytes 2867200 | tf_op jit(solution)/shard_map/all_gather | solution.py:121
  117.0 82.1 %all-gather.4.cloned.1.call-start = ((), (), s32[]{:S(2)}) async-start(), calls=%async_computation | async-start | bytes 2949120 | tf_op jit(solution)/shard_map/all_gather | solution.py:113
  167.6 37.5 %copy-start = (s32[1,3]{1,0:T(1,128)S(1)}, s32[1,3]{1,0:T(1,128)}, u32[]{:S(2)}) copy-start(s32[1,3]{1,0:T(1,128)} %refs_0_.1) | copy-start | bytes 40
  167.6 51.7 %collective-permute-start.2 = (bf16[320,1792]{1,0:T(8,128)(2,1)S(1)}, bf16[320,1792]{1,0:T(8,128)(2,1)S(1)}, u32[]{:S(2)}, u32[]{:S(2)}) collective-permute-start(bf16[320,1792]{1,0:T(8,128)(2,1)S(1)} %get-tuple-element.5), channel_id=1, source_target_pairs={{0,1},{1,0},{2,3},{3,2},{4,5},{5,4},{6,7},{7,6},{8,9},{9,8},{10,11... | collective-permute-start | bytes 3440648 | tf_op jit(solution)/shard_map/ppermute | solution.py:110
  203.6 9.9 %collective-permute-start.1 = (bf16[320,512]{1,0:T(8,128)(2,1)S(1)}, bf16[320,512]{1,0:T(8,128)(2,1)S(1)}, u32[]{:S(2)}, u32[]{:S(2)}) collective-permute-start(bf16[320,512]{1,0:T(8,128)(2,1)S(1)} %convolution_convert_fusion), channel_id=1, source_target_pairs={{0,1},{1,0},{2,3},{3,2},{4,5},{5,4},{6,7},{7,6},{8,9},{9,8},{10,11... | collective-permute-start | bytes 983048 | tf_op jit(solution)/shard_map/ppermute | solution.py:110
  205.1 10.8 %collective-permute-start = (s32[1,3]{1,0:T(1,128)S(1)}, s32[1,3]{1,0:T(1,128)S(1)}, u32[]{:S(2)}, u32[]{:S(2)}) collective-permute-start(s32[1,3]{1,0:T(1,128)S(1)} %copy-done), channel_id=1, source_target_pairs={{0,1},{1,0},{2,3},{3,2},{4,5},{5,4},{6,7},{7,6},{8,9},{9,8},{10,11... | collective-permute-start | bytes 44 | tf_op jit(solution)/shard_map/ppermute | solution.py:110
  215.9 0.6 copy-start.1
  219.3 1.0 copy-start.2
Sparse Core Ops, SparseCore 0:
  9.0 91.2 all-gather.5
  117.2 47.6 all-gather.7
  166.5 32.5 all-gather.3

commit v2 on v1

v2 whole, which is shorter than its diff:
```python
import functools

import jax
import jax.numpy as jnp
from jax import lax
from jax.experimental import pallas as pl
from jax.experimental.pallas import tpu as pltpu
from jax.sharding import PartitionSpec as P

STEP = 64
VMEM_BYTES = 56 * 1024 * 1024


def span_of(lengths_ref, example):
    begin = 0
    for before in range(example):
        begin = begin + lengths_ref[0, before]
    return begin, begin + lengths_ref[0, example]


def window_start(begin, slack):
    return pl.multiple_of(jnp.minimum(begin // STEP * STEP, slack), STEP)


def mask_kernel(examples, window, core_ref, lengths_ref, mine_ref, theirs_ref, out_ref):
    slack = mine_ref.shape[0] - window
    half = mine_ref.shape[1]
    for example in range(examples):
        begin, end = span_of(lengths_ref, example)
        start = window_start(begin, slack)
        token = start + lax.broadcasted_iota(jnp.int32, (window, 1), 0)
        inside = (token >= begin) & (token < end)
        for place, ref in ((core_ref[0], mine_ref), (1 - core_ref[0], theirs_ref)):
            rows = ref[pl.ds(start, window), :]
            kept = jnp.where(inside, rows.astype(jnp.float32), 0.0)
            out_ref[example, pl.ds(pl.multiple_of(place * half, half), half), :] = kept.T.astype(out_ref.dtype)


def masked_windows(core, lengths, mine, theirs, window):
    tokens, half = mine.shape
    examples = lengths.shape[1]
    return pl.pallas_call(
        functools.partial(mask_kernel, examples, window),
        name="masked_windows",
        out_shape=jax.ShapeDtypeStruct((examples, 2 * half, window), mine.dtype),
        in_specs=[pl.BlockSpec(memory_space=pltpu.SMEM)] * 2 + [pl.BlockSpec(memory_space=pltpu.VMEM)] * 2,
        out_specs=pl.BlockSpec(memory_space=pltpu.VMEM),
        compiler_params=pltpu.CompilerParams(vmem_limit_bytes=VMEM_BYTES),
    )(core, lengths, mine, theirs)


def square_kernel(chunks, examples, window, total, place_ref, choice_ref, *refs):
    blocks = len(chunks)
    lengths_refs, act_refs, refs = refs[:blocks], refs[blocks : 2 * blocks], refs[2 * blocks :]
    sem, grad_refs, out_ref = refs[-1], refs[-1 - blocks : -1], refs[-2 - blocks]

    @pl.when(pl.program_id(0) == 0)
    def _():
        landed, at, place = [], 0, 0
        for block in range(blocks):
            top = 0
            for rows, arrays in chunks[block]:
                target = grad_refs[block].at[pl.ds(top, rows), :]
                for index in range(arrays):

                    @pl.when(choice_ref[place] == index)
                    def _():
                        pltpu.make_async_copy(refs[at + index], target, sem.at[place]).start()

                landed.append(pltpu.make_async_copy(refs[at], target, sem.at[place]))
                top, at, place = top + rows, at + arrays, place + 1
        for copy in landed:
            copy.wait()

    rows, columns = out_ref.shape
    wide, tall = min(columns, 256), min(rows, 128)
    for left in range(0, columns, wide):
        right = min(left + wide, columns)
        for top in range(0, rows, tall):
            acc = None
            for block in range(blocks):
                slack = grad_refs[block].shape[0] - window
                for example in range(examples):
                    begin, _ = span_of(lengths_refs[block], example)
                    product = jnp.dot(
                        act_refs[block][example, top : top + tall, :],
                        grad_refs[block][pl.ds(window_start(begin, slack), window), left:right],
                        preferred_element_type=jnp.float32,
                    )
                    acc = product * product if acc is None else acc + product * product
            out_ref[top : top + tall, left:right] = acc / total


def squared_sums(lengths, acts, grads, window, total, places=1, place=None, onto=None):
    blocks = len(acts)
    examples, directions, _ = acts[0].shape
    columns = grads[0][0][1][0].shape[1]
    chunks = [[(arrays[0].shape[0], len(arrays)) for _, arrays in block] for block in grads]
    choices = jnp.stack([jnp.asarray(choice, jnp.int32) for block in grads for choice, _ in block])
    flat = [x for block in grads for _, arrays in block for x in arrays]
    tall = min(directions, 512)
    place = jnp.asarray(0 if place is None else place, jnp.int32).reshape(1)
    operands = [choices, *lengths, *acts, *flat]
    in_specs = (
        [pl.BlockSpec(memory_space=pltpu.SMEM)] * (1 + blocks)
        + [pl.BlockSpec((examples, tall, window), lambda i, place: (0, i, 0))] * blocks
        + [pl.BlockSpec(memory_space=pl.ANY)] * len(flat)
    )
    aliases = {}
    if onto is not None:
        aliases = {1 + len(operands): 0}
        operands.append(onto)
        in_specs.append(pl.BlockSpec(memory_space=pl.ANY))
    return pl.pallas_call(
        functools.partial(square_kernel, chunks, examples, window, total),
        name="squared_sums",
        out_shape=jax.ShapeDtypeStruct((directions, places * columns), jnp.float32),
        grid_spec=pltpu.PrefetchScalarGridSpec(
            num_scalar_prefetch=1,
            grid=(directions // tall,),
            in_specs=in_specs,
            out_specs=pl.BlockSpec((tall, columns), lambda i, place: (i, place[0])),
            scratch_shapes=[pltpu.VMEM((sum(rows for rows, _ in c), columns), jnp.bfloat16) for c in chunks]
            + [pltpu.SemaphoreType.DMA((len(choices),))],
        ),
        input_output_aliases=aliases,
        compiler_params=pltpu.CompilerParams(vmem_limit_bytes=VMEM_BYTES),
    )(place, *operands)


def fold_kernel(started, parts, offsets_ref, *refs):
    start_ref = refs[0] if started else None
    mine, theirs = refs[started : started + parts], refs[started + parts : started + 2 * parts]
    basis_ref, *out_refs, sum_ref = refs[started + 2 * parts :]
    step = pl.program_id(0)

    def product(pieces):
        rows = pieces[0][...] if parts == 1 else jnp.concatenate([x[...] for x in pieces], axis=0)
        return jnp.dot(rows, basis_ref[...], preferred_element_type=jnp.float32)

    @pl.when(step == 0)
    def _():
        sum_ref[...] = start_ref[...] + product(mine) if started else product(mine)

    @pl.when(step == 1)
    def _():
        total = sum_ref[...] + product(theirs)
        rows = total.shape[0] // len(out_refs)
        for index, out_ref in enumerate(out_refs):
            out_ref[...] = total[index * rows : index * rows + rows, :].astype(out_ref.dtype)


def fold_block(start, mine, theirs, basis, features, offsets, place, kind, chunks=1):
    tokens = sum(x.shape[0] for x in mine)
    columns = basis.shape[1]
    started = start is not None
    sections = [pl.BlockSpec((x.shape[0], features), lambda i, offsets: (0, 0)) for x in (*mine, *theirs)]
    return pl.pallas_call(
        functools.partial(fold_kernel, started, len(mine)),
        name=f"fold_{place}",
        out_shape=[jax.ShapeDtypeStruct((tokens // chunks, columns), kind)] * chunks,
        grid_spec=pltpu.PrefetchScalarGridSpec(
            num_scalar_prefetch=1,
            grid=(2,),
            in_specs=[pl.BlockSpec((tokens, columns), lambda i, offsets: (0, 0))] * started
            + sections
            + [pl.BlockSpec((features, columns), lambda i, offsets: (offsets[2 * place + i], 0))],
            out_specs=[pl.BlockSpec((tokens // chunks, columns), lambda i, offsets: (0, 0))] * chunks,
            scratch_shapes=[pltpu.VMEM((tokens, columns), jnp.float32)],
        ),
        compiler_params=pltpu.CompilerParams(vmem_limit_bytes=VMEM_BYTES),
    )(offsets, *([start] if started else []), *mine, *theirs, basis)


def project_kernel(steps, offsets_ref, *refs):
    blocks, basis_ref, out_ref, sum_ref = refs[:-3], refs[-3], refs[-2], refs[-1]
    step = pl.program_id(0)
    deep = blocks[0].shape[1]
    total = None
    for place, ref in enumerate(blocks):
        begin = pl.multiple_of((offsets_ref[place] * steps + step) * deep, deep)
        product = jnp.dot(ref[...], basis_ref[pl.ds(begin, deep), :], preferred_element_type=jnp.float32)
        total = product if total is None else total + product

    @pl.when(step == 0)
    def _():
        sum_ref[...] = total

    @pl.when(step > 0)
    def _():
        sum_ref[...] += total

    @pl.when(step == steps - 1)
    def _():
        out_ref[...] = sum_ref[...].astype(out_ref.dtype)


def project(blocks, features, basis, offsets):
    tokens, width = blocks[-1].shape
    columns = basis.shape[1]
    deep = 256
    steps = width // deep

    def tail(x):
        skipped = features // deep if x.shape[1] > width else 0
        return pl.BlockSpec((tokens, deep), lambda i: (0, skipped + i))

    return pl.pallas_call(
        functools.partial(project_kernel, steps),
        name="project",
        out_shape=jax.ShapeDtypeStruct((tokens, columns), basis.dtype),
        grid=(steps,),
        in_specs=[pl.BlockSpec(memory_space=pltpu.SMEM)]
        + [tail(x) for x in blocks]
        + [pl.BlockSpec(basis.shape, lambda i: (0, 0))],
        out_specs=pl.BlockSpec((tokens, columns), lambda i: (0, 0)),
        scratch_shapes=[pltpu.VMEM((tokens, columns), jnp.float32)],
        compiler_params=pltpu.CompilerParams(vmem_limit_bytes=VMEM_BYTES),
    )(offsets, *blocks, basis)


RING = [(0, 1), (1, 3), (3, 2), (2, 0)]


def slots_of(row):
    before = jnp.where(row < 2, 2 - 2 * row, 7 - 2 * row)
    return row, before, 3 - row, 3 - before


def hop(x, what, back=False):
    with jax.named_scope(what):
        return lax.ppermute(x, "row", [hop[::-1] for hop in RING] if back else RING)


def swap(x, axis, what):
    with jax.named_scope(what):
        return lax.ppermute(x, axis, [(0, 1), (1, 0)])


def after(x, *others):
    return lax.optimization_barrier((x, *others))[0]


def chained(activations, gradients, q_act, basis_grad, lengths):
    tokens = activations.shape[0]
    total = 2 * lengths.shape[1]
    window = min(tokens, 256)
    half = tokens // 2
    row, core, me = lax.axis_index("row"), lax.axis_index("col"), lax.axis_index("dp")
    home = row // 2 == me
    outer = (row == 0) | (row == 3)
    cores = core.reshape(1)
    spans = [lengths, swap(lengths, "dp", "lengths_dp")]
    offsets = jnp.stack([2 * s + c for s in slots_of(row) for c in (core, 1 - core)]).astype(jnp.int32)

    features = gradients.shape[1]

    def crossed(chunks, place):
        return [swap(x, "col", f"tokens_{place}_cols_{i}") for i, x in enumerate(chunks)]

    def fold(start, mine, theirs, place):
        return fold_block(start, mine, theirs, basis_grad, features, offsets, place, jnp.float32)[0]

    own = jnp.concatenate([gradients, activations], axis=1)
    slots = [([own], crossed([own], 0))]
    first = hop(own, "tokens_first")
    sums = fold(None, *slots[0], 0)
    second = hop(after(first, sums, spans[1]), "tokens_second")
    slots.append(([first], crossed([first], 1)))
    sums = fold(sums, *slots[1], 1)
    second = after(second, sums)
    third = hop(second[:, :features], "grad_third")
    act_third = hop(second[:, features:], "act_third")
    slots.append(([second], crossed([second], 2)))
    sums = fold(sums, *slots[2], 2)
    third = after(third, sums)
    owns = fold_block(sums, [third], crossed([third], 3), basis_grad, features, offsets, 3, jnp.bfloat16, 2)

    def hops(chunks, what):
        return [hop(x, f"{what}_{i}", i == 1) for i, x in enumerate(chunks)]

    turn = home == outer
    act_third = after(act_third, *owns)
    blocks = [x for mine, theirs in slots for x in (*mine, *theirs)] + [act_third, swap(act_third, "col", "act_third_cols")]
    first = hops(owns, "rot_first")
    rotated = project(blocks, features, q_act, offsets)
    first = after(tuple(first), rotated)
    other = swap(after(rotated, *first), "dp", "act_dp")
    cross_first = swap(jnp.where(turn, first[0], first[1]), "dp", "rot_first_dp")
    second = hops(first, "rot_second")
    second = after(tuple(second), other, cross_first)
    early = [swap(jnp.where(home, s, o), "dp", f"rot_second_dp_{i}") for i, (s, o) in enumerate(zip(second, owns))]
    third = hops(second, "rot_third")
    acts = [(x, swap(x, "col", "rot_act_cols")) for x in (rotated, other)]
    acts = [masked_windows(cores, s, *x, window) for s, x in zip(spans, acts)]
    cross_third = swap(after(jnp.where(turn, third[1], third[0]), *acts, *early), "dp", "rot_third_dp")

    near = [
        [(jnp.where(home, 0, 1), (o, s)) for o, s in zip(owns, second)],
        [(0, (x,)) for x in early],
    ]
    far = [
        [(jnp.where(turn, 1, 0), (first[0], third[0])), (jnp.where(turn, 0, 1), (first[1], third[1]))],
        [(jnp.where(turn, 1, 0), (cross_first, cross_third)), (jnp.where(turn, 0, 1), (cross_first, cross_third))],
    ]
    place = jnp.where(home, row % 2, (3 - row) % 2)
    out = squared_sums(spans, acts, near, window, total, 2, place)
    return squared_sums(spans, acts, far, window, total, 2, 1 - place, out)


def fold_with(basis, section):
    return jnp.dot(section, basis, preferred_element_type=jnp.float32).astype(jnp.bfloat16)


def gathered(activations, gradients, q_act, basis_grad, lengths):
    n_dp = lax.axis_size("dp")
    total = lengths.shape[1] * n_dp
    window = min(activations.shape[0], 256)
    core, me = lax.axis_index("col"), lax.axis_index("dp")
    cores = core.reshape(1)

    def shifted(x, k):
        return lax.ppermute(x, "dp", [(i, (i + k) % n_dp) for i in range(n_dp)])

    rotated_g = fold_with(basis_grad, lax.all_gather(gradients, ("row", "col"), axis=1, tiled=True))
    rotated = fold_with(q_act, lax.all_gather(activations, ("row", "col"), axis=1, tiled=True))
    acts, spans = [rotated], [lengths]
    for k in range(1, n_dp):
        acts.append(shifted(rotated, k))
        spans.append(shifted(lengths, k))
    acts = [masked_windows(cores, s, x, swap(x, "col", "cols"), window) for x, s in zip(acts, spans)]

    rotated_g = lax.all_gather(rotated_g, "row", axis=1, tiled=True)
    columns = rotated_g.shape[1] // n_dp

    def columns_of(d):
        return lax.dynamic_slice_in_dim(rotated_g, d % n_dp * columns, columns, axis=1)

    grads = [columns_of(me)]
    for k in range(1, n_dp):
        grads.append(shifted(columns_of(me + k), k))
    return squared_sums(spans, acts, [[(0, [x])] for x in grads], window, total)


def on_device(activations, gradients, q_act, q_grad, lengths):
    basis_grad = q_grad.reshape(q_grad.shape[0], q_grad.shape[2])
    fits = lax.axis_size("row") == 4 and lax.axis_size("dp") == 2 and lax.axis_size("col") == 2
    plan = chained if fits else gathered
    return plan(activations, gradients, q_act, basis_grad, lengths)


def solution(mesh):
    return jax.shard_map(
        on_device,
        mesh=mesh,
        in_specs=(
            P(("parts", "dp"), ("row", "col")),
            P(("parts", "dp"), ("row", "col")),
            P(None, ("row", "col")),
            P(None, "col", "row"),
            P(("parts", "dp"), None),
        ),
        out_specs=P(("parts", "row"), ("col", "dp")),
        check_vma=False,
    )
```

time: 238 us -> 188 us (0.79)
  waiting for transfers between devices: 174 us -> 98.5 us
  Pallas kernels: 16.9 us -> 55.6 us
  matrix products: 21.2 us -> 0 us
  starting transfers between devices: 3.66 us -> 21.9 us
  between operations: 13.1 us -> 0.37 us
  local copies, waits for them, and re-layouts: 4.39 us -> 10.3 us
  blocking collectives: 4.79 us -> 0 us
    all_gather x3 -> x0, waiting for transfers between devices: 170 us -> none  [the longest x1 93 us: on_device(): lax.all_gather(gradients, ('row', 'col'), axis=1, tiled=True)]
    ppermute x3 -> x23, waiting for transfers between devices: 2.6 us -> 98.5 us  [the longest x10 81.8 us: hop(): return lax.ppermute(x, 'row', [hop[::-1] for hop in RING] if back else RING)]
    pallas_call x3 -> x9, Pallas kernels: 16.9 us -> 55.6 us  [the longest x4 28.9 us: fold_block(): pl.pallas_call(functools.partial(fold_kernel, started, len(mine)), name=f...]
    dot_general x2 -> x0, matrix products: 21.2 us -> none  [fold_with(): jnp.dot(section, basis, preferred_element_type=jnp.float32)]
    ppermute x3 -> x23, starting transfers between devices: 3.57 us -> 21.9 us  [the longest x10 14.1 us: hop(): return lax.ppermute(x, 'row', [hop[::-1] for hop in RING] if back else RING)]
    unnamed x6 -> x55, local copies, waits for them, and re-layouts: 1.6 us -> 8.33 us
    all_gather x2 -> x0, blocking collectives: 4.79 us -> none  [on_device(): acts = [lax.all_gather(x, 'col', axis=1, tiled=True) for x in acts]]
    dynamic_slice x1 -> x0, local copies, waits for them, and re-layouts: 2.79 us -> none  [columns_of(): lax.dynamic_slice_in_dim(rotated_g, d % n_dp * columns, columns, axis=1)]
  transfers between devices with their start and end apart: 6 -> 23, of which waited for: 4 -> 12; matrix products, arithmetic and copies ran while one was open for 3% -> 2% of each run, Pallas kernels for 2% -> 25%
where the time goes in v2:
time: 188 us
  waiting for transfers between devices  98.5 us (52%)
  Pallas kernels  55.6 us (30%)
  starting transfers between devices  21.9 us (12%)
  local copies, waits for them, and re-layouts  10.3 us (5%)
    ppermute x10, waiting for transfers between devices, hop(): return lax.ppermute(x, 'row', [hop[::-1] for hop in RING] if back else RING)  81.8 us
    pallas_call x4, Pallas kernels, fold_block(): pl.pallas_call(functools.partial(fold_kernel, started, len(mine)), name=f...  28.9 us
    ppermute x13, waiting for transfers between devices, swap(): return lax.ppermute(x, axis, [(0, 1), (1, 0)])  16.6 us
    pallas_call x2, Pallas kernels, squared_sums(): pl.pallas_call(functools.partial(square_kernel, chunks, examples, window,...  15.4 us
    ppermute x10, starting transfers between devices, hop(): return lax.ppermute(x, 'row', [hop[::-1] for hop in RING] if back else RING)  14.1 us
    unnamed x55, local copies, waits for them, and re-layouts  8.33 us
    ppermute x13, starting transfers between devices, swap(): return lax.ppermute(x, axis, [(0, 1), (1, 0)])  7.82 us
    pallas_call x2, Pallas kernels, masked_windows(): pl.pallas_call(functools.partial(mask_kernel, examples, window), name='ma...  5.67 us
  transfers between devices with their start and end apart: 23, of which 12 were waited for; matrix products, arithmetic and copies ran while one was open for 2% of the time, Pallas kernels for 25%

profile of v2, /device:TPU:0, one launch (start us, length us, event | category | flops | bytes accessed | tf_op | source)
XLA Modules:
  0.0 188.0 jit_solution(10827635321100833098)
XLA Ops:
  0.0 1.4 constant_dynamic-update-slice_fusion.1
  1.4 0.0 copy-start.1
  1.4 0.5 collective-permute-start.1
  2.0 2.6 %collective-permute-start.2 = (bf16[320,2304]{1,0:T(8,128)(2,1)S(1)}, bf16[320,2304]{1,0:T(8,128)(2,1)}, u32[]{:S(2)}, u32[]{:S(2)}) collective-permute-start(bf16[320,2304]{1,0:T(8,128)(2,1)S(1)} %constant_dynamic-update-slice_fusion.refs_0_), channel_id=1, source_target_pairs={{0,4},{4,12},{12,8},{8,0},{1,5},{5,13},{13,9},{9,1},{2,6},{6,14},{... | collective-permute-start | bytes 4423688 | tf_op jit(solution)/shard_map/tokens_first/ppermute | solution.py:232
  4.6 1.5 collective-permute-start
  6.1 0.7 stack.56.offsets_ref
  6.7 0.0 collective-permute-done.1.refs_1_
  6.8 1.1 copy-done.2
  7.9 7.0 %fold_0.1.refs_0_ = f32[320,896]{1,0:T(8,128)} custom-call(s32[8]{0:T(128)} %stack.56.offsets_ref, bf16[320,2304]{1,0:T(8,128)(2,1)} %copy-done.1, bf16[320,2304]{1,0:T(8,128)(2,1)} %copy-done.2, bf16[14336,896]{1,0:T(8,128)(2,1)} %bitcast.15), custom_call_target="tpu_custom_call" | custom-call | tf_op jit(solution)/shard_map/fold_0/pallas_call | solution.py:158
  14.9 0.0 collective-permute-done.lengths_ref.refs_1_
  14.9 23.7 %collective-permute-done.2.refs_1_.refs_2_ = bf16[320,2304]{1,0:T(8,128)(2,1)} collective-permute-done((bf16[320,2304]{1,0:T(8,128)(2,1)S(1)}, bf16[320,2304]{1,0:T(8,128)(2,1)}, u32[]{:S(2)}, u32[]{:S(2)}) %collective-permute-start.2) | collective-permute-done | bytes 1474592 | tf_op jit(solution)/shard_map/tokens_first/ppermute | solution.py:232
  38.6 0.0 collective-permute-start.3
  38.6 0.7 collective-permute-start.4
  39.3 2.7 %collective-permute-done.3.refs_2_.refs_3_ = bf16[320,2304]{1,0:T(8,128)(2,1)S(1)} collective-permute-done((bf16[320,2304]{1,0:T(8,128)(2,1)}, bf16[320,2304]{1,0:T(8,128)(2,1)S(1)}, u32[]{:S(2)}, u32[]{:S(2)}) %collective-permute-start.3) | collective-permute-done | bytes 1474592 | tf_op jit(solution)/shard_map/tokens_1_cols_0/ppermute | solution.py:237
  42.1 1.1 copy-done.3
  43.2 7.3 %fold_1.1.refs_0_ = f32[320,896]{1,0:T(8,128)} custom-call(s32[8]{0:T(128)} %stack.56.offsets_ref, f32[320,896]{1,0:T(8,128)} %fold_0.1.refs_0_, bf16[320,2304]{1,0:T(8,128)(2,1)} %collective-permute-done.2.refs_1_.refs_2_, bf16[320,2304]{1,0:T(8,128)(2,1)} %copy-done.3, bf16[14336,896]{1,0:T(8,128)(2,1)} %bitcast.16), custom_call_target="tpu_custom_call" | custom-call | tf_op jit(solution)/shard_map/fold_1/pallas_call | solution.py:158
  50.6 23.9 %collective-permute-done.4.refs_1_.refs_4_ = bf16[320,2304]{1,0:T(8,128)(2,1)S(1)} collective-permute-done((bf16[320,2304]{1,0:T(8,128)(2,1)}, bf16[320,2304]{1,0:T(8,128)(2,1)S(1)}, u32[]{:S(2)}, u32[]{:S(2)}) %collective-permute-start.4) | collective-permute-done | bytes 1474592 | tf_op jit(solution)/shard_map/tokens_second/ppermute | solution.py:232
  74.4 0.1 slice.7
  74.5 1.0 collective-permute-start.7
  75.5 2.2 %collective-permute-done.5.refs_2_.refs_5_ = bf16[320,2304]{1,0:T(8,128)(2,1)S(1)} collective-permute-done((bf16[320,2304]{1,0:T(8,128)(2,1)S(1)}, bf16[320,2304]{1,0:T(8,128)(2,1)S(1)}, u32[]{:S(2)}, u32[]{:S(2)}) %collective-permute-start.5) | collective-permute-done | bytes 1474592 | tf_op jit(solution)/shard_map/tokens_2_cols_0/ppermute | solution.py:237
  77.7 1.1 copy-done.4
  78.8 7.4 %fold_2.1.refs_0_ = f32[320,896]{1,0:T(8,128)} custom-call(s32[8]{0:T(128)} %stack.56.offsets_ref, f32[320,896]{1,0:T(8,128)} %fold_1.1.refs_0_, bf16[320,2304]{1,0:T(8,128)(2,1)} %copy-done, bf16[320,2304]{1,0:T(8,128)(2,1)} %copy-done.4, bf16[14336,896]{1,0:T(8,128)(2,1)} %bitcast.17), custom_call_target="tpu_custom_call" | custom-call | tf_op jit(solution)/shard_map/fold_2/pallas_call | solution.py:158
  86.2 16.9 %collective-permute-done.7.refs_1_ = bf16[320,1792]{1,0:T(8,128)(2,1)S(1)} collective-permute-done((bf16[320,1792]{1,0:T(8,128)(2,1)S(1)}, bf16[320,1792]{1,0:T(8,128)(2,1)S(1)}, u32[]{:S(2)}, u32[]{:S(2)}) %collective-permute-start.7) | collective-permute-done | bytes 1146912 | tf_op jit(solution)/shard_map/grad_third/ppermute | solution.py:232
  103.1 1.2 slice.6
  104.4 0.9 collective-permute-start.6
  105.2 0.7 collective-permute-done.8.refs_2_
  105.9 1.0 copy-done.6
  106.9 7.2 %fold_3.1 = (bf16[160,896]{1,0:T(8,128)(2,1)}, bf16[160,896]{1,0:T(8,128)(2,1)}) custom-call(s32[8]{0:T(128)} %stack.56.offsets_ref, f32[320,896]{1,0:T(8,128)} %fold_2.1.refs_0_, bf16[320,1792]{1,0:T(8,128)(2,1)} %copy-done.5, bf16[320,1792]{1,0:T(8,128)(2,1)} %copy-done.6, bf16[14336,896]{1,0:T(8,128)(2,1)} %bitcast.18), custom_call_target="tpu_custom_call" | custom-call | tf_op jit(solution)/shard_map/fold_3/pallas_call | solution.py:158
  114.1 1.1 collective-permute-done.6.refs_6_
  115.2 0.0 collective-permute-start.9
  115.2 1.7 collective-permute-start.11
  116.9 1.2 collective-permute-start.12
  118.1 0.0 collective-permute-done.9.refs_7_
  118.2 0.8 copy-done.18
  118.9 5.6 %project.1.mine_ref = bf16[320,512]{1,0:T(8,128)(2,1)} custom-call(s32[8]{0:T(128)} %stack.56.offsets_ref, bf16[320,2304]{1,0:T(8,128)(2,1)} %copy-done.1, bf16[320,2304]{1,0:T(8,128)(2,1)} %copy-done.2, bf16[320,2304]{1,0:T(8,128)(2,1)} %collective-permute-done.2.refs_1_.refs_2_, bf16[320,2304]{1,0:T(8,128)(2,1)} %copy-done.3, bf16[320,2304]{1,0:T(8,128)(2,1)} %copy-done, ...), custom_call_target="tpu_custom_call" | custom-call | tf_op jit(solution)/shard_map/project/pallas_call | solution.py:208
  124.5 1.2 collective-permute-done.11.refs_4_
  125.7 6.0 %collective-permute-done.12.refs_6_ = bf16[160,896]{1,0:T(8,128)(2,1)S(1)} collective-permute-done((bf16[160,896]{1,0:T(8,128)(2,1)}, bf16[160,896]{1,0:T(8,128)(2,1)S(1)}, u32[]{:S(2)}, u32[]{:S(2)}) %collective-permute-start.12) | collective-permute-done | bytes 286752 | tf_op jit(solution)/shard_map/rot_first_1/ppermute | solution.py:232
  131.7 1.6 collective-permute-start.13
  133.3 0.5 collective-permute-start.17
  133.9 1.6 collective-permute-start.15
  135.4 1.3 collective-permute-start.16
  136.8 0.0 collective-permute-start.10
  136.8 11.0 %collective-permute-done.17.refs_8_.refs_10_ = bf16[160,896]{1,0:T(8,128)(2,1)S(1)} collective-permute-done((bf16[160,896]{1,0:T(8,128)(2,1)S(1)}, bf16[160,896]{1,0:T(8,128)(2,1)S(1)}, u32[]{:S(2)}, u32[]{:S(2)}) %collective-permute-start.17) | collective-permute-done | bytes 286752 | tf_op jit(solution)/shard_map/rot_first_dp/ppermute | solution.py:237
  147.8 1.4 collective-permute-done.16.refs_7_
  149.1 0.0 collective-permute-done.13.mine_ref
  149.2 1.4 collective-permute-start.18
  150.6 1.6 collective-permute-start.19
  152.2 0.0 collective-permute-start.14
  152.2 1.6 collective-permute-start.21
  153.8 0.0 collective-permute-done.10.theirs_ref
  153.8 0.5 collective-permute-start.20
  154.3 0.2 copy-done.21
  154.6 2.9 %masked_windows.2.refs_2_ = bf16[3,1024,256]{2,1,0:T(8,128)(2,1)} custom-call(s32[1]{0:T(128)} %bitcast.3.core_ref, s32[1,3]{1,0:T(1,128)} %refs_0_.3, bf16[320,512]{1,0:T(8,128)(2,1)} %project.1.mine_ref, bf16[320,512]{1,0:T(8,128)(2,1)} %copy-done.21), custom_call_target="tpu_custom_call" | custom-call | tf_op jit(solution)/shard_map/masked_windows/pallas_call | solution.py:42
  157.5 7.6 %collective-permute-done.18.refs_5_ = bf16[160,896]{1,0:T(8,128)(2,1)S(1)} collective-permute-done((bf16[160,896]{1,0:T(8,128)(2,1)S(1)}, bf16[160,896]{1,0:T(8,128)(2,1)S(1)}, u32[]{:S(2)}, u32[]{:S(2)}) %collective-permute-start.18) | collective-permute-done | bytes 286752 | tf_op jit(solution)/shard_map/rot_third_0/ppermute | solution.py:232
  165.2 0.0 copy-start.22
  165.2 0.8 copy-done.22
  166.0 2.8 %masked_windows.3.refs_3_ = bf16[3,1024,256]{2,1,0:T(8,128)(2,1)} custom-call(s32[1]{0:T(128)} %bitcast.3.core_ref, s32[1,3]{1,0:T(1,128)} %copy-done.26, bf16[320,512]{1,0:T(8,128)(2,1)} %copy-done.20, bf16[320,512]{1,0:T(8,128)(2,1)} %copy-done.22), custom_call_target="tpu_custom_call" | custom-call | tf_op jit(solution)/shard_map/masked_windows/pallas_call | solution.py:42
  168.8 0.0 collective-permute-done.20.refs_8_
  168.8 1.6 collective-permute-start.22
  170.4 0.6 pad_add_fusion.choice_ref
  171.0 0.6 pad_add_fusion.1.choice_ref
  171.7 7.7 %squared_sums.2.refs_12_ = f32[1024,1792]{1,0:T(8,128)} custom-call(s32[1]{0:T(128)} %bitcast.13.place_ref, s32[4]{0:T(128)} %pad_add_fusion.1.choice_ref, s32[1,3]{1,0:T(1,128)} %refs_0_.3, s32[1,3]{1,0:T(1,128)} %copy-done.26, bf16[3,1024,256]{2,1,0:T(8,128)(2,1)} %masked_windows.2.refs_2_, bf16[3,1024,256]{2,1,0:T(8,128)(2,1)} %masked_windows.3.refs_3_, ...), custom_call_target="tpu_custom_call" | custom-call | tf_op jit(solution)/shard_map/squared_sums/pallas_call | solution.py:114
  179.4 0.7 copy-done.16
  180.1 7.7 %squared_sums.3 = f32[1024,1792]{1,0:T(8,128)} custom-call(s32[1]{0:T(128)} %bitcast.place_ref, s32[4]{0:T(128)} %pad_add_fusion.choice_ref, s32[1,3]{1,0:T(1,128)} %refs_0_.3, s32[1,3]{1,0:T(1,128)} %copy-done.26, bf16[3,1024,256]{2,1,0:T(8,128)(2,1)} %masked_windows.2.refs_2_, ...), custom_call_target="tpu_custom_call", output_to_operand_aliasing={{}: (14, {})} | custom-call | tf_op jit(solution)/shard_map/squared_sums/pallas_call | solution.py:114
  (57 shorter events, 0.3 us)
Async XLA Ops:
  0.0 1.4 copy-start.19
  0.0 4.6 %copy-start.25 = (s32[1,3]{1,0:T(1,128)S(1)}, s32[1,3]{1,0:T(1,128)}, u32[]{:S(2)}) copy-start(s32[1,3]{1,0:T(1,128)} %refs_0_.3) | copy-start | bytes 40
  1.4 5.3 %copy-start.1 = (bf16[320,2304]{1,0:T(8,128)(2,1)}, bf16[320,2304]{1,0:T(8,128)(2,1)S(1)}, u32[]{:S(2)}) copy-start(bf16[320,2304]{1,0:T(8,128)(2,1)S(1)} %constant_dynamic-update-slice_fusion.refs_0_) | copy-start | bytes 4423684
  1.4 5.3 %collective-permute-start.1 = (bf16[320,2304]{1,0:T(8,128)(2,1)S(1)}, bf16[320,2304]{1,0:T(8,128)(2,1)S(1)}, u32[]{:S(2)}, u32[]{:S(2)}) collective-permute-start(bf16[320,2304]{1,0:T(8,128)(2,1)S(1)} %constant_dynamic-update-slice_fusion.refs_0_), channel_id=1, source_target_pairs={{0,2},{2,0},{1,3},{3,1},{4,6},{6,4},{5,7},{7,5},{8,10},{10,8},{9,1... | collective-permute-start | bytes 4423688 | tf_op jit(solution)/shard_map/tokens_0_cols_0/ppermute | solution.py:237
  2.0 36.6 %collective-permute-start.2 = (bf16[320,2304]{1,0:T(8,128)(2,1)S(1)}, bf16[320,2304]{1,0:T(8,128)(2,1)}, u32[]{:S(2)}, u32[]{:S(2)}) collective-permute-start(bf16[320,2304]{1,0:T(8,128)(2,1)S(1)} %constant_dynamic-update-slice_fusion.refs_0_), channel_id=1, source_target_pairs={{0,4},{4,12},{12,8},{8,0},{1,5},{5,13},{13,9},{9,1},{2,6},{6,14},{... | collective-permute-start | bytes 4423688 | tf_op jit(solution)/shard_map/tokens_first/ppermute | solution.py:232
  4.6 10.3 %collective-permute-start = (s32[1,3]{1,0:T(1,128)S(1)}, s32[1,3]{1,0:T(1,128)S(1)}, u32[]{:S(2)}, u32[]{:S(2)}) collective-permute-start(s32[1,3]{1,0:T(1,128)S(1)} %copy-done.25), channel_id=1, source_target_pairs={{0,1},{1,0},{2,3},{3,2},{4,5},{5,4},{6,7},{7,6},{8,9},{9,8},{10,11... | collective-permute-start | bytes 44 | tf_op jit(solution)/shard_map/lengths_dp/ppermute | solution.py:237
  6.8 1.1 copy-start.2
  14.9 35.7 %copy-start.26 = (s32[1,3]{1,0:T(1,128)}, s32[1,3]{1,0:T(1,128)S(1)}, u32[]{:S(2)}) copy-start(s32[1,3]{1,0:T(1,128)S(1)} %collective-permute-done.lengths_ref.refs_1_) | copy-start | bytes 40
  38.6 3.5 %collective-permute-start.3 = (bf16[320,2304]{1,0:T(8,128)(2,1)}, bf16[320,2304]{1,0:T(8,128)(2,1)S(1)}, u32[]{:S(2)}, u32[]{:S(2)}) collective-permute-start(bf16[320,2304]{1,0:T(8,128)(2,1)} %collective-permute-done.2.refs_1_.refs_2_), channel_id=1, source_target_pairs={{0,2},{2,0},{1,3},{3,1},{4,6},{6,4},{5,7},{7,5},{8,10},{10,8},{9,1... | collective-permute-start | bytes 4423688 | tf_op jit(solution)/shard_map/tokens_1_cols_0/ppermute | solution.py:237
  38.6 35.8 %collective-permute-start.4 = (bf16[320,2304]{1,0:T(8,128)(2,1)}, bf16[320,2304]{1,0:T(8,128)(2,1)S(1)}, u32[]{:S(2)}, u32[]{:S(2)}) collective-permute-start(bf16[320,2304]{1,0:T(8,128)(2,1)} %collective-permute-done.2.refs_1_.refs_2_), channel_id=1, source_target_pairs={{0,4},{4,12},{12,8},{8,0},{1,5},{5,13},{13,9},{9,1},{2,6},{6,14},{... | collective-permute-start | bytes 4423688 | tf_op jit(solution)/shard_map/tokens_second/ppermute | solution.py:232
  42.1 1.1 copy-start.3
  74.4 3.3 %copy-start = (bf16[320,2304]{1,0:T(8,128)(2,1)}, bf16[320,2304]{1,0:T(8,128)(2,1)S(1)}, u32[]{:S(2)}) copy-start(bf16[320,2304]{1,0:T(8,128)(2,1)S(1)} %collective-permute-done.4.refs_1_.refs_4_) | copy-start | bytes 4423684
  74.4 3.3 %collective-permute-start.5 = (bf16[320,2304]{1,0:T(8,128)(2,1)S(1)}, bf16[320,2304]{1,0:T(8,128)(2,1)S(1)}, u32[]{:S(2)}, u32[]{:S(2)}) collective-permute-start(bf16[320,2304]{1,0:T(8,128)(2,1)S(1)} %collective-permute-done.4.refs_1_.refs_4_), channel_id=1, source_target_pairs={{0,2},{2,0},{1,3},{3,1},{4,6},{6,4},{5,7},{7,5},{8,10},{10,8},{9,1... | collective-permute-start | bytes 4423688 | tf_op jit(solution)/shard_map/tokens_2_cols_0/ppermute | solution.py:237
  74.5 28.6 %collective-permute-start.7 = (bf16[320,1792]{1,0:T(8,128)(2,1)S(1)}, bf16[320,1792]{1,0:T(8,128)(2,1)S(1)}, u32[]{:S(2)}, u32[]{:S(2)}) collective-permute-start(bf16[320,1792]{1,0:T(8,128)(2,1)S(1)} %slice.7), channel_id=1, source_target_pairs={{0,4},{4,12},{12,8},{8,0},{1,5},{5,13},{13,9},{9,1},{2,6},{6,14},{... | collective-permute-start | bytes 3440648 | tf_op jit(solution)/shard_map/grad_third/ppermute | solution.py:232
  77.7 1.1 copy-start.4
  103.1 2.8 %copy-start.5 = (bf16[320,1792]{1,0:T(8,128)(2,1)}, bf16[320,1792]{1,0:T(8,128)(2,1)S(1)}, u32[]{:S(2)}) copy-start(bf16[320,1792]{1,0:T(8,128)(2,1)S(1)} %collective-permute-done.7.refs_1_) | copy-start | bytes 3440644
  103.1 2.8 %collective-permute-start.8 = (bf16[320,1792]{1,0:T(8,128)(2,1)S(1)}, bf16[320,1792]{1,0:T(8,128)(2,1)S(1)}, u32[]{:S(2)}, u32[]{:S(2)}) collective-permute-start(bf16[320,1792]{1,0:T(8,128)(2,1)S(1)} %collective-permute-done.7.refs_1_), channel_id=1, source_target_pairs={{0,2},{2,0},{1,3},{3,1},{4,6},{6,4},{5,7},{7,5},{8,10},{10,8},{9,1... | collective-permute-start | bytes 3440648 | tf_op jit(solution)/shard_map/tokens_3_cols_0/ppermute | solution.py:237
  104.4 10.9 %collective-permute-start.6 = (bf16[320,512]{1,0:T(8,128)(2,1)S(1)}, bf16[320,512]{1,0:T(8,128)(2,1)S(1)}, u32[]{:S(2)}, u32[]{:S(2)}) collective-permute-start(bf16[320,512]{1,0:T(8,128)(2,1)S(1)} %slice.6), channel_id=1, source_target_pairs={{0,4},{4,12},{12,8},{8,0},{1,5},{5,13},{13,9},{9,1},{2,6},{6,14},{... | collective-permute-start | bytes 983048 | tf_op jit(solution)/shard_map/act_third/ppermute | solution.py:232
  105.9 1.0 copy-start.6
  115.2 2.9 %copy-start.17 = (bf16[320,512]{1,0:T(8,128)(2,1)}, bf16[320,512]{1,0:T(8,128)(2,1)S(1)}, u32[]{:S(2)}) copy-start(bf16[320,512]{1,0:T(8,128)(2,1)S(1)} %collective-permute-done.6.refs_6_) | copy-start | bytes 983044
  115.2 2.9 %collective-permute-start.9 = (bf16[320,512]{1,0:T(8,128)(2,1)S(1)}, bf16[320,512]{1,0:T(8,128)(2,1)S(1)}, u32[]{:S(2)}, u32[]{:S(2)}) collective-permute-start(bf16[320,512]{1,0:T(8,128)(2,1)S(1)} %collective-permute-done.6.refs_6_), channel_id=1, source_target_pairs={{0,2},{2,0},{1,3},{3,1},{4,6},{6,4},{5,7},{7,5},{8,10},{10,8},{9,1... | collective-permute-start | bytes 983048 | tf_op jit(solution)/shard_map/act_third_cols/ppermute | solution.py:237
  115.2 10.5 %collective-permute-start.11 = (bf16[160,896]{1,0:T(8,128)(2,1)}, bf16[160,896]{1,0:T(8,128)(2,1)S(1)}, u32[]{:S(2)}, u32[]{:S(2)}) collective-permute-start(bf16[160,896]{1,0:T(8,128)(2,1)} %get-tuple-element.20.refs_4_), channel_id=1, source_target_pairs={{0,4},{4,12},{12,8},{8,0},{1,5},{5,13},{13,9},{9,1},{2,6},{6,14},{... | collective-permute-start | bytes 860168 | tf_op jit(solution)/shard_map/rot_first_0/ppermute | solution.py:232
  116.9 14.8 %collective-permute-start.12 = (bf16[160,896]{1,0:T(8,128)(2,1)}, bf16[160,896]{1,0:T(8,128)(2,1)S(1)}, u32[]{:S(2)}, u32[]{:S(2)}) collective-permute-start(bf16[160,896]{1,0:T(8,128)(2,1)} %get-tuple-element.21.refs_6_), channel_id=1, source_target_pairs={{4,0},{12,4},{8,12},{0,8},{5,1},{13,5},{9,13},{1,9},{6,2},{14,6},{... | collective-permute-start | bytes 860168 | tf_op jit(solution)/shard_map/rot_first_1/ppermute | solution.py:232
  118.1 31.0 %copy-start.7 = (bf16[160,896]{1,0:T(8,128)(2,1)S(1)}, bf16[160,896]{1,0:T(8,128)(2,1)}, u32[]{:S(2)}) copy-start(bf16[160,896]{1,0:T(8,128)(2,1)} %get-tuple-element.20.refs_4_) | copy-start | bytes 860164
  118.2 0.8 copy-start.18
  124.5 27.7 %copy-start.8 = (bf16[160,896]{1,0:T(8,128)(2,1)S(1)}, bf16[160,896]{1,0:T(8,128)(2,1)}, u32[]{:S(2)}) copy-start(bf16[160,896]{1,0:T(8,128)(2,1)} %get-tuple-element.21.refs_6_) | copy-start | bytes 860164
  125.7 31.7 %copy-start.11 = (bf16[160,896]{1,0:T(8,128)(2,1)}, bf16[160,896]{1,0:T(8,128)(2,1)S(1)}, u32[]{:S(2)}) copy-start(bf16[160,896]{1,0:T(8,128)(2,1)S(1)} %collective-permute-done.11.refs_4_) | copy-start | bytes 860164
  131.7 25.7 %copy-start.12 = (bf16[160,896]{1,0:T(8,128)(2,1)}, bf16[160,896]{1,0:T(8,128)(2,1)S(1)}, u32[]{:S(2)}) copy-start(bf16[160,896]{1,0:T(8,128)(2,1)S(1)} %collective-permute-done.12.refs_6_) | copy-start | bytes 860164
  131.7 17.4 %collective-permute-start.13 = (bf16[320,512]{1,0:T(8,128)(2,1)}, bf16[320,512]{1,0:T(8,128)(2,1)S(1)}, u32[]{:S(2)}, u32[]{:S(2)}) collective-permute-start(bf16[320,512]{1,0:T(8,128)(2,1)} %project.1.mine_ref), channel_id=1, source_target_pairs={{0,1},{1,0},{2,3},{3,2},{4,5},{5,4},{6,7},{7,6},{8,9},{9,8},{10,11... | collective-permute-start | bytes 983048 | tf_op jit(solution)/shard_map/act_dp/ppermute | solution.py:237
  133.3 14.4 %collective-permute-start.17 = (bf16[160,896]{1,0:T(8,128)(2,1)S(1)}, bf16[160,896]{1,0:T(8,128)(2,1)S(1)}, u32[]{:S(2)}, u32[]{:S(2)}) collective-permute-start(bf16[160,896]{1,0:T(8,128)(2,1)S(1)} %broadcast_select_fusion.3), channel_id=1, source_target_pairs={{0,1},{1,0},{2,3},{3,2},{4,5},{5,4},{6,7},{7,6},{8,9},{9,8},{10,11... | collective-permute-start | bytes 860168 | tf_op jit(solution)/shard_map/rot_first_dp/ppermute | solution.py:237
  133.9 13.9 %collective-permute-start.15 = (bf16[160,896]{1,0:T(8,128)(2,1)S(1)}, bf16[160,896]{1,0:T(8,128)(2,1)S(1)}, u32[]{:S(2)}, u32[]{:S(2)}) collective-permute-start(bf16[160,896]{1,0:T(8,128)(2,1)S(1)} %collective-permute-done.11.refs_4_), channel_id=1, source_target_pairs={{0,4},{4,12},{12,8},{8,0},{1,5},{5,13},{13,9},{9,1},{2,6},{6,14},{... | collective-permute-start | bytes 860168 | tf_op jit(solution)/shard_map/rot_second_0/ppermute | solution.py:232
  135.4 13.7 %collective-permute-start.16 = (bf16[160,896]{1,0:T(8,128)(2,1)S(1)}, bf16[160,896]{1,0:T(8,128)(2,1)S(1)}, u32[]{:S(2)}, u32[]{:S(2)}) collective-permute-start(bf16[160,896]{1,0:T(8,128)(2,1)S(1)} %collective-permute-done.12.refs_6_), channel_id=1, source_target_pairs={{4,0},{12,4},{8,12},{0,8},{5,1},{13,5},{9,13},{1,9},{6,2},{14,6},{... | collective-permute-start | bytes 860168 | tf_op jit(solution)/shard_map/rot_second_1/ppermute | solution.py:232
  136.8 17.1 %collective-permute-start.10 = (bf16[320,512]{1,0:T(8,128)(2,1)}, bf16[320,512]{1,0:T(8,128)(2,1)S(1)}, u32[]{:S(2)}, u32[]{:S(2)}) collective-permute-start(bf16[320,512]{1,0:T(8,128)(2,1)} %project.1.mine_ref), channel_id=1, source_target_pairs={{0,2},{2,0},{1,3},{3,1},{4,6},{6,4},{5,7},{7,5},{8,10},{10,8},{9,1... | collective-permute-start | bytes 983048 | tf_op jit(solution)/shard_map/rot_act_cols/ppermute | solution.py:237
  147.8 9.7 %copy-start.15 = (bf16[160,896]{1,0:T(8,128)(2,1)}, bf16[160,896]{1,0:T(8,128)(2,1)S(1)}, u32[]{:S(2)}) copy-start(bf16[160,896]{1,0:T(8,128)(2,1)S(1)} %collective-permute-done.17.refs_8_.refs_10_) | copy-start | bytes 860164
  147.8 9.7 %copy-start.9 = (bf16[160,896]{1,0:T(8,128)(2,1)}, bf16[160,896]{1,0:T(8,128)(2,1)S(1)}, u32[]{:S(2)}) copy-start(bf16[160,896]{1,0:T(8,128)(2,1)S(1)} %collective-permute-done.15.refs_5_) | copy-start | bytes 860164
  149.1 8.3 %copy-start.10 = (bf16[160,896]{1,0:T(8,128)(2,1)}, bf16[160,896]{1,0:T(8,128)(2,1)S(1)}, u32[]{:S(2)}) copy-start(bf16[160,896]{1,0:T(8,128)(2,1)S(1)} %collective-permute-done.16.refs_7_) | copy-start | bytes 860164
  149.2 8.3 %copy-start.20 = (bf16[320,512]{1,0:T(8,128)(2,1)}, bf16[320,512]{1,0:T(8,128)(2,1)S(1)}, u32[]{:S(2)}) copy-start(bf16[320,512]{1,0:T(8,128)(2,1)S(1)} %collective-permute-done.13.mine_ref) | copy-start | bytes 983044
  149.2 15.9 %collective-permute-start.18 = (bf16[160,896]{1,0:T(8,128)(2,1)S(1)}, bf16[160,896]{1,0:T(8,128)(2,1)S(1)}, u32[]{:S(2)}, u32[]{:S(2)}) collective-permute-start(bf16[160,896]{1,0:T(8,128)(2,1)S(1)} %collective-permute-done.15.refs_5_), channel_id=1, source_target_pairs={{0,4},{4,12},{12,8},{8,0},{1,5},{5,13},{13,9},{9,1},{2,6},{6,14},{... | collective-permute-start | bytes 860168 | tf_op jit(solution)/shard_map/rot_third_0/ppermute | solution.py:232
  150.6 14.5 %collective-permute-start.19 = (bf16[160,896]{1,0:T(8,128)(2,1)S(1)}, bf16[160,896]{1,0:T(8,128)(2,1)S(1)}, u32[]{:S(2)}, u32[]{:S(2)}) collective-permute-start(bf16[160,896]{1,0:T(8,128)(2,1)S(1)} %collective-permute-done.16.refs_7_), channel_id=1, source_target_pairs={{4,0},{12,4},{8,12},{0,8},{5,1},{13,5},{9,13},{1,9},{6,2},{14,6},{... | collective-permute-start | bytes 860168 | tf_op jit(solution)/shard_map/rot_third_1/ppermute | solution.py:232
  152.2 13.0 %collective-permute-start.14 = (bf16[320,512]{1,0:T(8,128)(2,1)S(1)}, bf16[320,512]{1,0:T(8,128)(2,1)S(1)}, u32[]{:S(2)}, u32[]{:S(2)}) collective-permute-start(bf16[320,512]{1,0:T(8,128)(2,1)S(1)} %collective-permute-done.13.mine_ref), channel_id=1, source_target_pairs={{0,2},{2,0},{1,3},{3,1},{4,6},{6,4},{5,7},{7,5},{8,10},{10,8},{9,1... | collective-permute-start | bytes 983048 | tf_op jit(solution)/shard_map/rot_act_cols/ppermute | solution.py:237
  152.2 16.6 %collective-permute-start.21 = (bf16[160,896]{1,0:T(8,128)(2,1)S(1)}, bf16[160,896]{1,0:T(8,128)(2,1)S(1)}, u32[]{:S(2)}, u32[]{:S(2)}) collective-permute-start(bf16[160,896]{1,0:T(8,128)(2,1)S(1)} %broadcast_select_fusion), channel_id=1, source_target_pairs={{0,1},{1,0},{2,3},{3,2},{4,5},{5,4},{6,7},{7,6},{8,9},{9,8},{10,11... | collective-permute-start | bytes 860168 | tf_op jit(solution)/shard_map/rot_second_dp_1/ppermute | solution.py:237
  153.8 0.7 copy-start.21
  153.8 15.0 %collective-permute-start.20 = (bf16[160,896]{1,0:T(8,128)(2,1)S(1)}, bf16[160,896]{1,0:T(8,128)(2,1)S(1)}, u32[]{:S(2)}, u32[]{:S(2)}) collective-permute-start(bf16[160,896]{1,0:T(8,128)(2,1)S(1)} %broadcast_select_fusion.1), channel_id=1, source_target_pairs={{0,1},{1,0},{2,3},{3,2},{4,5},{5,4},{6,7},{7,6},{8,9},{9,8},{10,11... | collective-permute-start | bytes 860168 | tf_op jit(solution)/shard_map/rot_second_dp_0/ppermute | solution.py:237
  165.1 3.7 %copy-start.13 = (bf16[160,896]{1,0:T(8,128)(2,1)}, bf16[160,896]{1,0:T(8,128)(2,1)S(1)}, u32[]{:S(2)}) copy-start(bf16[160,896]{1,0:T(8,128)(2,1)S(1)} %collective-permute-done.18.refs_5_) | copy-start | bytes 860164
  165.1 3.7 %copy-start.14 = (bf16[160,896]{1,0:T(8,128)(2,1)}, bf16[160,896]{1,0:T(8,128)(2,1)S(1)}, u32[]{:S(2)}) copy-start(bf16[160,896]{1,0:T(8,128)(2,1)S(1)} %collective-permute-done.19.refs_7_) | copy-start | bytes 860164
  165.2 0.8 copy-start.22
  168.8 2.9 %copy-start.23 = (bf16[160,896]{1,0:T(8,128)(2,1)}, bf16[160,896]{1,0:T(8,128)(2,1)S(1)}, u32[]{:S(2)}) copy-start(bf16[160,896]{1,0:T(8,128)(2,1)S(1)} %collective-permute-done.21.refs_9_) | copy-start | bytes 860164
  168.8 2.8 %copy-start.24 = (bf16[160,896]{1,0:T(8,128)(2,1)}, bf16[160,896]{1,0:T(8,128)(2,1)S(1)}, u32[]{:S(2)}) copy-start(bf16[160,896]{1,0:T(8,128)(2,1)S(1)} %collective-permute-done.20.refs_8_) | copy-start | bytes 860164
  168.8 10.6 %collective-permute-start.22 = (bf16[160,896]{1,0:T(8,128)(2,1)S(1)}, bf16[160,896]{1,0:T(8,128)(2,1)S(1)}, u32[]{:S(2)}, u32[]{:S(2)}) collective-permute-start(bf16[160,896]{1,0:T(8,128)(2,1)S(1)} %broadcast_select_fusion.2), channel_id=1, source_target_pairs={{0,1},{1,0},{2,3},{3,2},{4,5},{5,4},{6,7},{7,6},{8,9},{9,8},{10,11... | collective-permute-start | bytes 860168 | tf_op jit(solution)/shard_map/rot_third_dp/ppermute | solution.py:237
  179.4 0.7 copy-start.16

commit v3 on v2

v3 whole, which is shorter than its diff:
```python
import functools

import jax
import jax.numpy as jnp
from jax import lax
from jax.experimental import pallas as pl
from jax.experimental.pallas import tpu as pltpu
from jax.sharding import PartitionSpec as P

STEP = 64
VMEM_BYTES = 56 * 1024 * 1024


def span_of(lengths_ref, example):
    begin = 0
    for before in range(example):
        begin = begin + lengths_ref[0, before]
    return begin, begin + lengths_ref[0, example]


def window_start(begin, slack):
    return pl.multiple_of(jnp.minimum(begin // STEP * STEP, slack), STEP)


def mask_kernel(examples, window, place_at, plan_ref, lengths_ref, mine_ref, theirs_ref, out_ref):
    slack = mine_ref.shape[0] - window
    half = mine_ref.shape[1]
    for example in range(examples):
        begin, end = span_of(lengths_ref, example)
        start = window_start(begin, slack)
        token = start + lax.broadcasted_iota(jnp.int32, (window, 1), 0)
        inside = (token >= begin) & (token < end)
        for place, ref in ((plan_ref[place_at], mine_ref), (1 - plan_ref[place_at], theirs_ref)):
            rows = ref[pl.ds(start, window), :]
            kept = jnp.where(inside, rows.astype(jnp.float32), 0.0)
            out_ref[example, pl.ds(pl.multiple_of(place * half, half), half), :] = kept.T.astype(out_ref.dtype)


def masked_windows(plan, place_at, lengths, mine, theirs, window):
    tokens, half = mine.shape
    examples = lengths.shape[1]
    return pl.pallas_call(
        functools.partial(mask_kernel, examples, window, place_at),
        name="masked_windows",
        out_shape=jax.ShapeDtypeStruct((examples, 2 * half, window), mine.dtype),
        in_specs=[pl.BlockSpec(memory_space=pltpu.SMEM)] * 2 + [pl.BlockSpec(memory_space=pltpu.VMEM)] * 2,
        out_specs=pl.BlockSpec(memory_space=pltpu.VMEM),
        compiler_params=pltpu.CompilerParams(vmem_limit_bytes=VMEM_BYTES),
    )(plan, lengths, mine, theirs)


def square_kernel(chunks, examples, window, total, plan_ref, *refs):
    blocks = len(chunks)
    lengths_refs, act_inputs, refs = refs[:blocks], refs[blocks : 2 * blocks], refs[2 * blocks :]
    act_sem, sem, refs = refs[-1], refs[-2], refs[:-2]
    out_ref, grad_refs, act_refs = refs[-2 * blocks - 1], refs[-2 * blocks : -blocks], refs[-blocks:]
    tall = out_ref.shape[0]
    steps = act_refs[0].shape[1] // tall
    now = pl.program_id(0)

    def act_copy(block, step):
        rows = pl.ds(pl.multiple_of(step * tall, tall), tall)
        return pltpu.make_async_copy(act_inputs[block].at[:, rows, :], act_refs[block].at[:, rows, :], act_sem.at[block, step])

    @pl.when(now == 0)
    def _():
        landed, at, place = [], 0, 0
        for block in range(blocks):
            act_copy(block, 0).start()
            top = 0
            for rows, arrays, choice_at in chunks[block]:
                target = grad_refs[block].at[pl.ds(top, rows), :]
                for index in range(arrays):

                    @pl.when((plan_ref[choice_at] == index) | (arrays == 1))
                    def _():
                        pltpu.make_async_copy(refs[at + index], target, sem.at[place]).start()

                landed.append(pltpu.make_async_copy(refs[at], target, sem.at[place]))
                top, at, place = top + rows, at + arrays, place + 1
        for step in range(1, steps):
            for block in range(blocks):
                act_copy(block, step).start()
        for copy in landed:
            copy.wait()

    for block in range(blocks):
        act_copy(block, now).wait()

    rows, columns = out_ref.shape
    wide, high = min(columns, 256), min(rows, 128)
    for left in range(0, columns, wide):
        right = min(left + wide, columns)
        for top in range(0, rows, high):
            acc = None
            for block in range(blocks):
                slack = grad_refs[block].shape[0] - window
                for example in range(examples):
                    begin, _ = span_of(lengths_refs[block], example)
                    product = jnp.dot(
                        act_refs[block][example, pl.ds(pl.multiple_of(now * rows + top, high), high), :],
                        grad_refs[block][pl.ds(window_start(begin, slack), window), left:right],
                        preferred_element_type=jnp.float32,
                    )
                    acc = product * product if acc is None else acc + product * product
            out_ref[top : top + high, left:right] = acc / total


def squared_sums(plan, lengths, acts, grads, window, total, places=1, place_at=0, onto=None):
    blocks = len(acts)
    examples, directions, _ = acts[0].shape
    columns = grads[0][0][1][0].shape[1]
    chunks = [[(arrays[0].shape[0], len(arrays), choice_at) for choice_at, arrays in block] for block in grads]
    flat = [x for block in grads for _, arrays in block for x in arrays]
    tall = min(directions, 512)
    operands = [*lengths, *acts, *flat]
    in_specs = (
        [pl.BlockSpec(memory_space=pltpu.SMEM)] * blocks
        + [pl.BlockSpec(memory_space=pl.ANY)] * (blocks + len(flat))
    )
    aliases = {}
    if onto is not None:
        aliases = {1 + len(operands): 0}
        operands.append(onto)
        in_specs.append(pl.BlockSpec(memory_space=pl.ANY))
    return pl.pallas_call(
        functools.partial(square_kernel, chunks, examples, window, total),
        name="squared_sums",
        out_shape=jax.ShapeDtypeStruct((directions, places * columns), jnp.float32),
        grid_spec=pltpu.PrefetchScalarGridSpec(
            num_scalar_prefetch=1,
            grid=(directions // tall,),
            in_specs=in_specs,
            out_specs=pl.BlockSpec((tall, columns), lambda i, plan: (i, plan[place_at])),
            scratch_shapes=[pltpu.VMEM((sum(c[0] for c in block), columns), jnp.bfloat16) for block in chunks]
            + [pltpu.VMEM(x.shape, x.dtype) for x in acts]
            + [pltpu.SemaphoreType.DMA((sum(len(block) for block in chunks),))]
            + [pltpu.SemaphoreType.DMA((blocks, directions // tall))],
        ),
        input_output_aliases=aliases,
        compiler_params=pltpu.CompilerParams(vmem_limit_bytes=VMEM_BYTES),
    )(plan, *operands)


def fold_kernel(started, parts, offsets_ref, *refs):
    start_ref = refs[0] if started else None
    mine, theirs = refs[started : started + parts], refs[started + parts : started + 2 * parts]
    basis_ref, *out_refs, sum_ref = refs[started + 2 * parts :]
    step = pl.program_id(0)

    def product(pieces):
        rows = pieces[0][...] if parts == 1 else jnp.concatenate([x[...] for x in pieces], axis=0)
        return jnp.dot(rows, basis_ref[...], preferred_element_type=jnp.float32)

    @pl.when(step == 0)
    def _():
        sum_ref[...] = start_ref[...] + product(mine) if started else product(mine)

    @pl.when(step == 1)
    def _():
        total = sum_ref[...] + product(theirs)
        rows = total.shape[0] // len(out_refs)
        for index, out_ref in enumerate(out_refs):
            out_ref[...] = total[index * rows : index * rows + rows, :].astype(out_ref.dtype)


def fold_block(start, mine, theirs, basis, features, offsets, place, kind, chunks=1):
    tokens = sum(x.shape[0] for x in mine)
    columns = basis.shape[1]
    started = start is not None
    sections = [pl.BlockSpec((x.shape[0], features), lambda i, offsets: (0, 0)) for x in (*mine, *theirs)]
    return pl.pallas_call(
        functools.partial(fold_kernel, started, len(mine)),
        name=f"fold_{place}",
        out_shape=[jax.ShapeDtypeStruct((tokens // chunks, columns), kind)] * chunks,
        grid_spec=pltpu.PrefetchScalarGridSpec(
            num_scalar_prefetch=1,
            grid=(2,),
            in_specs=[pl.BlockSpec((tokens, columns), lambda i, offsets: (0, 0))] * started
            + sections
            + [pl.BlockSpec((features, columns), lambda i, offsets: (offsets[2 * place + i], 0))],
            out_specs=[pl.BlockSpec((tokens // chunks, columns), lambda i, offsets: (0, 0))] * chunks,
            scratch_shapes=[pltpu.VMEM((tokens, columns), jnp.float32)],
        ),
        compiler_params=pltpu.CompilerParams(vmem_limit_bytes=VMEM_BYTES),
    )(offsets, *([start] if started else []), *mine, *theirs, basis)


def project_kernel(plan_ref, *refs):
    blocks, basis_ref, out_ref = refs[:-2], refs[-2], refs[-1]
    deep = blocks[0].shape[1]
    total = None
    for place, ref in enumerate(blocks):
        rows = pl.ds(pl.multiple_of(plan_ref[place] * deep, deep), deep)
        product = jnp.dot(ref[...], basis_ref[rows, :], preferred_element_type=jnp.float32)
        total = product if total is None else total + product
    out_ref[...] = total.astype(out_ref.dtype)


def project(blocks, basis, plan):
    return pl.pallas_call(
        project_kernel,
        name="project",
        out_shape=jax.ShapeDtypeStruct((blocks[0].shape[0], basis.shape[1]), basis.dtype),
        in_specs=[pl.BlockSpec(memory_space=pltpu.SMEM)] + [pl.BlockSpec(memory_space=pltpu.VMEM)] * (len(blocks) + 1),
        out_specs=pl.BlockSpec(memory_space=pltpu.VMEM),
        compiler_params=pltpu.CompilerParams(vmem_limit_bytes=VMEM_BYTES),
    )(plan, *blocks, basis)


RING = [(0, 1), (1, 3), (3, 2), (2, 0)]


def slots_of(row):
    before = jnp.where(row < 2, 2 - 2 * row, 7 - 2 * row)
    return row, before, 3 - row, 3 - before


def hop(x, what, back=False):
    with jax.named_scope(what):
        return lax.ppermute(x, "row", [hop[::-1] for hop in RING] if back else RING)


def swap(x, axis, what):
    with jax.named_scope(what):
        return lax.ppermute(x, axis, [(0, 1), (1, 0)])


def after(x, *others):
    return lax.optimization_barrier((x, *others))[0]


def chained(activations, gradients, q_act, basis_grad, lengths):
    tokens = activations.shape[0]
    total = 2 * lengths.shape[1]
    window = min(tokens, 256)
    half = tokens // 2
    row, core, me = lax.axis_index("row"), lax.axis_index("col"), lax.axis_index("dp")
    home = row // 2 == me
    outer = (row == 0) | (row == 3)
    spans = [lengths, swap(lengths, "dp", "lengths_dp")]
    places = [2 * x + c for x in slots_of(row) for c in (core, 1 - core)]
    turn = home == outer
    picks = [jnp.where(home, 0, 1), jnp.where(turn, 1, 0), jnp.where(turn, 0, 1)]
    place = jnp.where(home, row, 3 - row) % 2
    plan = jnp.stack([*places, *picks, place, 1 - place, core]).astype(jnp.int32)
    PICK, TURN, AGAIN, NEAR, FAR, CORE = range(8, 14)

    features = gradients.shape[1]

    def crossed(chunks, place):
        return [swap(x, "col", f"grad_{place}_cols_{i}") for i, x in enumerate(chunks)]

    def fold(start, mine, theirs, place):
        return fold_block(start, mine, theirs, basis_grad, features, plan, place, jnp.float32)[0]

    def piece(sums, x, place, i):
        theirs = swap(x, "col", f"grad_{place}_cols_{i}")
        kind = jnp.bfloat16 if place == 3 else jnp.float32
        return fold_block(sums, [x], [theirs], basis_grad, features, plan, place, kind)[0]

    own = [gradients[i : i + half] for i in (0, half)]
    sums = list(fold_block(None, own, crossed(own, 0), basis_grad, features, plan, 0, jnp.float32, 2))
    firsts = [after(hop(x, f"grad_first_{i}"), sums[i], spans[1]) for i, x in enumerate(own)]
    act_first = hop(after(activations, *sums), "act_first")
    seconds = [hop(after(x, act_first) if 0 else x, f"grad_second_{i}") for i, x in enumerate(firsts)]
    act_second = hop(act_first, "act_second")
    act_third = hop(act_second, "act_third")
    thirds = []
    for i in range(2):
        sums[i] = piece(sums[i], firsts[i], 1, i)
        thirds.append(hop(after(seconds[i], sums[i], *([act_second] if i else [])), f"grad_third_{i}"))
    sums[1] = piece(sums[1], seconds[1], 2, 1)
    acts = (activations, act_first, act_second, act_third)
    rotated = project([x for s in acts for x in (s, swap(s, "col", "act_cols"))], q_act, plan)
    other = swap(rotated, "dp", "act_dp")
    acts = [(x, swap(x, "col", "rot_act_cols")) for x in (rotated, other)]
    owns = [None, piece(sums[1], after(thirds[1], sums[1], rotated), 3, 1)]
    sums[0] = piece(after(sums[0], owns[1]) if 0 else sums[0], seconds[0], 2, 0)
    owns[0] = piece(sums[0], after(thirds[0], sums[0], owns[1], *acts[1]), 3, 0)

    acts = [masked_windows(plan, CORE, s, *x, window) for s, x in zip(spans, acts)]
    first = [hop(x, f"rot_first_{i}", i == 1) for i, x in enumerate(owns)]
    second = [None, hop(after(first[1], owns[0]), "rot_second_1", True)]
    second[0] = hop(first[0], "rot_second_0")
    cross_first = swap(jnp.where(turn, first[0], first[1]), "dp", "rot_first_dp")
    early = [jnp.where(home, s, o) for s, o in zip(second, owns)]
    early[1] = swap(early[1], "dp", "rot_second_dp_1")
    third = [None, hop(second[1], "rot_third_1", True)]
    third[0] = hop(after(second[0], third[1], cross_first, early[1]), "rot_third_0")
    early[0] = swap(early[0], "dp", "rot_second_dp_0")
    cross_third = jnp.where(turn, third[1], third[0])
    cross_third = swap(after(cross_third, *early, *acts), "dp", "rot_third_dp")

    near = [[(PICK, (o, s)) for o, s in zip(owns, second)], [(PICK, (x,)) for x in early]]
    far = [[(TURN, (first[0], third[0])), (AGAIN, (first[1], third[1]))], [(at, (cross_first, cross_third)) for at in (TURN, AGAIN)]]
    out = squared_sums(plan, spans, acts, near, window, total, 2, NEAR)
    return squared_sums(plan, spans, acts, far, window, total, 2, FAR, out)


def fold_with(basis, section):
    return jnp.dot(section, basis, preferred_element_type=jnp.float32).astype(jnp.bfloat16)


def gathered(activations, gradients, q_act, basis_grad, lengths):
    n_dp = lax.axis_size("dp")
    total = lengths.shape[1] * n_dp
    window = min(activations.shape[0], 256)
    me = lax.axis_index("dp")
    plan = jnp.stack([jnp.int32(0), lax.axis_index("col").astype(jnp.int32)])

    def shifted(x, k):
        return lax.ppermute(x, "dp", [(i, (i + k) % n_dp) for i in range(n_dp)])

    rotated_g = fold_with(basis_grad, lax.all_gather(gradients, ("row", "col"), axis=1, tiled=True))
    rotated = fold_with(q_act, lax.all_gather(activations, ("row", "col"), axis=1, tiled=True))
    acts, spans = [rotated], [lengths]
    for k in range(1, n_dp):
        acts.append(shifted(rotated, k))
        spans.append(shifted(lengths, k))
    acts = [masked_windows(plan, 1, s, x, swap(x, "col", "cols"), window) for x, s in zip(acts, spans)]

    rotated_g = lax.all_gather(rotated_g, "row", axis=1, tiled=True)
    columns = rotated_g.shape[1] // n_dp

    def columns_of(d):
        return lax.dynamic_slice_in_dim(rotated_g, d % n_dp * columns, columns, axis=1)

    grads = [columns_of(me)]
    for k in range(1, n_dp):
        grads.append(shifted(columns_of(me + k), k))
    return squared_sums(plan, spans, acts, [[(0, [x])] for x in grads], window, total)


def on_device(activations, gradients, q_act, q_grad, lengths):
    basis_grad = q_grad.reshape(q_grad.shape[0], q_grad.shape[2])
    fits = lax.axis_size("row") == 4 and lax.axis_size("dp") == 2 and lax.axis_size("col") == 2
    plan = chained if fits else gathered
    return plan(activations, gradients, q_act, basis_grad, lengths)


def solution(mesh):
    return jax.shard_map(
        on_device,
        mesh=mesh,
        in_specs=(
            P(("parts", "dp"), ("row", "col")),
            P(("parts", "dp"), ("row", "col")),
            P(None, ("row", "col")),
            P(None, "col", "row"),
            P(("parts", "dp"), None),
        ),
        out_specs=P(("parts", "row"), ("col", "dp")),
        check_vma=False,
    )
```

time: 188 us -> 174 us (0.926)
  waiting for transfers between devices: 98.5 us -> 57.7 us
  starting transfers between devices: 21.9 us -> 36.4 us
  Pallas kernels: 55.6 us -> 68.4 us
    ppermute x10 -> x15, waiting for transfers between devices: 81.8 us -> 49.6 us  [hop(): return lax.ppermute(x, 'row', [hop[::-1] for hop in RING] if back else RING)]
    pallas_call x4 -> x7, Pallas kernels: 28.9 us -> 41.1 us  [fold_block(): pl.pallas_call(functools.partial(fold_kernel, started, len(mine)), name=f...]
    ppermute x10 -> x15, starting transfers between devices: 14.1 us -> 25.7 us  [hop(): return lax.ppermute(x, 'row', [hop[::-1] for hop in RING] if back else RING)]
    ppermute x13 -> x20, waiting for transfers between devices: 16.6 us -> 8.07 us  [swap(): return lax.ppermute(x, axis, [(0, 1), (1, 0)])]
    ppermute x13 -> x20, starting transfers between devices: 7.82 us -> 10.7 us  [swap(): return lax.ppermute(x, axis, [(0, 1), (1, 0)])]
    unnamed x55 -> x82, local copies, waits for them, and re-layouts: 8.33 us -> 8.3 us
  transfers between devices with their start and end apart: 23 -> 35, of which waited for: 12 -> 16; matrix products, arithmetic and copies ran while one was open for 2% -> 0% of each run, Pallas kernels for 25% -> 35%
where the time goes in v3:
time: 174 us; the launch traced here: 173 us
  Pallas kernels  68.4 us (39%)
  waiting for transfers between devices  57.7 us (33%)
  starting transfers between devices  36.4 us (21%)
  local copies, waits for them, and re-layouts  10.3 us (6%)
    ppermute x15, waiting for transfers between devices, hop(): return lax.ppermute(x, 'row', [hop[::-1] for hop in RING] if back else RING)  49.6 us
    pallas_call x7, Pallas kernels, fold_block(): pl.pallas_call(functools.partial(fold_kernel, started, len(mine)), name=f...  41.1 us
    ppermute x15, starting transfers between devices, hop(): return lax.ppermute(x, 'row', [hop[::-1] for hop in RING] if back else RING)  25.7 us
    pallas_call x2, Pallas kernels, squared_sums(): pl.pallas_call(functools.partial(square_kernel, chunks, examples, window,...  16.4 us
    ppermute x20, starting transfers between devices, swap(): return lax.ppermute(x, axis, [(0, 1), (1, 0)])  10.7 us
    unnamed x82, local copies, waits for them, and re-layouts  8.3 us
    ppermute x20, waiting for transfers between devices, swap(): return lax.ppermute(x, axis, [(0, 1), (1, 0)])  8.07 us
    pallas_call x2, Pallas kernels, masked_windows(): pl.pallas_call(functools.partial(mask_kernel, examples, window, place_at)...  5.66 us
  transfers between devices with their start and end apart: 35, of which 16 were waited for; matrix products, arithmetic and copies ran while one was open for 0% of the time, Pallas kernels for 35%

profile of v3, /device:TPU:0, one launch (start us, length us, event | category | flops | bytes accessed | tf_op | source)
XLA Modules:
  0.0 173.4 jit_solution(17234747367302007711)
XLA Ops:
  0.0 1.3 fusion
  1.3 0.5 collective-permute-start.3
  1.9 0.1 collective-permute-start.2
  1.9 3.0 %collective-permute-start.18 = (bf16[160,1792]{1,0:T(8,128)(2,1)S(1)}, bf16[160,1792]{1,0:T(8,128)(2,1)S(1)}, u32[]{:S(2)}, u32[]{:S(2)}) collective-permute-start(bf16[160,1792]{1,0:T(8,128)(2,1)S(1)} %get-tuple-element.29.refs_1_), channel_id=1, source_target_pairs={{0,4},{4,12},{12,8},{8,0},{1,5},{5,13},{13,9},{9,1},{2,6},{6,14},{... | collective-permute-start | bytes 1720328 | tf_op jit(solution)/shard_map/grad_first_1/ppermute | solution.py:221
  4.9 0.7 stack.59.offsets_ref.plan_ref
  5.6 0.8 copy-done.13
  6.4 0.2 copy-done.14
  6.6 7.1 %fold_0.1 = (f32[160,896]{1,0:T(8,128)}, f32[160,896]{1,0:T(8,128)}) custom-call(s32[14]{0:T(128)} %stack.59.offsets_ref.plan_ref, bf16[160,1792]{1,0:T(8,128)(2,1)} %copy-done.1, bf16[160,1792]{1,0:T(8,128)(2,1)} %copy-done.2, bf16[160,1792]{1,0:T(8,128)(2,1)} %copy-done.14, bf16[160,1792]{1,0:T(8,128)(2,1)} %copy-done.13, bf16[14336,896]{1,0:T(8,128)(2,1)} %bitcast.15), custom_call_target="tpu_custom_call" | custom-call | tf_op jit(solution)/shard_map/fold_0/pallas_call | solution.py:172
  13.7 2.6 %collective-permute-start.4 = (bf16[320,512]{1,0:T(8,128)(2,1)S(1)}, bf16[320,512]{1,0:T(8,128)(2,1)S(1)}, u32[]{:S(2)}, u32[]{:S(2)}) collective-permute-start(bf16[320,512]{1,0:T(8,128)(2,1)S(1)} %copy-done.26), channel_id=1, source_target_pairs={{0,4},{4,12},{12,8},{8,0},{1,5},{5,13},{13,9},{9,1},{2,6},{6,14},{... | collective-permute-start | bytes 983048 | tf_op jit(solution)/shard_map/act_first/ppermute | solution.py:221
  16.3 1.4 collective-permute-start.13
  17.7 1.5 collective-permute-start
  19.2 2.0 %collective-permute-done.lengths_ref.refs_1_ = s32[1,3]{1,0:T(1,128)S(1)} collective-permute-done((s32[1,3]{1,0:T(1,128)S(1)}, s32[1,3]{1,0:T(1,128)S(1)}, u32[]{:S(2)}, u32[]{:S(2)}) %collective-permute-start) | collective-permute-done | bytes 44 | tf_op jit(solution)/shard_map/lengths_dp/ppermute | solution.py:226
  21.4 5.4 %collective-permute-done.4.refs_2_ = bf16[320,512]{1,0:T(8,128)(2,1)S(1)} collective-permute-done((bf16[320,512]{1,0:T(8,128)(2,1)S(1)}, bf16[320,512]{1,0:T(8,128)(2,1)S(1)}, u32[]{:S(2)}, u32[]{:S(2)}) %collective-permute-start.4) | collective-permute-done | bytes 327712 | tf_op jit(solution)/shard_map/act_first/ppermute | solution.py:221
  26.7 1.2 collective-permute-start.6
  27.9 3.4 %collective-permute-start.20 = (bf16[160,1792]{1,0:T(8,128)(2,1)S(1)}, bf16[160,1792]{1,0:T(8,128)(2,1)S(1)}, u32[]{:S(2)}, u32[]{:S(2)}) collective-permute-start(bf16[160,1792]{1,0:T(8,128)(2,1)S(1)} %collective-permute-done.18.refs_1_), channel_id=1, source_target_pairs={{0,4},{4,12},{12,8},{8,0},{1,5},{5,13},{13,9},{9,1},{2,6},{6,14},{... | collective-permute-start | bytes 1720328 | tf_op jit(solution)/shard_map/grad_second_1/ppermute | solution.py:221
  31.3 7.7 %collective-permute-done.13.refs_1_ = bf16[160,1792]{1,0:T(8,128)(2,1)S(1)} collective-permute-done((bf16[160,1792]{1,0:T(8,128)(2,1)}, bf16[160,1792]{1,0:T(8,128)(2,1)S(1)}, u32[]{:S(2)}, u32[]{:S(2)}) %collective-permute-start.13) | collective-permute-done | bytes 573472 | tf_op jit(solution)/shard_map/grad_first_0/ppermute | solution.py:221
  39.0 7.0 %collective-permute-done.6.refs_4_ = bf16[320,512]{1,0:T(8,128)(2,1)S(1)} collective-permute-done((bf16[320,512]{1,0:T(8,128)(2,1)S(1)}, bf16[320,512]{1,0:T(8,128)(2,1)S(1)}, u32[]{:S(2)}, u32[]{:S(2)}) %collective-permute-start.6) | collective-permute-done | bytes 327712 | tf_op jit(solution)/shard_map/act_second/ppermute | solution.py:221
  46.1 1.2 collective-permute-start.8
  47.2 0.8 copy-done.20
  48.0 5.7 %fold_1.3.refs_0_ = f32[160,896]{1,0:T(8,128)} custom-call(s32[14]{0:T(128)} %stack.59.offsets_ref.plan_ref, f32[160,896]{1,0:T(8,128)} %get-tuple-element.18.refs_0_, bf16[160,1792]{1,0:T(8,128)(2,1)} %copy-done.12, bf16[160,1792]{1,0:T(8,128)(2,1)} %copy-done.20, bf16[14336,896]{1,0:T(8,128)(2,1)} %bitcast.16), custom_call_target="tpu_custom_call" | custom-call | tf_op jit(solution)/shard_map/fold_1/pallas_call | solution.py:172
  53.8 4.6 %collective-permute-done.20.refs_1_ = bf16[160,1792]{1,0:T(8,128)(2,1)S(1)} collective-permute-done((bf16[160,1792]{1,0:T(8,128)(2,1)S(1)}, bf16[160,1792]{1,0:T(8,128)(2,1)S(1)}, u32[]{:S(2)}, u32[]{:S(2)}) %collective-permute-start.20) | collective-permute-done | bytes 573472 | tf_op jit(solution)/shard_map/grad_second_1/ppermute | solution.py:221
  58.4 1.2 collective-permute-start.15
  59.6 0.2 collective-permute-start.21
  59.8 5.6 %collective-permute-done.8.refs_6_ = bf16[320,512]{1,0:T(8,128)(2,1)S(1)} collective-permute-done((bf16[320,512]{1,0:T(8,128)(2,1)S(1)}, bf16[320,512]{1,0:T(8,128)(2,1)S(1)}, u32[]{:S(2)}, u32[]{:S(2)}) %collective-permute-start.8) | collective-permute-done | bytes 327712 | tf_op jit(solution)/shard_map/act_third/ppermute | solution.py:221
  65.4 1.2 collective-permute-start.22
  66.5 1.6 collective-permute-done.9.refs_7_
  68.2 0.7 copy-done.33
  68.9 5.3 %project.1.mine_ref = bf16[320,512]{1,0:T(8,128)(2,1)} custom-call(s32[14]{0:T(128)} %stack.59.offsets_ref.plan_ref, bf16[320,512]{1,0:T(8,128)(2,1)} %refs_0_.3, bf16[320,512]{1,0:T(8,128)(2,1)} %copy-done.29, bf16[320,512]{1,0:T(8,128)(2,1)} %copy-done.27, bf16[320,512]{1,0:T(8,128)(2,1)} %copy-done.30, bf16[320,512]{1,0:T(8,128)(2,1)} %copy-done.28, ...), custom_call_target="tpu_custom_call" | custom-call | tf_op jit(solution)/shard_map/project/pallas_call | solution.py:201
  74.2 1.5 collective-permute-start.11
  75.7 0.8 copy-done.18
  76.5 5.7 %fold_1.2.refs_0_ = f32[160,896]{1,0:T(8,128)} custom-call(s32[14]{0:T(128)} %stack.59.offsets_ref.plan_ref, f32[160,896]{1,0:T(8,128)} %get-tuple-element.17.refs_0_, bf16[160,1792]{1,0:T(8,128)(2,1)} %copy-done.15, bf16[160,1792]{1,0:T(8,128)(2,1)} %copy-done.18, bf16[14336,896]{1,0:T(8,128)(2,1)} %bitcast.17), custom_call_target="tpu_custom_call" | custom-call | tf_op jit(solution)/shard_map/fold_1/pallas_call | solution.py:172
  82.3 0.9 copy-done.19
  83.2 5.7 %fold_2.3.refs_0_ = f32[160,896]{1,0:T(8,128)} custom-call(s32[14]{0:T(128)} %stack.59.offsets_ref.plan_ref, f32[160,896]{1,0:T(8,128)} %fold_1.3.refs_0_, bf16[160,1792]{1,0:T(8,128)(2,1)} %copy-done.16, bf16[160,1792]{1,0:T(8,128)(2,1)} %copy-done.19, bf16[14336,896]{1,0:T(8,128)(2,1)} %bitcast.18), custom_call_target="tpu_custom_call" | custom-call | tf_op jit(solution)/shard_map/fold_2/pallas_call | solution.py:172
  88.9 0.5 collective-permute-done.22.refs_1_
  89.4 3.3 %collective-permute-start.17 = (bf16[160,1792]{1,0:T(8,128)(2,1)S(1)}, bf16[160,1792]{1,0:T(8,128)(2,1)S(1)}, u32[]{:S(2)}, u32[]{:S(2)}) collective-permute-start(bf16[160,1792]{1,0:T(8,128)(2,1)S(1)} %collective-permute-done.15.refs_1_), channel_id=1, source_target_pairs={{0,4},{4,12},{12,8},{8,0},{1,5},{5,13},{13,9},{9,1},{2,6},{6,14},{... | collective-permute-start | bytes 1720328 | tf_op jit(solution)/shard_map/grad_third_0/ppermute | solution.py:221
  92.7 0.9 copy-done.21
  93.6 5.7 %fold_2.2.refs_0_ = f32[160,896]{1,0:T(8,128)} custom-call(s32[14]{0:T(128)} %stack.59.offsets_ref.plan_ref, f32[160,896]{1,0:T(8,128)} %fold_1.2.refs_0_, bf16[160,1792]{1,0:T(8,128)(2,1)} %copy-done.17, bf16[160,1792]{1,0:T(8,128)(2,1)} %copy-done.21, bf16[14336,896]{1,0:T(8,128)(2,1)} %bitcast.19), custom_call_target="tpu_custom_call" | custom-call | tf_op jit(solution)/shard_map/fold_2/pallas_call | solution.py:172
  99.3 0.8 copy-done.24
  100.1 5.6 %fold_3.2.refs_6_ = bf16[160,896]{1,0:T(8,128)(2,1)} custom-call(s32[14]{0:T(128)} %stack.59.offsets_ref.plan_ref, f32[160,896]{1,0:T(8,128)} %fold_2.3.refs_0_, bf16[160,1792]{1,0:T(8,128)(2,1)} %copy-done.22, bf16[160,1792]{1,0:T(8,128)(2,1)} %copy-done.24, bf16[14336,896]{1,0:T(8,128)(2,1)} %bitcast.20), custom_call_target="tpu_custom_call" | custom-call | tf_op jit(solution)/shard_map/fold_3/pallas_call | solution.py:172
  105.7 0.5 collective-permute-start.24
  106.2 1.3 collective-permute-start.27
  107.6 0.3 collective-permute-done.24.refs_2_
  107.9 0.8 copy-done.25
  108.7 5.6 %fold_3.3.refs_4_ = bf16[160,896]{1,0:T(8,128)(2,1)} custom-call(s32[14]{0:T(128)} %stack.59.offsets_ref.plan_ref, f32[160,896]{1,0:T(8,128)} %fold_2.2.refs_0_, bf16[160,1792]{1,0:T(8,128)(2,1)} %copy-done.23, bf16[160,1792]{1,0:T(8,128)(2,1)} %copy-done.25, bf16[14336,896]{1,0:T(8,128)(2,1)} %bitcast.21), custom_call_target="tpu_custom_call" | custom-call | tf_op jit(solution)/shard_map/fold_3/pallas_call | solution.py:172
  114.3 1.2 collective-permute-done.27.refs_6_
  115.5 2.2 %collective-permute-start.28 = (bf16[160,896]{1,0:T(8,128)(2,1)S(1)}, bf16[160,896]{1,0:T(8,128)(2,1)S(1)}, u32[]{:S(2)}, u32[]{:S(2)}) collective-permute-start(bf16[160,896]{1,0:T(8,128)(2,1)S(1)} %collective-permute-done.27.refs_6_), channel_id=1, source_target_pairs={{4,0},{12,4},{8,12},{0,8},{5,1},{13,5},{9,13},{1,9},{6,2},{14,6},{... | collective-permute-start | bytes 860168 | tf_op jit(solution)/shard_map/rot_second_1/ppermute | solution.py:221
  117.7 0.4 collective-permute-start.25
  118.1 6.9 %collective-permute-done.28.refs_7_ = bf16[160,896]{1,0:T(8,128)(2,1)S(1)} collective-permute-done((bf16[160,896]{1,0:T(8,128)(2,1)S(1)}, bf16[160,896]{1,0:T(8,128)(2,1)S(1)}, u32[]{:S(2)}, u32[]{:S(2)}) %collective-permute-start.28) | collective-permute-done | bytes 286752 | tf_op jit(solution)/shard_map/rot_second_1/ppermute | solution.py:221
  125.1 1.6 collective-permute-start.31
  126.6 3.4 %collective-permute-start.29 = (bf16[160,896]{1,0:T(8,128)(2,1)S(1)}, bf16[160,896]{1,0:T(8,128)(2,1)S(1)}, u32[]{:S(2)}, u32[]{:S(2)}) collective-permute-start(bf16[160,896]{1,0:T(8,128)(2,1)S(1)} %collective-permute-done.28.refs_7_), channel_id=1, source_target_pairs={{4,0},{12,4},{8,12},{0,8},{5,1},{13,5},{9,13},{1,9},{6,2},{14,6},{... | collective-permute-start | bytes 860168 | tf_op jit(solution)/shard_map/rot_third_1/ppermute | solution.py:221
  130.0 4.4 %collective-permute-done.25.refs_4_ = bf16[160,896]{1,0:T(8,128)(2,1)S(1)} collective-permute-done((bf16[160,896]{1,0:T(8,128)(2,1)}, bf16[160,896]{1,0:T(8,128)(2,1)S(1)}, u32[]{:S(2)}, u32[]{:S(2)}) %collective-permute-start.25) | collective-permute-done | bytes 286752 | tf_op jit(solution)/shard_map/rot_first_0/ppermute | solution.py:221
  134.4 1.1 collective-permute-start.30
  135.6 3.5 %collective-permute-done.29.refs_7_ = bf16[160,896]{1,0:T(8,128)(2,1)S(1)} collective-permute-done((bf16[160,896]{1,0:T(8,128)(2,1)S(1)}, bf16[160,896]{1,0:T(8,128)(2,1)S(1)}, u32[]{:S(2)}, u32[]{:S(2)}) %collective-permute-start.29) | collective-permute-done | bytes 286752 | tf_op jit(solution)/shard_map/rot_third_1/ppermute | solution.py:221
  139.1 4.1 %collective-permute-done.30.refs_8_.refs_10_ = bf16[160,896]{1,0:T(8,128)(2,1)S(1)} collective-permute-done((bf16[160,896]{1,0:T(8,128)(2,1)S(1)}, bf16[160,896]{1,0:T(8,128)(2,1)S(1)}, u32[]{:S(2)}, u32[]{:S(2)}) %collective-permute-start.30) | collective-permute-done | bytes 286752 | tf_op jit(solution)/shard_map/rot_first_dp/ppermute | solution.py:226
  143.2 2.5 %collective-permute-done.26.refs_5_ = bf16[160,896]{1,0:T(8,128)(2,1)S(1)} collective-permute-done((bf16[160,896]{1,0:T(8,128)(2,1)S(1)}, bf16[160,896]{1,0:T(8,128)(2,1)S(1)}, u32[]{:S(2)}, u32[]{:S(2)}) %collective-permute-start.26) | collective-permute-done | bytes 286752 | tf_op jit(solution)/shard_map/rot_second_0/ppermute | solution.py:221
  145.7 2.2 %collective-permute-start.33 = (bf16[160,896]{1,0:T(8,128)(2,1)S(1)}, bf16[160,896]{1,0:T(8,128)(2,1)S(1)}, u32[]{:S(2)}, u32[]{:S(2)}) collective-permute-start(bf16[160,896]{1,0:T(8,128)(2,1)S(1)} %broadcast_select_fusion), channel_id=1, source_target_pairs={{0,1},{1,0},{2,3},{3,2},{4,5},{5,4},{6,7},{7,6},{8,9},{9,8},{10,11... | collective-permute-start | bytes 860168 | tf_op jit(solution)/shard_map/rot_second_dp_0/ppermute | solution.py:226
  147.9 0.7 copy-done.36
  148.7 2.8 %masked_windows.2.refs_2_ = bf16[3,1024,256]{2,1,0:T(8,128)(2,1)} custom-call(s32[14]{0:T(128)} %stack.59.offsets_ref.plan_ref, s32[1,3]{1,0:T(1,128)} %refs_0_.5, bf16[320,512]{1,0:T(8,128)(2,1)} %project.1.mine_ref, bf16[320,512]{1,0:T(8,128)(2,1)} %copy-done.36), custom_call_target="tpu_custom_call" | custom-call | tf_op jit(solution)/shard_map/masked_windows/pallas_call | solution.py:42
  151.5 2.8 %masked_windows.3.refs_3_ = bf16[3,1024,256]{2,1,0:T(8,128)(2,1)} custom-call(s32[14]{0:T(128)} %stack.59.offsets_ref.plan_ref, s32[1,3]{1,0:T(1,128)} %copy-done.40, bf16[320,512]{1,0:T(8,128)(2,1)} %copy-done.34, bf16[320,512]{1,0:T(8,128)(2,1)} %copy-done.35), custom_call_target="tpu_custom_call" | custom-call | tf_op jit(solution)/shard_map/masked_windows/pallas_call | solution.py:42
  154.3 0.4 collective-permute-done.32.refs_5_
  154.7 1.3 collective-permute-start.34
  156.1 8.3 %squared_sums.2.refs_12_ = f32[1024,1792]{1,0:T(8,128)} custom-call(s32[14]{0:T(128)} %stack.59.offsets_ref.plan_ref, s32[1,3]{1,0:T(1,128)} %refs_0_.5, s32[1,3]{1,0:T(1,128)} %copy-done.40, bf16[3,1024,256]{2,1,0:T(8,128)(2,1)} %masked_windows.2.refs_2_, bf16[3,1024,256]{2,1,0:T(8,128)(2,1)} %masked_windows.3.refs_3_, bf16[160,896]{1,0:T(8,128)(2,1)} %fold_3.3.refs_4_, ...), custom_call_target="tpu_custom_call" | custom-call | tf_op jit(solution)/shard_map/squared_sums/pallas_call | solution.py:126
  164.5 0.7 copy-done.5
  165.2 8.1 %squared_sums.3 = f32[1024,1792]{1,0:T(8,128)} custom-call(s32[14]{0:T(128)} %stack.59.offsets_ref.plan_ref, s32[1,3]{1,0:T(1,128)} %refs_0_.5, s32[1,3]{1,0:T(1,128)} %copy-done.40, bf16[3,1024,256]{2,1,0:T(8,128)(2,1)} %masked_windows.2.refs_2_, bf16[3,1024,256]{2,1,0:T(8,128)(2,1)} %masked_windows.3.refs_3_, ...), custom_call_target="tpu_custom_call", output_to_operand_aliasing={{}: (13, {})} | custom-call | tf_op jit(solution)/shard_map/squared_sums/pallas_call | solution.py:126
  (106 shorter events, 0.5 us)
Async XLA Ops:
  1.3 4.3 %copy-start.1 = (bf16[160,1792]{1,0:T(8,128)(2,1)}, bf16[160,1792]{1,0:T(8,128)(2,1)S(1)}, u32[]{:S(2)}) copy-start(bf16[160,1792]{1,0:T(8,128)(2,1)S(1)} %get-tuple-element.30.refs_0_) | copy-start | bytes 1720324
  1.3 4.3 %copy-start.2 = (bf16[160,1792]{1,0:T(8,128)(2,1)}, bf16[160,1792]{1,0:T(8,128)(2,1)S(1)}, u32[]{:S(2)}) copy-start(bf16[160,1792]{1,0:T(8,128)(2,1)S(1)} %get-tuple-element.29.refs_1_) | copy-start | bytes 1720324
  1.3 4.3 %collective-permute-start.3 = (bf16[160,1792]{1,0:T(8,128)(2,1)S(1)}, bf16[160,1792]{1,0:T(8,128)(2,1)S(1)}, u32[]{:S(2)}, u32[]{:S(2)}) collective-permute-start(bf16[160,1792]{1,0:T(8,128)(2,1)S(1)} %get-tuple-element.29.refs_1_), channel_id=1, source_target_pairs={{0,2},{2,0},{1,3},{3,1},{4,6},{6,4},{5,7},{7,5},{8,10},{10,8},{9,1... | collective-permute-start | bytes 1720328 | tf_op jit(solution)/shard_map/grad_0_cols_1/ppermute | solution.py:226
  1.9 3.8 %collective-permute-start.2 = (bf16[160,1792]{1,0:T(8,128)(2,1)S(1)}, bf16[160,1792]{1,0:T(8,128)(2,1)S(1)}, u32[]{:S(2)}, u32[]{:S(2)}) collective-permute-start(bf16[160,1792]{1,0:T(8,128)(2,1)S(1)} %get-tuple-element.30.refs_0_), channel_id=1, source_target_pairs={{0,2},{2,0},{1,3},{3,1},{4,6},{6,4},{5,7},{7,5},{8,10},{10,8},{9,1... | collective-permute-start | bytes 1720328 | tf_op jit(solution)/shard_map/grad_0_cols_0/ppermute | solution.py:226
  1.9 19.4 %collective-permute-start.18 = (bf16[160,1792]{1,0:T(8,128)(2,1)S(1)}, bf16[160,1792]{1,0:T(8,128)(2,1)S(1)}, u32[]{:S(2)}, u32[]{:S(2)}) collective-permute-start(bf16[160,1792]{1,0:T(8,128)(2,1)S(1)} %get-tuple-element.29.refs_1_), channel_id=1, source_target_pairs={{0,4},{4,12},{12,8},{8,0},{1,5},{5,13},{13,9},{9,1},{2,6},{6,14},{... | collective-permute-start | bytes 1720328 | tf_op jit(solution)/shard_map/grad_first_1/ppermute | solution.py:221
  6.6 7.1 %copy-start.26 = (bf16[320,512]{1,0:T(8,128)(2,1)S(1)}, bf16[320,512]{1,0:T(8,128)(2,1)}, u32[]{:S(2)}) copy-start(bf16[320,512]{1,0:T(8,128)(2,1)} %refs_0_.3) | copy-start | bytes 983044
  6.6 11.1 %copy-start.39 = (s32[1,3]{1,0:T(1,128)S(1)}, s32[1,3]{1,0:T(1,128)}, u32[]{:S(2)}) copy-start(s32[1,3]{1,0:T(1,128)} %refs_0_.5) | copy-start | bytes 40
  13.7 13.0 %collective-permute-start.4 = (bf16[320,512]{1,0:T(8,128)(2,1)S(1)}, bf16[320,512]{1,0:T(8,128)(2,1)S(1)}, u32[]{:S(2)}, u32[]{:S(2)}) collective-permute-start(bf16[320,512]{1,0:T(8,128)(2,1)S(1)} %copy-done.26), channel_id=1, source_target_pairs={{0,4},{4,12},{12,8},{8,0},{1,5},{5,13},{13,9},{9,1},{2,6},{6,14},{... | collective-permute-start | bytes 983048 | tf_op jit(solution)/shard_map/act_first/ppermute | solution.py:221
  16.3 22.7 %collective-permute-start.13 = (bf16[160,1792]{1,0:T(8,128)(2,1)}, bf16[160,1792]{1,0:T(8,128)(2,1)S(1)}, u32[]{:S(2)}, u32[]{:S(2)}) collective-permute-start(bf16[160,1792]{1,0:T(8,128)(2,1)} %copy-done.1), channel_id=1, source_target_pairs={{0,4},{4,12},{12,8},{8,0},{1,5},{5,13},{13,9},{9,1},{2,6},{6,14},{... | collective-permute-start | bytes 1720328 | tf_op jit(solution)/shard_map/grad_first_0/ppermute | solution.py:221
  17.7 3.5 %collective-permute-start = (s32[1,3]{1,0:T(1,128)S(1)}, s32[1,3]{1,0:T(1,128)S(1)}, u32[]{:S(2)}, u32[]{:S(2)}) collective-permute-start(s32[1,3]{1,0:T(1,128)S(1)} %copy-done.39), channel_id=1, source_target_pairs={{0,1},{1,0},{2,3},{3,2},{4,5},{5,4},{6,7},{7,6},{8,9},{9,8},{10,11... | collective-permute-start | bytes 44 | tf_op jit(solution)/shard_map/lengths_dp/ppermute | solution.py:226
  21.3 32.5 %copy-start.40 = (s32[1,3]{1,0:T(1,128)}, s32[1,3]{1,0:T(1,128)S(1)}, u32[]{:S(2)}) copy-start(s32[1,3]{1,0:T(1,128)S(1)} %collective-permute-done.lengths_ref.refs_1_) | copy-start | bytes 40
  21.3 25.9 %copy-start.12 = (bf16[160,1792]{1,0:T(8,128)(2,1)}, bf16[160,1792]{1,0:T(8,128)(2,1)S(1)}, u32[]{:S(2)}) copy-start(bf16[160,1792]{1,0:T(8,128)(2,1)S(1)} %collective-permute-done.18.refs_1_) | copy-start | bytes 1720324
  21.3 25.9 %collective-permute-start.19 = (bf16[160,1792]{1,0:T(8,128)(2,1)S(1)}, bf16[160,1792]{1,0:T(8,128)(2,1)S(1)}, u32[]{:S(2)}, u32[]{:S(2)}) collective-permute-start(bf16[160,1792]{1,0:T(8,128)(2,1)S(1)} %collective-permute-done.18.refs_1_), channel_id=1, source_target_pairs={{0,2},{2,0},{1,3},{3,1},{4,6},{6,4},{5,7},{7,5},{8,10},{10,8},{9,1... | collective-permute-start | bytes 1720328 | tf_op jit(solution)/shard_map/grad_1_cols_1/ppermute | solution.py:226
  26.7 27.0 %copy-start.27 = (bf16[320,512]{1,0:T(8,128)(2,1)}, bf16[320,512]{1,0:T(8,128)(2,1)S(1)}, u32[]{:S(2)}) copy-start(bf16[320,512]{1,0:T(8,128)(2,1)S(1)} %collective-permute-done.4.refs_2_) | copy-start | bytes 983044
  26.7 19.3 %collective-permute-start.6 = (bf16[320,512]{1,0:T(8,128)(2,1)S(1)}, bf16[320,512]{1,0:T(8,128)(2,1)S(1)}, u32[]{:S(2)}, u32[]{:S(2)}) collective-permute-start(bf16[320,512]{1,0:T(8,128)(2,1)S(1)} %collective-permute-done.4.refs_2_), channel_id=1, source_target_pairs={{0,4},{4,12},{12,8},{8,0},{1,5},{5,13},{13,9},{9,1},{2,6},{6,14},{... | collective-permute-start | bytes 983048 | tf_op jit(solution)/shard_map/act_second/ppermute | solution.py:221
  27.9 30.4 %collective-permute-start.20 = (bf16[160,1792]{1,0:T(8,128)(2,1)S(1)}, bf16[160,1792]{1,0:T(8,128)(2,1)S(1)}, u32[]{:S(2)}, u32[]{:S(2)}) collective-permute-start(bf16[160,1792]{1,0:T(8,128)(2,1)S(1)} %collective-permute-done.18.refs_1_), channel_id=1, source_target_pairs={{0,4},{4,12},{12,8},{8,0},{1,5},{5,13},{13,9},{9,1},{2,6},{6,14},{... | collective-permute-start | bytes 1720328 | tf_op jit(solution)/shard_map/grad_second_1/ppermute | solution.py:221
  31.3 27.1 %collective-permute-start.1 = (bf16[320,512]{1,0:T(8,128)(2,1)S(1)}, bf16[320,512]{1,0:T(8,128)(2,1)S(1)}, u32[]{:S(2)}, u32[]{:S(2)}) collective-permute-start(bf16[320,512]{1,0:T(8,128)(2,1)S(1)} %copy-done.26), channel_id=1, source_target_pairs={{0,2},{2,0},{1,3},{3,1},{4,6},{6,4},{5,7},{7,5},{8,10},{10,8},{9,1... | collective-permute-start | bytes 983048 | tf_op jit(solution)/shard_map/act_cols/ppermute | solution.py:226
  39.0 19.3 %copy-start.15 = (bf16[160,1792]{1,0:T(8,128)(2,1)}, bf16[160,1792]{1,0:T(8,128)(2,1)S(1)}, u32[]{:S(2)}) copy-start(bf16[160,1792]{1,0:T(8,128)(2,1)S(1)} %collective-permute-done.13.refs_1_) | copy-start | bytes 1720324
  39.0 20.5 %collective-permute-start.5 = (bf16[320,512]{1,0:T(8,128)(2,1)S(1)}, bf16[320,512]{1,0:T(8,128)(2,1)S(1)}, u32[]{:S(2)}, u32[]{:S(2)}) collective-permute-start(bf16[320,512]{1,0:T(8,128)(2,1)S(1)} %collective-permute-done.4.refs_2_), channel_id=1, source_target_pairs={{0,2},{2,0},{1,3},{3,1},{4,6},{6,4},{5,7},{7,5},{8,10},{10,8},{9,1... | collective-permute-start | bytes 983048 | tf_op jit(solution)/shard_map/act_cols/ppermute | solution.py:226
  46.0 7.7 %copy-start.28 = (bf16[320,512]{1,0:T(8,128)(2,1)}, bf16[320,512]{1,0:T(8,128)(2,1)S(1)}, u32[]{:S(2)}) copy-start(bf16[320,512]{1,0:T(8,128)(2,1)S(1)} %collective-permute-done.6.refs_4_) | copy-start | bytes 983044
  46.1 19.3 %collective-permute-start.8 = (bf16[320,512]{1,0:T(8,128)(2,1)S(1)}, bf16[320,512]{1,0:T(8,128)(2,1)S(1)}, u32[]{:S(2)}, u32[]{:S(2)}) collective-permute-start(bf16[320,512]{1,0:T(8,128)(2,1)S(1)} %collective-permute-done.6.refs_4_), channel_id=1, source_target_pairs={{0,4},{4,12},{12,8},{8,0},{1,5},{5,13},{13,9},{9,1},{2,6},{6,14},{... | collective-permute-start | bytes 983048 | tf_op jit(solution)/shard_map/act_third/ppermute | solution.py:221
  47.2 19.3 %collective-permute-start.7 = (bf16[320,512]{1,0:T(8,128)(2,1)S(1)}, bf16[320,512]{1,0:T(8,128)(2,1)S(1)}, u32[]{:S(2)}, u32[]{:S(2)}) collective-permute-start(bf16[320,512]{1,0:T(8,128)(2,1)S(1)} %collective-permute-done.6.refs_4_), channel_id=1, source_target_pairs={{0,2},{2,0},{1,3},{3,1},{4,6},{6,4},{5,7},{7,5},{8,10},{10,8},{9,1... | collective-permute-start | bytes 983048 | tf_op jit(solution)/shard_map/act_cols/ppermute | solution.py:226
  58.3 23.8 %copy-start.16 = (bf16[160,1792]{1,0:T(8,128)(2,1)}, bf16[160,1792]{1,0:T(8,128)(2,1)S(1)}, u32[]{:S(2)}) copy-start(bf16[160,1792]{1,0:T(8,128)(2,1)S(1)} %collective-permute-done.20.refs_1_) | copy-start | bytes 1720324
  58.3 17.3 %collective-permute-start.14 = (bf16[160,1792]{1,0:T(8,128)(2,1)S(1)}, bf16[160,1792]{1,0:T(8,128)(2,1)S(1)}, u32[]{:S(2)}, u32[]{:S(2)}) collective-permute-start(bf16[160,1792]{1,0:T(8,128)(2,1)S(1)} %collective-permute-done.13.refs_1_), channel_id=1, source_target_pairs={{0,2},{2,0},{1,3},{3,1},{4,6},{6,4},{5,7},{7,5},{8,10},{10,8},{9,1... | collective-permute-start | bytes 1720328 | tf_op jit(solution)/shard_map/grad_1_cols_0/ppermute | solution.py:226
  58.4 9.8 %copy-start.29 = (bf16[320,512]{1,0:T(8,128)(2,1)}, bf16[320,512]{1,0:T(8,128)(2,1)S(1)}, u32[]{:S(2)}) copy-start(bf16[320,512]{1,0:T(8,128)(2,1)S(1)} %collective-permute-done.1.refs_1_) | copy-start | bytes 983044
  58.4 23.8 %collective-permute-start.15 = (bf16[160,1792]{1,0:T(8,128)(2,1)S(1)}, bf16[160,1792]{1,0:T(8,128)(2,1)S(1)}, u32[]{:S(2)}, u32[]{:S(2)}) collective-permute-start(bf16[160,1792]{1,0:T(8,128)(2,1)S(1)} %collective-permute-done.13.refs_1_), channel_id=1, source_target_pairs={{0,4},{4,12},{12,8},{8,0},{1,5},{5,13},{13,9},{9,1},{2,6},{6,14},{... | collective-permute-start | bytes 1720328 | tf_op jit(solution)/shard_map/grad_second_0/ppermute | solution.py:221
  59.6 8.6 %copy-start.30 = (bf16[320,512]{1,0:T(8,128)(2,1)}, bf16[320,512]{1,0:T(8,128)(2,1)S(1)}, u32[]{:S(2)}) copy-start(bf16[320,512]{1,0:T(8,128)(2,1)S(1)} %collective-permute-done.5.refs_3_) | copy-start | bytes 983044
  59.6 22.7 %collective-permute-start.21 = (bf16[160,1792]{1,0:T(8,128)(2,1)S(1)}, bf16[160,1792]{1,0:T(8,128)(2,1)S(1)}, u32[]{:S(2)}, u32[]{:S(2)}) collective-permute-start(bf16[160,1792]{1,0:T(8,128)(2,1)S(1)} %collective-permute-done.20.refs_1_), channel_id=1, source_target_pairs={{0,2},{2,0},{1,3},{3,1},{4,6},{6,4},{5,7},{7,5},{8,10},{10,8},{9,1... | collective-permute-start | bytes 1720328 | tf_op jit(solution)/shard_map/grad_2_cols_1/ppermute | solution.py:226
  65.4 2.8 %copy-start.31 = (bf16[320,512]{1,0:T(8,128)(2,1)}, bf16[320,512]{1,0:T(8,128)(2,1)S(1)}, u32[]{:S(2)}) copy-start(bf16[320,512]{1,0:T(8,128)(2,1)S(1)} %collective-permute-done.8.refs_6_) | copy-start | bytes 983044
  65.4 24.0 %collective-permute-start.22 = (bf16[160,1792]{1,0:T(8,128)(2,1)S(1)}, bf16[160,1792]{1,0:T(8,128)(2,1)S(1)}, u32[]{:S(2)}, u32[]{:S(2)}) collective-permute-start(bf16[160,1792]{1,0:T(8,128)(2,1)S(1)} %collective-permute-done.20.refs_1_), channel_id=1, source_target_pairs={{0,4},{4,12},{12,8},{8,0},{1,5},{5,13},{13,9},{9,1},{2,6},{6,14},{... | collective-permute-start | bytes 1720328 | tf_op jit(solution)/shard_map/grad_third_1/ppermute | solution.py:221
  66.5 1.6 copy-start.32
  66.5 1.6 collective-permute-start.9
  74.2 18.5 %collective-permute-start.11 = (bf16[320,512]{1,0:T(8,128)(2,1)}, bf16[320,512]{1,0:T(8,128)(2,1)S(1)}, u32[]{:S(2)}, u32[]{:S(2)}) collective-permute-start(bf16[320,512]{1,0:T(8,128)(2,1)} %project.1.mine_ref), channel_id=1, source_target_pairs={{0,1},{1,0},{2,3},{3,2},{4,5},{5,4},{6,7},{7,6},{8,9},{9,8},{10,11... | collective-permute-start | bytes 983048 | tf_op jit(solution)/shard_map/act_dp/ppermute | solution.py:226
  82.2 7.2 %copy-start.17 = (bf16[160,1792]{1,0:T(8,128)(2,1)}, bf16[160,1792]{1,0:T(8,128)(2,1)S(1)}, u32[]{:S(2)}) copy-start(bf16[160,1792]{1,0:T(8,128)(2,1)S(1)} %collective-permute-done.15.refs_1_) | copy-start | bytes 1720324
  82.2 10.5 %collective-permute-start.16 = (bf16[160,1792]{1,0:T(8,128)(2,1)S(1)}, bf16[160,1792]{1,0:T(8,128)(2,1)S(1)}, u32[]{:S(2)}, u32[]{:S(2)}) collective-permute-start(bf16[160,1792]{1,0:T(8,128)(2,1)S(1)} %collective-permute-done.15.refs_1_), channel_id=1, source_target_pairs={{0,2},{2,0},{1,3},{3,1},{4,6},{6,4},{5,7},{7,5},{8,10},{10,8},{9,1... | collective-permute-start | bytes 1720328 | tf_op jit(solution)/shard_map/grad_2_cols_0/ppermute | solution.py:226
  89.4 9.9 %copy-start.22 = (bf16[160,1792]{1,0:T(8,128)(2,1)}, bf16[160,1792]{1,0:T(8,128)(2,1)S(1)}, u32[]{:S(2)}) copy-start(bf16[160,1792]{1,0:T(8,128)(2,1)S(1)} %collective-permute-done.22.refs_1_) | copy-start | bytes 1720324
  89.4 9.9 %collective-permute-start.23 = (bf16[160,1792]{1,0:T(8,128)(2,1)S(1)}, bf16[160,1792]{1,0:T(8,128)(2,1)S(1)}, u32[]{:S(2)}, u32[]{:S(2)}) collective-permute-start(bf16[160,1792]{1,0:T(8,128)(2,1)S(1)} %collective-permute-done.22.refs_1_), channel_id=1, source_target_pairs={{0,2},{2,0},{1,3},{3,1},{4,6},{6,4},{5,7},{7,5},{8,10},{10,8},{9,1... | collective-permute-start | bytes 1720328 | tf_op jit(solution)/shard_map/grad_3_cols_1/ppermute | solution.py:226
  89.4 16.3 %collective-permute-start.17 = (bf16[160,1792]{1,0:T(8,128)(2,1)S(1)}, bf16[160,1792]{1,0:T(8,128)(2,1)S(1)}, u32[]{:S(2)}, u32[]{:S(2)}) collective-permute-start(bf16[160,1792]{1,0:T(8,128)(2,1)S(1)} %collective-permute-done.15.refs_1_), channel_id=1, source_target_pairs={{0,4},{4,12},{12,8},{8,0},{1,5},{5,13},{13,9},{9,1},{2,6},{6,14},{... | collective-permute-start | bytes 1720328 | tf_op jit(solution)/shard_map/grad_third_0/ppermute | solution.py:221
  92.7 6.6 %copy-start.34 = (bf16[320,512]{1,0:T(8,128)(2,1)}, bf16[320,512]{1,0:T(8,128)(2,1)S(1)}, u32[]{:S(2)}) copy-start(bf16[320,512]{1,0:T(8,128)(2,1)S(1)} %collective-permute-done.11.mine_ref) | copy-start | bytes 983044
  92.7 13.0 %collective-permute-start.12 = (bf16[320,512]{1,0:T(8,128)(2,1)S(1)}, bf16[320,512]{1,0:T(8,128)(2,1)S(1)}, u32[]{:S(2)}, u32[]{:S(2)}) collective-permute-start(bf16[320,512]{1,0:T(8,128)(2,1)S(1)} %collective-permute-done.11.mine_ref), channel_id=1, source_target_pairs={{0,2},{2,0},{1,3},{3,1},{4,6},{6,4},{5,7},{7,5},{8,10},{10,8},{9,1... | collective-permute-start | bytes 983048 | tf_op jit(solution)/shard_map/rot_act_cols/ppermute | solution.py:226
  105.7 19.3 %copy-start = (bf16[160,896]{1,0:T(8,128)(2,1)S(1)}, bf16[160,896]{1,0:T(8,128)(2,1)}, u32[]{:S(2)}) copy-start(bf16[160,896]{1,0:T(8,128)(2,1)} %fold_3.2.refs_6_) | copy-start | bytes 860164
  105.7 29.9 %copy-start.3 = (bf16[320,512]{1,0:T(8,128)(2,1)S(1)}, bf16[320,512]{1,0:T(8,128)(2,1)}, u32[]{:S(2)}) copy-start(bf16[320,512]{1,0:T(8,128)(2,1)} %project.1.mine_ref) | copy-start | bytes 983044
  105.7 2.2 %copy-start.23 = (bf16[160,1792]{1,0:T(8,128)(2,1)}, bf16[160,1792]{1,0:T(8,128)(2,1)S(1)}, u32[]{:S(2)}) copy-start(bf16[160,1792]{1,0:T(8,128)(2,1)S(1)} %collective-permute-done.17.refs_1_) | copy-start | bytes 1720324
  105.7 8.6 %copy-start.35 = (bf16[320,512]{1,0:T(8,128)(2,1)}, bf16[320,512]{1,0:T(8,128)(2,1)S(1)}, u32[]{:S(2)}) copy-start(bf16[320,512]{1,0:T(8,128)(2,1)S(1)} %collective-permute-done.12.theirs_ref) | copy-start | bytes 983044
  105.7 2.1 %collective-permute-start.24 = (bf16[160,1792]{1,0:T(8,128)(2,1)S(1)}, bf16[160,1792]{1,0:T(8,128)(2,1)S(1)}, u32[]{:S(2)}, u32[]{:S(2)}) collective-permute-start(bf16[160,1792]{1,0:T(8,128)(2,1)S(1)} %collective-permute-done.17.refs_1_), channel_id=1, source_target_pairs={{0,2},{2,0},{1,3},{3,1},{4,6},{6,4},{5,7},{7,5},{8,10},{10,8},{9,1... | collective-permute-start | bytes 1720328 | tf_op jit(solution)/shard_map/grad_3_cols_0/ppermute | solution.py:226
  106.2 9.2 %collective-permute-start.27 = (bf16[160,896]{1,0:T(8,128)(2,1)}, bf16[160,896]{1,0:T(8,128)(2,1)S(1)}, u32[]{:S(2)}, u32[]{:S(2)}) collective-permute-start(bf16[160,896]{1,0:T(8,128)(2,1)} %fold_3.2.refs_6_), channel_id=1, source_target_pairs={{4,0},{12,4},{8,12},{0,8},{5,1},{13,5},{9,13},{1,9},{6,2},{14,6},{... | collective-permute-start | bytes 860168 | tf_op jit(solution)/shard_map/rot_first_1/ppermute | solution.py:221
  115.5 49.0 %copy-start.6 = (bf16[160,896]{1,0:T(8,128)(2,1)}, bf16[160,896]{1,0:T(8,128)(2,1)S(1)}, u32[]{:S(2)}) copy-start(bf16[160,896]{1,0:T(8,128)(2,1)S(1)} %collective-permute-done.27.refs_6_) | copy-start | bytes 860164
  115.5 9.6 %collective-permute-start.28 = (bf16[160,896]{1,0:T(8,128)(2,1)S(1)}, bf16[160,896]{1,0:T(8,128)(2,1)S(1)}, u32[]{:S(2)}, u32[]{:S(2)}) collective-permute-start(bf16[160,896]{1,0:T(8,128)(2,1)S(1)} %collective-permute-done.27.refs_6_), channel_id=1, source_target_pairs={{4,0},{12,4},{8,12},{0,8},{5,1},{13,5},{9,13},{1,9},{6,2},{14,6},{... | collective-permute-start | bytes 860168 | tf_op jit(solution)/shard_map/rot_second_1/ppermute | solution.py:221
  117.7 16.7 %collective-permute-start.25 = (bf16[160,896]{1,0:T(8,128)(2,1)}, bf16[160,896]{1,0:T(8,128)(2,1)S(1)}, u32[]{:S(2)}, u32[]{:S(2)}) collective-permute-start(bf16[160,896]{1,0:T(8,128)(2,1)} %fold_3.3.refs_4_), channel_id=1, source_target_pairs={{0,4},{4,12},{12,8},{8,0},{1,5},{5,13},{13,9},{9,1},{2,6},{6,14},{... | collective-permute-start | bytes 860168 | tf_op jit(solution)/shard_map/rot_first_0/ppermute | solution.py:221
  125.0 31.1 %copy-start.10 = (bf16[160,896]{1,0:T(8,128)(2,1)}, bf16[160,896]{1,0:T(8,128)(2,1)S(1)}, u32[]{:S(2)}) copy-start(bf16[160,896]{1,0:T(8,128)(2,1)S(1)} %collective-permute-done.28.refs_7_) | copy-start | bytes 860164
  125.1 10.5 %collective-permute-start.31 = (bf16[160,896]{1,0:T(8,128)(2,1)S(1)}, bf16[160,896]{1,0:T(8,128)(2,1)S(1)}, u32[]{:S(2)}, u32[]{:S(2)}) collective-permute-start(bf16[160,896]{1,0:T(8,128)(2,1)S(1)} %broadcast_select_fusion.1), channel_id=1, source_target_pairs={{0,1},{1,0},{2,3},{3,2},{4,5},{5,4},{6,7},{7,6},{8,9},{9,8},{10,11... | collective-permute-start | bytes 860168 | tf_op jit(solution)/shard_map/rot_second_dp_1/ppermute | solution.py:226
  126.6 12.5 %collective-permute-start.29 = (bf16[160,896]{1,0:T(8,128)(2,1)S(1)}, bf16[160,896]{1,0:T(8,128)(2,1)S(1)}, u32[]{:S(2)}, u32[]{:S(2)}) collective-permute-start(bf16[160,896]{1,0:T(8,128)(2,1)S(1)} %collective-permute-done.28.refs_7_), channel_id=1, source_target_pairs={{4,0},{12,4},{8,12},{0,8},{5,1},{13,5},{9,13},{1,9},{6,2},{14,6},{... | collective-permute-start | bytes 860168 | tf_op jit(solution)/shard_map/rot_third_1/ppermute | solution.py:221
  134.4 30.0 %copy-start.7 = (bf16[160,896]{1,0:T(8,128)(2,1)}, bf16[160,896]{1,0:T(8,128)(2,1)S(1)}, u32[]{:S(2)}) copy-start(bf16[160,896]{1,0:T(8,128)(2,1)S(1)} %collective-permute-done.25.refs_4_) | copy-start | bytes 860164
  134.4 8.7 %collective-permute-start.30 = (bf16[160,896]{1,0:T(8,128)(2,1)S(1)}, bf16[160,896]{1,0:T(8,128)(2,1)S(1)}, u32[]{:S(2)}, u32[]{:S(2)}) collective-permute-start(bf16[160,896]{1,0:T(8,128)(2,1)S(1)} %broadcast_select_fusion.3), channel_id=1, source_target_pairs={{0,1},{1,0},{2,3},{3,2},{4,5},{5,4},{6,7},{7,6},{8,9},{9,8},{10,11... | collective-permute-start | bytes 860168 | tf_op jit(solution)/shard_map/rot_first_dp/ppermute | solution.py:226
  135.5 10.1 %collective-permute-start.26 = (bf16[160,896]{1,0:T(8,128)(2,1)S(1)}, bf16[160,896]{1,0:T(8,128)(2,1)S(1)}, u32[]{:S(2)}, u32[]{:S(2)}) collective-permute-start(bf16[160,896]{1,0:T(8,128)(2,1)S(1)} %collective-permute-done.25.refs_4_), channel_id=1, source_target_pairs={{0,4},{4,12},{12,8},{8,0},{1,5},{5,13},{13,9},{9,1},{2,6},{6,14},{... | collective-permute-start | bytes 860168 | tf_op jit(solution)/shard_map/rot_second_0/ppermute | solution.py:221
  135.5 12.4 %collective-permute-start.10 = (bf16[320,512]{1,0:T(8,128)(2,1)S(1)}, bf16[320,512]{1,0:T(8,128)(2,1)S(1)}, u32[]{:S(2)}, u32[]{:S(2)}) collective-permute-start(bf16[320,512]{1,0:T(8,128)(2,1)S(1)} %copy-done.3), channel_id=1, source_target_pairs={{0,2},{2,0},{1,3},{3,1},{4,6},{6,4},{5,7},{7,5},{8,10},{10,8},{9,1... | collective-permute-start | bytes 983048 | tf_op jit(solution)/shard_map/rot_act_cols/ppermute | solution.py:226
  135.6 20.5 %copy-start.37 = (bf16[160,896]{1,0:T(8,128)(2,1)}, bf16[160,896]{1,0:T(8,128)(2,1)S(1)}, u32[]{:S(2)}) copy-start(bf16[160,896]{1,0:T(8,128)(2,1)S(1)} %collective-permute-done.31.refs_9_) | copy-start | bytes 860164
  139.1 25.4 %copy-start.8 = (bf16[160,896]{1,0:T(8,128)(2,1)}, bf16[160,896]{1,0:T(8,128)(2,1)S(1)}, u32[]{:S(2)}) copy-start(bf16[160,896]{1,0:T(8,128)(2,1)S(1)} %collective-permute-done.29.refs_7_) | copy-start | bytes 860164
  143.2 21.3 %copy-start.4 = (bf16[160,896]{1,0:T(8,128)(2,1)}, bf16[160,896]{1,0:T(8,128)(2,1)S(1)}, u32[]{:S(2)}) copy-start(bf16[160,896]{1,0:T(8,128)(2,1)S(1)} %collective-permute-done.30.refs_8_.refs_10_) | copy-start | bytes 860164
  145.6 10.4 %copy-start.11 = (bf16[160,896]{1,0:T(8,128)(2,1)}, bf16[160,896]{1,0:T(8,128)(2,1)S(1)}, u32[]{:S(2)}) copy-start(bf16[160,896]{1,0:T(8,128)(2,1)S(1)} %collective-permute-done.26.refs_5_) | copy-start | bytes 860164
  145.6 9.0 %collective-permute-start.32 = (bf16[160,896]{1,0:T(8,128)(2,1)S(1)}, bf16[160,896]{1,0:T(8,128)(2,1)S(1)}, u32[]{:S(2)}, u32[]{:S(2)}) collective-permute-start(bf16[160,896]{1,0:T(8,128)(2,1)S(1)} %collective-permute-done.26.refs_5_), channel_id=1, source_target_pairs={{0,4},{4,12},{12,8},{8,0},{1,5},{5,13},{13,9},{9,1},{2,6},{6,14},{... | collective-permute-start | bytes 860168 | tf_op jit(solution)/shard_map/rot_third_0/ppermute | solution.py:221
  145.7 9.0 %collective-permute-start.33 = (bf16[160,896]{1,0:T(8,128)(2,1)S(1)}, bf16[160,896]{1,0:T(8,128)(2,1)S(1)}, u32[]{:S(2)}, u32[]{:S(2)}) collective-permute-start(bf16[160,896]{1,0:T(8,128)(2,1)S(1)} %broadcast_select_fusion), channel_id=1, source_target_pairs={{0,1},{1,0},{2,3},{3,2},{4,5},{5,4},{6,7},{7,6},{8,9},{9,8},{10,11... | collective-permute-start | bytes 860168 | tf_op jit(solution)/shard_map/rot_second_dp_0/ppermute | solution.py:226
  154.7 9.8 %copy-start.9 = (bf16[160,896]{1,0:T(8,128)(2,1)}, bf16[160,896]{1,0:T(8,128)(2,1)S(1)}, u32[]{:S(2)}) copy-start(bf16[160,896]{1,0:T(8,128)(2,1)S(1)} %collective-permute-done.32.refs_5_) | copy-start | bytes 860164
  154.7 9.7 %collective-permute-start.34 = (bf16[160,896]{1,0:T(8,128)(2,1)S(1)}, bf16[160,896]{1,0:T(8,128)(2,1)S(1)}, u32[]{:S(2)}, u32[]{:S(2)}) collective-permute-start(bf16[160,896]{1,0:T(8,128)(2,1)S(1)} %broadcast_select_fusion.2), channel_id=1, source_target_pairs={{0,1},{1,0},{2,3},{3,2},{4,5},{5,4},{6,7},{7,6},{8,9},{9,8},{10,11... | collective-permute-start | bytes 860168 | tf_op jit(solution)/shard_map/rot_third_dp/ppermute | solution.py:226
  (12 other events, 10.4 us)

commit v4 on v3

--- a/solution.py
+++ b/solution.py
@@ -8,7 +8,7 @@
 from jax.sharding import PartitionSpec as P
 
 STEP = 64
-VMEM_BYTES = 56 * 1024 * 1024
+VMEM_BYTES = 40 * 1024 * 1024
 
 
 def span_of(lengths_ref, example):
@@ -263,20 +263,21 @@
     sums = list(fold_block(None, own, crossed(own, 0), basis_grad, features, plan, 0, jnp.float32, 2))
     firsts = [after(hop(x, f"grad_first_{i}"), sums[i], spans[1]) for i, x in enumerate(own)]
     act_first = hop(after(activations, *sums), "act_first")
-    seconds = [hop(after(x, act_first) if 0 else x, f"grad_second_{i}") for i, x in enumerate(firsts)]
+    seconds = [hop(x, f"grad_second_{i}") for i, x in enumerate(firsts)]
     act_second = hop(act_first, "act_second")
-    act_third = hop(act_second, "act_third")
-    thirds = []
-    for i in range(2):
-        sums[i] = piece(sums[i], firsts[i], 1, i)
-        thirds.append(hop(after(seconds[i], sums[i], *([act_second] if i else [])), f"grad_third_{i}"))
-    sums[1] = piece(sums[1], seconds[1], 2, 1)
+    thirds = [None, None]
+    sums[1] = piece(sums[1], firsts[1], 1, 1)
+    act_third = hop(after(act_second, sums[1]), "act_third")
+    sums[0] = piece(sums[0], firsts[0], 1, 0)
+    thirds[1] = hop(after(seconds[1], sums[1], act_second), "grad_third_1")
+    thirds[0] = hop(after(seconds[0], sums[0]), "grad_third_0")
     acts = (activations, act_first, act_second, act_third)
     rotated = project([x for s in acts for x in (s, swap(s, "col", "act_cols"))], q_act, plan)
     other = swap(rotated, "dp", "act_dp")
     acts = [(x, swap(x, "col", "rot_act_cols")) for x in (rotated, other)]
+    sums[1] = piece(sums[1], seconds[1], 2, 1)
     owns = [None, piece(sums[1], after(thirds[1], sums[1], rotated), 3, 1)]
-    sums[0] = piece(after(sums[0], owns[1]) if 0 else sums[0], seconds[0], 2, 0)
+    sums[0] = piece(sums[0], seconds[0], 2, 0)
     owns[0] = piece(sums[0], after(thirds[0], sums[0], owns[1], *acts[1]), 3, 0)
 
     acts = [masked_windows(plan, CORE, s, *x, window) for s, x in zip(spans, acts)]

time: 174 us -> 170 us (0.977)
  waiting for transfers between devices: 57.7 us -> 82.8 us
  Pallas kernels: 68.4 us -> 48.8 us
  local copies, waits for them, and re-layouts: 10.3 us -> 1.41 us
    ppermute x15, waiting for transfers between devices: 49.6 us -> 75.3 us  [hop(): return lax.ppermute(x, 'row', [hop[::-1] for hop in RING] if back else RING)]
    pallas_call x7, Pallas kernels: 41.1 us -> 30.7 us  [fold_block(): pl.pallas_call(functools.partial(fold_kernel, started, len(mine)), name=f...]
    unnamed x82 -> x6, local copies, waits for them, and re-layouts: 8.3 us -> 0.02 us
    pallas_call x2, Pallas kernels: 5.66 us -> 2.27 us  [masked_windows(): pl.pallas_call(functools.partial(mask_kernel, examples, window, place_at)...]
    pallas_call x1, Pallas kernels: 5.26 us -> 2.05 us  [project(): pl.pallas_call(project_kernel, name='project', out_shape=jax.ShapeDtypeSt...]
    pallas_call x2, Pallas kernels: 16.4 us -> 13.8 us  [squared_sums(): pl.pallas_call(functools.partial(square_kernel, chunks, examples, window,...]
  transfers between devices with their start and end apart: 35 -> 35, of which waited for: 16 -> 18; matrix products, arithmetic and copies ran while one was open for 0% -> 0% of each run, Pallas kernels for 35% -> 25%
where the time goes in v4:
time: 170 us
  waiting for transfers between devices  82.8 us (49%)
  Pallas kernels  48.8 us (29%)
  starting transfers between devices  36.1 us (21%)
    ppermute x15, waiting for transfers between devices, hop(): return lax.ppermute(x, 'row', [hop[::-1] for hop in RING] if back else RING)  75.3 us
    pallas_call x7, Pallas kernels, fold_block(): pl.pallas_call(functools.partial(fold_kernel, started, len(mine)), name=f...  30.7 us
    ppermute x15, starting transfers between devices, hop(): return lax.ppermute(x, 'row', [hop[::-1] for hop in RING] if back else RING)  25.4 us
    pallas_call x2, Pallas kernels, squared_sums(): pl.pallas_call(functools.partial(square_kernel, chunks, examples, window,...  13.8 us
    ppermute x20, starting transfers between devices, swap(): return lax.ppermute(x, axis, [(0, 1), (1, 0)])  10.7 us
    ppermute x20, waiting for transfers between devices, swap(): return lax.ppermute(x, axis, [(0, 1), (1, 0)])  7.5 us
  transfers between devices with their start and end apart: 35, of which 18 were waited for; matrix products, arithmetic and copies ran while one was open for 0% of the time, Pallas kernels for 25%

profile of v4, /device:TPU:0, one launch (start us, length us, event | category | flops | bytes accessed | tf_op | source)
XLA Modules:
  0.0 169.6 jit_solution(16717604477453619197)
XLA Ops:
  0.0 1.3 fusion
  1.3 0.5 collective-permute-start.3
  1.8 0.1 collective-permute-start.2
  1.9 3.0 %collective-permute-start.8 = (bf16[160,1792]{1,0:T(8,128)(2,1)S(1)}, bf16[160,1792]{1,0:T(8,128)(2,1)S(1)}, u32[]{:S(2)}, u32[]{:S(2)}) collective-permute-start(bf16[160,1792]{1,0:T(8,128)(2,1)S(1)} %get-tuple-element.31.refs_1_), channel_id=1, source_target_pairs={{0,4},{4,12},{12,8},{8,0},{1,5},{5,13},{13,9},{9,1},{2,6},{6,14},{... | collective-permute-start | bytes 1720328 | tf_op jit(solution)/shard_map/grad_first_1/ppermute | solution.py:221
  4.9 0.1 stack.59.offsets_ref.plan_ref
  5.0 0.0 collective-permute-done.3.refs_3_
  5.0 0.0 collective-permute-done.2.refs_2_
  5.0 0.0 copy-start.1
  5.0 0.0 copy-start.2
  5.0 5.2 %fold_0.1 = (f32[160,896]{1,0:T(8,128)S(1)}, f32[160,896]{1,0:T(8,128)S(1)}) custom-call(s32[14]{0:T(128)S(1)} %stack.59.offsets_ref.plan_ref, bf16[160,1792]{1,0:T(8,128)(2,1)S(1)} %get-tuple-element.32.refs_0_, bf16[160,1792]{1,0:T(8,128)(2,1)S(1)} %get-tuple-element.31.refs_1_, bf16[160,1792]{1,0:T(8,128)(2,1)S(1)} %collective-permute-done.2.refs_2_, ...), custom_call_target="tpu_custom_call" | custom-call | tf_op jit(solution)/shard_map/fold_0/pallas_call | solution.py:172
  10.3 0.0 copy-start
  10.3 2.6 %collective-permute-start.4 = (bf16[320,512]{1,0:T(8,128)(2,1)S(1)}, bf16[320,512]{1,0:T(8,128)(2,1)S(1)}, u32[]{:S(2)}, u32[]{:S(2)}) collective-permute-start(bf16[320,512]{1,0:T(8,128)(2,1)S(1)} %copy-done.1), channel_id=1, source_target_pairs={{0,4},{4,12},{12,8},{8,0},{1,5},{5,13},{13,9},{9,1},{2,6},{6,14},{... | collective-permute-start | bytes 983048 | tf_op jit(solution)/shard_map/act_first/ppermute | solution.py:221
  12.9 1.5 collective-permute-start
  14.4 2.0 %collective-permute-done.lengths_ref.refs_1_ = s32[1,3]{1,0:T(1,128)S(1)} collective-permute-done((s32[1,3]{1,0:T(1,128)S(1)}, s32[1,3]{1,0:T(1,128)S(1)}, u32[]{:S(2)}, u32[]{:S(2)}) %collective-permute-start) | collective-permute-done | bytes 44 | tf_op jit(solution)/shard_map/lengths_dp/ppermute | solution.py:226
  16.5 3.2 %collective-permute-done.8.refs_1_ = bf16[160,1792]{1,0:T(8,128)(2,1)S(1)} collective-permute-done((bf16[160,1792]{1,0:T(8,128)(2,1)S(1)}, bf16[160,1792]{1,0:T(8,128)(2,1)S(1)}, u32[]{:S(2)}, u32[]{:S(2)}) %collective-permute-start.8) | collective-permute-done | bytes 573472 | tf_op jit(solution)/shard_map/grad_first_1/ppermute | solution.py:221
  19.7 0.0 collective-permute-start.9
  19.7 1.2 collective-permute-start.15
  20.9 5.9 %collective-permute-done.4.refs_2_ = bf16[320,512]{1,0:T(8,128)(2,1)S(1)} collective-permute-done((bf16[320,512]{1,0:T(8,128)(2,1)S(1)}, bf16[320,512]{1,0:T(8,128)(2,1)S(1)}, u32[]{:S(2)}, u32[]{:S(2)}) %collective-permute-start.4) | collective-permute-done | bytes 327712 | tf_op jit(solution)/shard_map/act_first/ppermute | solution.py:221
  26.7 1.2 collective-permute-start.6
  27.9 3.4 %collective-permute-start.20 = (bf16[160,1792]{1,0:T(8,128)(2,1)S(1)}, bf16[160,1792]{1,0:T(8,128)(2,1)S(1)}, u32[]{:S(2)}, u32[]{:S(2)}) collective-permute-start(bf16[160,1792]{1,0:T(8,128)(2,1)S(1)} %collective-permute-done.8.refs_1_), channel_id=1, source_target_pairs={{0,4},{4,12},{12,8},{8,0},{1,5},{5,13},{13,9},{9,1},{2,6},{6,14},{... | collective-permute-start | bytes 1720328 | tf_op jit(solution)/shard_map/grad_second_1/ppermute | solution.py:221
  31.3 0.5 collective-permute-start.5
  31.8 14.3 %collective-permute-done.6.refs_4_ = bf16[320,512]{1,0:T(8,128)(2,1)S(1)} collective-permute-done((bf16[320,512]{1,0:T(8,128)(2,1)S(1)}, bf16[320,512]{1,0:T(8,128)(2,1)S(1)}, u32[]{:S(2)}, u32[]{:S(2)}) %collective-permute-start.6) | collective-permute-done | bytes 327712 | tf_op jit(solution)/shard_map/act_second/ppermute | solution.py:221
  46.0 4.2 %fold_1.2.refs_0_ = f32[160,896]{1,0:T(8,128)S(1)} custom-call(s32[14]{0:T(128)S(1)} %stack.59.offsets_ref.plan_ref, f32[160,896]{1,0:T(8,128)S(1)} %get-tuple-element.19.refs_0_, bf16[160,1792]{1,0:T(8,128)(2,1)S(1)} %collective-permute-done.8.refs_1_, bf16[160,1792]{1,0:T(8,128)(2,1)S(1)} %collective-permute-done.9.refs_2_, bf16[14336,896]{1,0:T(8,128)(2,1)} %bitcast.16), custom_call_target="tpu_custom_call" | custom-call | tf_op jit(solution)/shard_map/fold_1/pallas_call | solution.py:172
  50.3 0.0 collective-permute-done.15.refs_1_
  50.3 1.2 collective-permute-start.10
  51.5 6.8 %collective-permute-done.20.refs_1_ = bf16[160,1792]{1,0:T(8,128)(2,1)S(1)} collective-permute-done((bf16[160,1792]{1,0:T(8,128)(2,1)S(1)}, bf16[160,1792]{1,0:T(8,128)(2,1)S(1)}, u32[]{:S(2)}, u32[]{:S(2)}) %collective-permute-start.20) | collective-permute-done | bytes 573472 | tf_op jit(solution)/shard_map/grad_second_1/ppermute | solution.py:221
  58.3 0.0 collective-permute-start.16
  58.3 1.2 collective-permute-start.17
  59.5 0.2 collective-permute-start.21
  59.7 3.4 %collective-permute-start.22 = (bf16[160,1792]{1,0:T(8,128)(2,1)S(1)}, bf16[160,1792]{1,0:T(8,128)(2,1)S(1)}, u32[]{:S(2)}, u32[]{:S(2)}) collective-permute-start(bf16[160,1792]{1,0:T(8,128)(2,1)S(1)} %collective-permute-done.20.refs_1_), channel_id=1, source_target_pairs={{0,4},{4,12},{12,8},{8,0},{1,5},{5,13},{13,9},{9,1},{2,6},{6,14},{... | collective-permute-start | bytes 1720328 | tf_op jit(solution)/shard_map/grad_third_1/ppermute | solution.py:221
  63.1 2.2 %collective-permute-done.10.refs_6_ = bf16[320,512]{1,0:T(8,128)(2,1)S(1)} collective-permute-done((bf16[320,512]{1,0:T(8,128)(2,1)S(1)}, bf16[320,512]{1,0:T(8,128)(2,1)S(1)}, u32[]{:S(2)}, u32[]{:S(2)}) %collective-permute-start.10) | collective-permute-done | bytes 327712 | tf_op jit(solution)/shard_map/act_third/ppermute | solution.py:221
  65.3 1.6 collective-permute-done.11.refs_7_
  67.0 2.1 %project.1.mine_ref = bf16[320,512]{1,0:T(8,128)(2,1)S(1)} custom-call(s32[14]{0:T(128)S(1)} %stack.59.offsets_ref.plan_ref, bf16[320,512]{1,0:T(8,128)(2,1)S(1)} %copy-done.1, bf16[320,512]{1,0:T(8,128)(2,1)S(1)} %collective-permute-done.1.refs_1_, bf16[320,512]{1,0:T(8,128)(2,1)S(1)} %collective-permute-done.4.refs_2_, ...), custom_call_target="tpu_custom_call" | custom-call | tf_op jit(solution)/shard_map/project/pallas_call | solution.py:201
  69.0 1.9 %collective-permute-start.13 = (bf16[320,512]{1,0:T(8,128)(2,1)S(1)}, bf16[320,512]{1,0:T(8,128)(2,1)S(1)}, u32[]{:S(2)}, u32[]{:S(2)}) collective-permute-start(bf16[320,512]{1,0:T(8,128)(2,1)S(1)} %project.1.mine_ref), channel_id=1, source_target_pairs={{0,1},{1,0},{2,3},{3,2},{4,5},{5,4},{6,7},{7,6},{8,9},{9,8},{10,11... | collective-permute-start | bytes 983048 | tf_op jit(solution)/shard_map/act_dp/ppermute | solution.py:226
  71.0 4.2 %fold_1.3.refs_0_ = f32[160,896]{1,0:T(8,128)S(1)} custom-call(s32[14]{0:T(128)S(1)} %stack.59.offsets_ref.plan_ref, f32[160,896]{1,0:T(8,128)S(1)} %get-tuple-element.18.refs_0_, bf16[160,1792]{1,0:T(8,128)(2,1)S(1)} %collective-permute-done.15.refs_1_, bf16[160,1792]{1,0:T(8,128)(2,1)S(1)} %collective-permute-done.16.refs_2_, bf16[14336,896]{1,0:T(8,128)(2,1)} %bitcast.17), custom_call_target="tpu_custom_call" | custom-call | tf_op jit(solution)/shard_map/fold_1/pallas_call | solution.py:172
  75.2 2.4 %collective-permute-done.17.refs_1_ = bf16[160,1792]{1,0:T(8,128)(2,1)S(1)} collective-permute-done((bf16[160,1792]{1,0:T(8,128)(2,1)S(1)}, bf16[160,1792]{1,0:T(8,128)(2,1)S(1)}, u32[]{:S(2)}, u32[]{:S(2)}) %collective-permute-start.17) | collective-permute-done | bytes 573472 | tf_op jit(solution)/shard_map/grad_second_0/ppermute | solution.py:221
  77.6 4.2 %fold_2.3.refs_0_ = f32[160,896]{1,0:T(8,128)S(1)} custom-call(s32[14]{0:T(128)S(1)} %stack.59.offsets_ref.plan_ref, f32[160,896]{1,0:T(8,128)S(1)} %fold_1.2.refs_0_, bf16[160,1792]{1,0:T(8,128)(2,1)S(1)} %collective-permute-done.20.refs_1_, bf16[160,1792]{1,0:T(8,128)(2,1)S(1)} %collective-permute-done.21.refs_2_, bf16[14336,896]{1,0:T(8,128)(2,1)} %bitcast.18), custom_call_target="tpu_custom_call" | custom-call | tf_op jit(solution)/shard_map/fold_2/pallas_call | solution.py:172
  81.9 7.5 %collective-permute-done.22.refs_1_ = bf16[160,1792]{1,0:T(8,128)(2,1)S(1)} collective-permute-done((bf16[160,1792]{1,0:T(8,128)(2,1)S(1)}, bf16[160,1792]{1,0:T(8,128)(2,1)S(1)}, u32[]{:S(2)}, u32[]{:S(2)}) %collective-permute-start.22) | collective-permute-done | bytes 573472 | tf_op jit(solution)/shard_map/grad_third_1/ppermute | solution.py:221
  89.4 0.8 collective-permute-start.19
  90.2 0.2 collective-permute-start.14
  90.4 4.2 %fold_2.2.refs_0_ = f32[160,896]{1,0:T(8,128)S(1)} custom-call(s32[14]{0:T(128)S(1)} %stack.59.offsets_ref.plan_ref, f32[160,896]{1,0:T(8,128)S(1)} %fold_1.3.refs_0_, bf16[160,1792]{1,0:T(8,128)(2,1)S(1)} %collective-permute-done.17.refs_1_, bf16[160,1792]{1,0:T(8,128)(2,1)S(1)} %collective-permute-done.18.refs_2_, bf16[14336,896]{1,0:T(8,128)(2,1)} %bitcast.19), custom_call_target="tpu_custom_call" | custom-call | tf_op jit(solution)/shard_map/fold_2/pallas_call | solution.py:172
  94.7 4.2 %fold_3.2.refs_6_ = bf16[160,896]{1,0:T(8,128)(2,1)S(1)} custom-call(s32[14]{0:T(128)S(1)} %stack.59.offsets_ref.plan_ref, f32[160,896]{1,0:T(8,128)S(1)} %fold_2.3.refs_0_, bf16[160,1792]{1,0:T(8,128)(2,1)S(1)} %collective-permute-done.22.refs_1_, bf16[160,1792]{1,0:T(8,128)(2,1)S(1)} %collective-permute-done.23.refs_2_, bf16[14336,896]{1,0:T(8,128)(2,1)} %bitcast.20), custom_call_target="tpu_custom_call" | custom-call | tf_op jit(solution)/shard_map/fold_3/pallas_call | solution.py:172
  99.0 6.7 %collective-permute-done.19.refs_1_ = bf16[160,1792]{1,0:T(8,128)(2,1)S(1)} collective-permute-done((bf16[160,1792]{1,0:T(8,128)(2,1)S(1)}, bf16[160,1792]{1,0:T(8,128)(2,1)S(1)}, u32[]{:S(2)}, u32[]{:S(2)}) %collective-permute-start.19) | collective-permute-done | bytes 573472 | tf_op jit(solution)/shard_map/grad_third_0/ppermute | solution.py:221
  105.7 1.6 collective-permute-start.27
  107.2 0.4 collective-permute-done.24.refs_2_
  107.6 4.2 %fold_3.3.refs_4_ = bf16[160,896]{1,0:T(8,128)(2,1)S(1)} custom-call(s32[14]{0:T(128)S(1)} %stack.59.offsets_ref.plan_ref, f32[160,896]{1,0:T(8,128)S(1)} %fold_2.2.refs_0_, bf16[160,1792]{1,0:T(8,128)(2,1)S(1)} %collective-permute-done.19.refs_1_, bf16[160,1792]{1,0:T(8,128)(2,1)S(1)} %collective-permute-done.24.refs_2_, bf16[14336,896]{1,0:T(8,128)(2,1)} %bitcast.21), custom_call_target="tpu_custom_call" | custom-call | tf_op jit(solution)/shard_map/fold_3/pallas_call | solution.py:172
  111.9 3.0 %collective-permute-done.27.refs_6_ = bf16[160,896]{1,0:T(8,128)(2,1)S(1)} collective-permute-done((bf16[160,896]{1,0:T(8,128)(2,1)S(1)}, bf16[160,896]{1,0:T(8,128)(2,1)S(1)}, u32[]{:S(2)}, u32[]{:S(2)}) %collective-permute-start.27) | collective-permute-done | bytes 286752 | tf_op jit(solution)/shard_map/rot_first_1/ppermute | solution.py:221
  114.9 2.5 %collective-permute-start.28 = (bf16[160,896]{1,0:T(8,128)(2,1)S(1)}, bf16[160,896]{1,0:T(8,128)(2,1)S(1)}, u32[]{:S(2)}, u32[]{:S(2)}) collective-permute-start(bf16[160,896]{1,0:T(8,128)(2,1)S(1)} %collective-permute-done.27.refs_6_), channel_id=1, source_target_pairs={{4,0},{12,4},{8,12},{0,8},{5,1},{13,5},{9,13},{1,9},{6,2},{14,6},{... | collective-permute-start | bytes 860168 | tf_op jit(solution)/shard_map/rot_second_1/ppermute | solution.py:221
  117.4 0.0 collective-permute-start.25
  117.4 7.3 %collective-permute-done.28.refs_7_ = bf16[160,896]{1,0:T(8,128)(2,1)S(1)} collective-permute-done((bf16[160,896]{1,0:T(8,128)(2,1)S(1)}, bf16[160,896]{1,0:T(8,128)(2,1)S(1)}, u32[]{:S(2)}, u32[]{:S(2)}) %collective-permute-start.28) | collective-permute-done | bytes 286752 | tf_op jit(solution)/shard_map/rot_second_1/ppermute | solution.py:221
  124.7 1.6 collective-permute-start.31
  126.3 3.4 %collective-permute-start.29 = (bf16[160,896]{1,0:T(8,128)(2,1)S(1)}, bf16[160,896]{1,0:T(8,128)(2,1)S(1)}, u32[]{:S(2)}, u32[]{:S(2)}) collective-permute-start(bf16[160,896]{1,0:T(8,128)(2,1)S(1)} %collective-permute-done.28.refs_7_), channel_id=1, source_target_pairs={{4,0},{12,4},{8,12},{0,8},{5,1},{13,5},{9,13},{1,9},{6,2},{14,6},{... | collective-permute-start | bytes 860168 | tf_op jit(solution)/shard_map/rot_third_1/ppermute | solution.py:221
  129.7 4.0 %collective-permute-done.25.refs_4_ = bf16[160,896]{1,0:T(8,128)(2,1)S(1)} collective-permute-done((bf16[160,896]{1,0:T(8,128)(2,1)S(1)}, bf16[160,896]{1,0:T(8,128)(2,1)S(1)}, u32[]{:S(2)}, u32[]{:S(2)}) %collective-permute-start.25) | collective-permute-done | bytes 286752 | tf_op jit(solution)/shard_map/rot_first_0/ppermute | solution.py:221
  133.7 1.6 collective-permute-start.30
  135.2 3.8 %collective-permute-done.29.refs_7_ = bf16[160,896]{1,0:T(8,128)(2,1)S(1)} collective-permute-done((bf16[160,896]{1,0:T(8,128)(2,1)S(1)}, bf16[160,896]{1,0:T(8,128)(2,1)S(1)}, u32[]{:S(2)}, u32[]{:S(2)}) %collective-permute-start.29) | collective-permute-done | bytes 286752 | tf_op jit(solution)/shard_map/rot_third_1/ppermute | solution.py:221
  139.0 3.4 %collective-permute-done.30.refs_8_.refs_10_ = bf16[160,896]{1,0:T(8,128)(2,1)S(1)} collective-permute-done((bf16[160,896]{1,0:T(8,128)(2,1)S(1)}, bf16[160,896]{1,0:T(8,128)(2,1)S(1)}, u32[]{:S(2)}, u32[]{:S(2)}) %collective-permute-start.30) | collective-permute-done | bytes 286752 | tf_op jit(solution)/shard_map/rot_first_dp/ppermute | solution.py:226
  142.4 2.8 %collective-permute-done.26.refs_5_ = bf16[160,896]{1,0:T(8,128)(2,1)S(1)} collective-permute-done((bf16[160,896]{1,0:T(8,128)(2,1)S(1)}, bf16[160,896]{1,0:T(8,128)(2,1)S(1)}, u32[]{:S(2)}, u32[]{:S(2)}) %collective-permute-start.26) | collective-permute-done | bytes 286752 | tf_op jit(solution)/shard_map/rot_second_0/ppermute | solution.py:221
  145.2 1.2 collective-permute-start.33
  146.5 1.1 masked_windows.2.refs_2_
  147.6 1.1 masked_windows.3.refs_3_
  148.7 5.5 %collective-permute-done.32.refs_5_ = bf16[160,896]{1,0:T(8,128)(2,1)S(1)} collective-permute-done((bf16[160,896]{1,0:T(8,128)(2,1)S(1)}, bf16[160,896]{1,0:T(8,128)(2,1)S(1)}, u32[]{:S(2)}, u32[]{:S(2)}) %collective-permute-start.32) | collective-permute-done | bytes 286752 | tf_op jit(solution)/shard_map/rot_third_0/ppermute | solution.py:221
  154.3 1.4 collective-permute-start.34
  155.7 6.9 %squared_sums.2.refs_12_ = f32[1024,1792]{1,0:T(8,128)} custom-call(s32[14]{0:T(128)S(1)} %stack.59.offsets_ref.plan_ref, s32[1,3]{1,0:T(1,128)S(1)} %copy-done.2, s32[1,3]{1,0:T(1,128)S(1)} %collective-permute-done.lengths_ref.refs_1_, bf16[3,1024,256]{2,1,0:T(8,128)(2,1)S(1)} %masked_windows.2.refs_2_, bf16[3,1024,256]{2,1,0:T(8,128)(2,1)S(1)} %masked_windows.3.refs_3_, ...), custom_call_target="tpu_custom_call" | custom-call | tf_op jit(solution)/shard_map/squared_sums/pallas_call | solution.py:126
  162.5 6.9 %squared_sums.3 = f32[1024,1792]{1,0:T(8,128)} custom-call(s32[14]{0:T(128)S(1)} %stack.59.offsets_ref.plan_ref, s32[1,3]{1,0:T(1,128)S(1)} %copy-done.2, s32[1,3]{1,0:T(1,128)S(1)} %collective-permute-done.lengths_ref.refs_1_, bf16[3,1024,256]{2,1,0:T(8,128)(2,1)S(1)} %masked_windows.2.refs_2_, ...), custom_call_target="tpu_custom_call", output_to_operand_aliasing={{}: (13, {})} | custom-call | tf_op jit(solution)/shard_map/squared_sums/pallas_call | solution.py:126
  (30 shorter events, 0.2 us)
Async XLA Ops:
  1.3 3.7 %collective-permute-start.3 = (bf16[160,1792]{1,0:T(8,128)(2,1)S(1)}, bf16[160,1792]{1,0:T(8,128)(2,1)S(1)}, u32[]{:S(2)}, u32[]{:S(2)}) collective-permute-start(bf16[160,1792]{1,0:T(8,128)(2,1)S(1)} %get-tuple-element.31.refs_1_), channel_id=1, source_target_pairs={{0,2},{2,0},{1,3},{3,1},{4,6},{6,4},{5,7},{7,5},{8,10},{10,8},{9,1... | collective-permute-start | bytes 1720328 | tf_op jit(solution)/shard_map/grad_0_cols_1/ppermute | solution.py:226
  1.8 3.2 %collective-permute-start.2 = (bf16[160,1792]{1,0:T(8,128)(2,1)S(1)}, bf16[160,1792]{1,0:T(8,128)(2,1)S(1)}, u32[]{:S(2)}, u32[]{:S(2)}) collective-permute-start(bf16[160,1792]{1,0:T(8,128)(2,1)S(1)} %get-tuple-element.32.refs_0_), channel_id=1, source_target_pairs={{0,2},{2,0},{1,3},{3,1},{4,6},{6,4},{5,7},{7,5},{8,10},{10,8},{9,1... | collective-permute-start | bytes 1720328 | tf_op jit(solution)/shard_map/grad_0_cols_0/ppermute | solution.py:226
  1.9 17.8 %collective-permute-start.8 = (bf16[160,1792]{1,0:T(8,128)(2,1)S(1)}, bf16[160,1792]{1,0:T(8,128)(2,1)S(1)}, u32[]{:S(2)}, u32[]{:S(2)}) collective-permute-start(bf16[160,1792]{1,0:T(8,128)(2,1)S(1)} %get-tuple-element.31.refs_1_), channel_id=1, source_target_pairs={{0,4},{4,12},{12,8},{8,0},{1,5},{5,13},{13,9},{9,1},{2,6},{6,14},{... | collective-permute-start | bytes 1720328 | tf_op jit(solution)/shard_map/grad_first_1/ppermute | solution.py:221
  5.0 5.2 %copy-start.1 = (bf16[320,512]{1,0:T(8,128)(2,1)S(1)}, bf16[320,512]{1,0:T(8,128)(2,1)}, u32[]{:S(2)}) copy-start(bf16[320,512]{1,0:T(8,128)(2,1)} %refs_0_.3) | copy-start | bytes 983044
  5.0 7.9 %copy-start.2 = (s32[1,3]{1,0:T(1,128)S(1)}, s32[1,3]{1,0:T(1,128)}, u32[]{:S(2)}) copy-start(s32[1,3]{1,0:T(1,128)} %refs_0_.5) | copy-start | bytes 40
  10.3 56.7 %copy-start = (bf16[4096,512]{1,0:T(8,128)(2,1)S(1)}, bf16[4096,512]{1,0:T(8,128)(2,1)}, u32[]{:S(2)}) copy-start(bf16[4096,512]{1,0:T(8,128)(2,1)} %refs_8_.1) | copy-start | bytes 12582916
  10.3 16.4 %collective-permute-start.4 = (bf16[320,512]{1,0:T(8,128)(2,1)S(1)}, bf16[320,512]{1,0:T(8,128)(2,1)S(1)}, u32[]{:S(2)}, u32[]{:S(2)}) collective-permute-start(bf16[320,512]{1,0:T(8,128)(2,1)S(1)} %copy-done.1), channel_id=1, source_target_pairs={{0,4},{4,12},{12,8},{8,0},{1,5},{5,13},{13,9},{9,1},{2,6},{6,14},{... | collective-permute-start | bytes 983048 | tf_op jit(solution)/shard_map/act_first/ppermute | solution.py:221
  12.9 3.5 %collective-permute-start = (s32[1,3]{1,0:T(1,128)S(1)}, s32[1,3]{1,0:T(1,128)S(1)}, u32[]{:S(2)}, u32[]{:S(2)}) collective-permute-start(s32[1,3]{1,0:T(1,128)S(1)} %copy-done.2), channel_id=1, source_target_pairs={{0,1},{1,0},{2,3},{3,2},{4,5},{5,4},{6,7},{7,6},{8,9},{9,8},{10,11... | collective-permute-start | bytes 44 | tf_op jit(solution)/shard_map/lengths_dp/ppermute | solution.py:226
  19.7 11.6 %collective-permute-start.9 = (bf16[160,1792]{1,0:T(8,128)(2,1)S(1)}, bf16[160,1792]{1,0:T(8,128)(2,1)S(1)}, u32[]{:S(2)}, u32[]{:S(2)}) collective-permute-start(bf16[160,1792]{1,0:T(8,128)(2,1)S(1)} %collective-permute-done.8.refs_1_), channel_id=1, source_target_pairs={{0,2},{2,0},{1,3},{3,1},{4,6},{6,4},{5,7},{7,5},{8,10},{10,8},{9,1... | collective-permute-start | bytes 1720328 | tf_op jit(solution)/shard_map/grad_1_cols_1/ppermute | solution.py:226
  19.7 30.6 %collective-permute-start.15 = (bf16[160,1792]{1,0:T(8,128)(2,1)S(1)}, bf16[160,1792]{1,0:T(8,128)(2,1)S(1)}, u32[]{:S(2)}, u32[]{:S(2)}) collective-permute-start(bf16[160,1792]{1,0:T(8,128)(2,1)S(1)} %get-tuple-element.32.refs_0_), channel_id=1, source_target_pairs={{0,4},{4,12},{12,8},{8,0},{1,5},{5,13},{13,9},{9,1},{2,6},{6,14},{... | collective-permute-start | bytes 1720328 | tf_op jit(solution)/shard_map/grad_first_0/ppermute | solution.py:221
  26.7 19.3 %collective-permute-start.6 = (bf16[320,512]{1,0:T(8,128)(2,1)S(1)}, bf16[320,512]{1,0:T(8,128)(2,1)S(1)}, u32[]{:S(2)}, u32[]{:S(2)}) collective-permute-start(bf16[320,512]{1,0:T(8,128)(2,1)S(1)} %collective-permute-done.4.refs_2_), channel_id=1, source_target_pairs={{0,4},{4,12},{12,8},{8,0},{1,5},{5,13},{13,9},{9,1},{2,6},{6,14},{... | collective-permute-start | bytes 983048 | tf_op jit(solution)/shard_map/act_second/ppermute | solution.py:221
  27.9 30.4 %collective-permute-start.20 = (bf16[160,1792]{1,0:T(8,128)(2,1)S(1)}, bf16[160,1792]{1,0:T(8,128)(2,1)S(1)}, u32[]{:S(2)}, u32[]{:S(2)}) collective-permute-start(bf16[160,1792]{1,0:T(8,128)(2,1)S(1)} %collective-permute-done.8.refs_1_), channel_id=1, source_target_pairs={{0,4},{4,12},{12,8},{8,0},{1,5},{5,13},{13,9},{9,1},{2,6},{6,14},{... | collective-permute-start | bytes 1720328 | tf_op jit(solution)/shard_map/grad_second_1/ppermute | solution.py:221
  31.3 27.1 %collective-permute-start.1 = (bf16[320,512]{1,0:T(8,128)(2,1)S(1)}, bf16[320,512]{1,0:T(8,128)(2,1)S(1)}, u32[]{:S(2)}, u32[]{:S(2)}) collective-permute-start(bf16[320,512]{1,0:T(8,128)(2,1)S(1)} %copy-done.1), channel_id=1, source_target_pairs={{0,2},{2,0},{1,3},{3,1},{4,6},{6,4},{5,7},{7,5},{8,10},{10,8},{9,1... | collective-permute-start | bytes 983048 | tf_op jit(solution)/shard_map/act_cols/ppermute | solution.py:226
  31.3 28.2 %collective-permute-start.5 = (bf16[320,512]{1,0:T(8,128)(2,1)S(1)}, bf16[320,512]{1,0:T(8,128)(2,1)S(1)}, u32[]{:S(2)}, u32[]{:S(2)}) collective-permute-start(bf16[320,512]{1,0:T(8,128)(2,1)S(1)} %collective-permute-done.4.refs_2_), channel_id=1, source_target_pairs={{0,2},{2,0},{1,3},{3,1},{4,6},{6,4},{5,7},{7,5},{8,10},{10,8},{9,1... | collective-permute-start | bytes 983048 | tf_op jit(solution)/shard_map/act_cols/ppermute | solution.py:226
  46.0 13.7 %collective-permute-start.7 = (bf16[320,512]{1,0:T(8,128)(2,1)S(1)}, bf16[320,512]{1,0:T(8,128)(2,1)S(1)}, u32[]{:S(2)}, u32[]{:S(2)}) collective-permute-start(bf16[320,512]{1,0:T(8,128)(2,1)S(1)} %collective-permute-done.6.refs_4_), channel_id=1, source_target_pairs={{0,2},{2,0},{1,3},{3,1},{4,6},{6,4},{5,7},{7,5},{8,10},{10,8},{9,1... | collective-permute-start | bytes 983048 | tf_op jit(solution)/shard_map/act_cols/ppermute | solution.py:226
  50.3 15.0 %collective-permute-start.10 = (bf16[320,512]{1,0:T(8,128)(2,1)S(1)}, bf16[320,512]{1,0:T(8,128)(2,1)S(1)}, u32[]{:S(2)}, u32[]{:S(2)}) collective-permute-start(bf16[320,512]{1,0:T(8,128)(2,1)S(1)} %collective-permute-done.6.refs_4_), channel_id=1, source_target_pairs={{0,4},{4,12},{12,8},{8,0},{1,5},{5,13},{13,9},{9,1},{2,6},{6,14},{... | collective-permute-start | bytes 983048 | tf_op jit(solution)/shard_map/act_third/ppermute | solution.py:221
  58.3 12.6 %collective-permute-start.16 = (bf16[160,1792]{1,0:T(8,128)(2,1)S(1)}, bf16[160,1792]{1,0:T(8,128)(2,1)S(1)}, u32[]{:S(2)}, u32[]{:S(2)}) collective-permute-start(bf16[160,1792]{1,0:T(8,128)(2,1)S(1)} %collective-permute-done.15.refs_1_), channel_id=1, source_target_pairs={{0,2},{2,0},{1,3},{3,1},{4,6},{6,4},{5,7},{7,5},{8,10},{10,8},{9,1... | collective-permute-start | bytes 1720328 | tf_op jit(solution)/shard_map/grad_1_cols_0/ppermute | solution.py:226
  58.3 19.3 %collective-permute-start.17 = (bf16[160,1792]{1,0:T(8,128)(2,1)S(1)}, bf16[160,1792]{1,0:T(8,128)(2,1)S(1)}, u32[]{:S(2)}, u32[]{:S(2)}) collective-permute-start(bf16[160,1792]{1,0:T(8,128)(2,1)S(1)} %collective-permute-done.15.refs_1_), channel_id=1, source_target_pairs={{0,4},{4,12},{12,8},{8,0},{1,5},{5,13},{13,9},{9,1},{2,6},{6,14},{... | collective-permute-start | bytes 1720328 | tf_op jit(solution)/shard_map/grad_second_0/ppermute | solution.py:221
  59.5 18.1 %collective-permute-start.21 = (bf16[160,1792]{1,0:T(8,128)(2,1)S(1)}, bf16[160,1792]{1,0:T(8,128)(2,1)S(1)}, u32[]{:S(2)}, u32[]{:S(2)}) collective-permute-start(bf16[160,1792]{1,0:T(8,128)(2,1)S(1)} %collective-permute-done.20.refs_1_), channel_id=1, source_target_pairs={{0,2},{2,0},{1,3},{3,1},{4,6},{6,4},{5,7},{7,5},{8,10},{10,8},{9,1... | collective-permute-start | bytes 1720328 | tf_op jit(solution)/shard_map/grad_2_cols_1/ppermute | solution.py:226
  59.7 29.6 %collective-permute-start.22 = (bf16[160,1792]{1,0:T(8,128)(2,1)S(1)}, bf16[160,1792]{1,0:T(8,128)(2,1)S(1)}, u32[]{:S(2)}, u32[]{:S(2)}) collective-permute-start(bf16[160,1792]{1,0:T(8,128)(2,1)S(1)} %collective-permute-done.20.refs_1_), channel_id=1, source_target_pairs={{0,4},{4,12},{12,8},{8,0},{1,5},{5,13},{13,9},{9,1},{2,6},{6,14},{... | collective-permute-start | bytes 1720328 | tf_op jit(solution)/shard_map/grad_third_1/ppermute | solution.py:221
  65.3 1.6 collective-permute-start.11
  69.0 21.2 %collective-permute-start.13 = (bf16[320,512]{1,0:T(8,128)(2,1)S(1)}, bf16[320,512]{1,0:T(8,128)(2,1)S(1)}, u32[]{:S(2)}, u32[]{:S(2)}) collective-permute-start(bf16[320,512]{1,0:T(8,128)(2,1)S(1)} %project.1.mine_ref), channel_id=1, source_target_pairs={{0,1},{1,0},{2,3},{3,2},{4,5},{5,4},{6,7},{7,6},{8,9},{9,8},{10,11... | collective-permute-start | bytes 983048 | tf_op jit(solution)/shard_map/act_dp/ppermute | solution.py:226
  77.6 12.8 %collective-permute-start.18 = (bf16[160,1792]{1,0:T(8,128)(2,1)S(1)}, bf16[160,1792]{1,0:T(8,128)(2,1)S(1)}, u32[]{:S(2)}, u32[]{:S(2)}) collective-permute-start(bf16[160,1792]{1,0:T(8,128)(2,1)S(1)} %collective-permute-done.17.refs_1_), channel_id=1, source_target_pairs={{0,2},{2,0},{1,3},{3,1},{4,6},{6,4},{5,7},{7,5},{8,10},{10,8},{9,1... | collective-permute-start | bytes 1720328 | tf_op jit(solution)/shard_map/grad_2_cols_0/ppermute | solution.py:226
  89.4 5.3 %collective-permute-start.23 = (bf16[160,1792]{1,0:T(8,128)(2,1)S(1)}, bf16[160,1792]{1,0:T(8,128)(2,1)S(1)}, u32[]{:S(2)}, u32[]{:S(2)}) collective-permute-start(bf16[160,1792]{1,0:T(8,128)(2,1)S(1)} %collective-permute-done.22.refs_1_), channel_id=1, source_target_pairs={{0,2},{2,0},{1,3},{3,1},{4,6},{6,4},{5,7},{7,5},{8,10},{10,8},{9,1... | collective-permute-start | bytes 1720328 | tf_op jit(solution)/shard_map/grad_3_cols_1/ppermute | solution.py:226
  89.4 16.3 %collective-permute-start.19 = (bf16[160,1792]{1,0:T(8,128)(2,1)S(1)}, bf16[160,1792]{1,0:T(8,128)(2,1)S(1)}, u32[]{:S(2)}, u32[]{:S(2)}) collective-permute-start(bf16[160,1792]{1,0:T(8,128)(2,1)S(1)} %collective-permute-done.17.refs_1_), channel_id=1, source_target_pairs={{0,4},{4,12},{12,8},{8,0},{1,5},{5,13},{13,9},{9,1},{2,6},{6,14},{... | collective-permute-start | bytes 1720328 | tf_op jit(solution)/shard_map/grad_third_0/ppermute | solution.py:221
  90.2 15.4 %collective-permute-start.14 = (bf16[320,512]{1,0:T(8,128)(2,1)S(1)}, bf16[320,512]{1,0:T(8,128)(2,1)S(1)}, u32[]{:S(2)}, u32[]{:S(2)}) collective-permute-start(bf16[320,512]{1,0:T(8,128)(2,1)S(1)} %collective-permute-done.13.mine_ref), channel_id=1, source_target_pairs={{0,2},{2,0},{1,3},{3,1},{4,6},{6,4},{5,7},{7,5},{8,10},{10,8},{9,1... | collective-permute-start | bytes 983048 | tf_op jit(solution)/shard_map/rot_act_cols/ppermute | solution.py:226
  105.7 2.0 %collective-permute-start.24 = (bf16[160,1792]{1,0:T(8,128)(2,1)S(1)}, bf16[160,1792]{1,0:T(8,128)(2,1)S(1)}, u32[]{:S(2)}, u32[]{:S(2)}) collective-permute-start(bf16[160,1792]{1,0:T(8,128)(2,1)S(1)} %collective-permute-done.19.refs_1_), channel_id=1, source_target_pairs={{0,2},{2,0},{1,3},{3,1},{4,6},{6,4},{5,7},{7,5},{8,10},{10,8},{9,1... | collective-permute-start | bytes 1720328 | tf_op jit(solution)/shard_map/grad_3_cols_0/ppermute | solution.py:226
  105.7 9.2 %collective-permute-start.27 = (bf16[160,896]{1,0:T(8,128)(2,1)S(1)}, bf16[160,896]{1,0:T(8,128)(2,1)S(1)}, u32[]{:S(2)}, u32[]{:S(2)}) collective-permute-start(bf16[160,896]{1,0:T(8,128)(2,1)S(1)} %fold_3.2.refs_6_), channel_id=1, source_target_pairs={{4,0},{12,4},{8,12},{0,8},{5,1},{13,5},{9,13},{1,9},{6,2},{14,6},{... | collective-permute-start | bytes 860168 | tf_op jit(solution)/shard_map/rot_first_1/ppermute | solution.py:221
  114.9 9.8 %collective-permute-start.28 = (bf16[160,896]{1,0:T(8,128)(2,1)S(1)}, bf16[160,896]{1,0:T(8,128)(2,1)S(1)}, u32[]{:S(2)}, u32[]{:S(2)}) collective-permute-start(bf16[160,896]{1,0:T(8,128)(2,1)S(1)} %collective-permute-done.27.refs_6_), channel_id=1, source_target_pairs={{4,0},{12,4},{8,12},{0,8},{5,1},{13,5},{9,13},{1,9},{6,2},{14,6},{... | collective-permute-start | bytes 860168 | tf_op jit(solution)/shard_map/rot_second_1/ppermute | solution.py:221
  117.4 16.2 %collective-permute-start.25 = (bf16[160,896]{1,0:T(8,128)(2,1)S(1)}, bf16[160,896]{1,0:T(8,128)(2,1)S(1)}, u32[]{:S(2)}, u32[]{:S(2)}) collective-permute-start(bf16[160,896]{1,0:T(8,128)(2,1)S(1)} %fold_3.3.refs_4_), channel_id=1, source_target_pairs={{0,4},{4,12},{12,8},{8,0},{1,5},{5,13},{13,9},{9,1},{2,6},{6,14},{... | collective-permute-start | bytes 860168 | tf_op jit(solution)/shard_map/rot_first_0/ppermute | solution.py:221
  124.7 10.5 %collective-permute-start.31 = (bf16[160,896]{1,0:T(8,128)(2,1)S(1)}, bf16[160,896]{1,0:T(8,128)(2,1)S(1)}, u32[]{:S(2)}, u32[]{:S(2)}) collective-permute-start(bf16[160,896]{1,0:T(8,128)(2,1)S(1)} %broadcast_select_fusion.1), channel_id=1, source_target_pairs={{0,1},{1,0},{2,3},{3,2},{4,5},{5,4},{6,7},{7,6},{8,9},{9,8},{10,11... | collective-permute-start | bytes 860168 | tf_op jit(solution)/shard_map/rot_second_dp_1/ppermute | solution.py:226
  126.3 12.7 %collective-permute-start.29 = (bf16[160,896]{1,0:T(8,128)(2,1)S(1)}, bf16[160,896]{1,0:T(8,128)(2,1)S(1)}, u32[]{:S(2)}, u32[]{:S(2)}) collective-permute-start(bf16[160,896]{1,0:T(8,128)(2,1)S(1)} %collective-permute-done.28.refs_7_), channel_id=1, source_target_pairs={{4,0},{12,4},{8,12},{0,8},{5,1},{13,5},{9,13},{1,9},{6,2},{14,6},{... | collective-permute-start | bytes 860168 | tf_op jit(solution)/shard_map/rot_third_1/ppermute | solution.py:221
  133.7 8.7 %collective-permute-start.30 = (bf16[160,896]{1,0:T(8,128)(2,1)S(1)}, bf16[160,896]{1,0:T(8,128)(2,1)S(1)}, u32[]{:S(2)}, u32[]{:S(2)}) collective-permute-start(bf16[160,896]{1,0:T(8,128)(2,1)S(1)} %broadcast_select_fusion.3), channel_id=1, source_target_pairs={{0,1},{1,0},{2,3},{3,2},{4,5},{5,4},{6,7},{7,6},{8,9},{9,8},{10,11... | collective-permute-start | bytes 860168 | tf_op jit(solution)/shard_map/rot_first_dp/ppermute | solution.py:226
  135.2 10.0 %collective-permute-start.26 = (bf16[160,896]{1,0:T(8,128)(2,1)S(1)}, bf16[160,896]{1,0:T(8,128)(2,1)S(1)}, u32[]{:S(2)}, u32[]{:S(2)}) collective-permute-start(bf16[160,896]{1,0:T(8,128)(2,1)S(1)} %collective-permute-done.25.refs_4_), channel_id=1, source_target_pairs={{0,4},{4,12},{12,8},{8,0},{1,5},{5,13},{13,9},{9,1},{2,6},{6,14},{... | collective-permute-start | bytes 860168 | tf_op jit(solution)/shard_map/rot_second_0/ppermute | solution.py:221
  135.2 11.2 %collective-permute-start.12 = (bf16[320,512]{1,0:T(8,128)(2,1)S(1)}, bf16[320,512]{1,0:T(8,128)(2,1)S(1)}, u32[]{:S(2)}, u32[]{:S(2)}) collective-permute-start(bf16[320,512]{1,0:T(8,128)(2,1)S(1)} %project.1.mine_ref), channel_id=1, source_target_pairs={{0,2},{2,0},{1,3},{3,1},{4,6},{6,4},{5,7},{7,5},{8,10},{10,8},{9,1... | collective-permute-start | bytes 983048 | tf_op jit(solution)/shard_map/rot_act_cols/ppermute | solution.py:226
  145.2 9.0 %collective-permute-start.32 = (bf16[160,896]{1,0:T(8,128)(2,1)S(1)}, bf16[160,896]{1,0:T(8,128)(2,1)S(1)}, u32[]{:S(2)}, u32[]{:S(2)}) collective-permute-start(bf16[160,896]{1,0:T(8,128)(2,1)S(1)} %collective-permute-done.26.refs_5_), channel_id=1, source_target_pairs={{0,4},{4,12},{12,8},{8,0},{1,5},{5,13},{13,9},{9,1},{2,6},{6,14},{... | collective-permute-start | bytes 860168 | tf_op jit(solution)/shard_map/rot_third_0/ppermute | solution.py:221
  145.2 9.0 %collective-permute-start.33 = (bf16[160,896]{1,0:T(8,128)(2,1)S(1)}, bf16[160,896]{1,0:T(8,128)(2,1)S(1)}, u32[]{:S(2)}, u32[]{:S(2)}) collective-permute-start(bf16[160,896]{1,0:T(8,128)(2,1)S(1)} %broadcast_select_fusion), channel_id=1, source_target_pairs={{0,1},{1,0},{2,3},{3,2},{4,5},{5,4},{6,7},{7,6},{8,9},{9,8},{10,11... | collective-permute-start | bytes 860168 | tf_op jit(solution)/shard_map/rot_second_dp_0/ppermute | solution.py:226
  154.3 8.2 %collective-permute-start.34 = (bf16[160,896]{1,0:T(8,128)(2,1)S(1)}, bf16[160,896]{1,0:T(8,128)(2,1)S(1)}, u32[]{:S(2)}, u32[]{:S(2)}) collective-permute-start(bf16[160,896]{1,0:T(8,128)(2,1)S(1)} %broadcast_select_fusion.2), channel_id=1, source_target_pairs={{0,1},{1,0},{2,3},{3,2},{4,5},{5,4},{6,7},{7,6},{8,9},{9,8},{10,11... | collective-permute-start | bytes 860168 | tf_op jit(solution)/shard_map/rot_third_dp/ppermute | solution.py:226

commit v5 on v3

--- a/solution.py
+++ b/solution.py
@@ -8,7 +8,7 @@
 from jax.sharding import PartitionSpec as P
 
 STEP = 64
-VMEM_BYTES = 56 * 1024 * 1024
+VMEM_BYTES = 40 * 1024 * 1024
 
 
 def span_of(lengths_ref, example):
@@ -88,7 +88,7 @@
         act_copy(block, now).wait()
 
     rows, columns = out_ref.shape
-    wide, high = min(columns, 256), min(rows, 128)
+    wide, high = min(columns, 256), min(rows, 256)
     for left in range(0, columns, wide):
         right = min(left + wide, columns)
         for top in range(0, rows, high):
@@ -186,26 +186,41 @@
     )(offsets, *([start] if started else []), *mine, *theirs, basis)
 
 
-def project_kernel(plan_ref, *refs):
-    blocks, basis_ref, out_ref = refs[:-2], refs[-2], refs[-1]
+def project_kernel(tops, steps, offsets_ref, *refs):
+    blocks, basis_ref, out_ref, sum_ref = refs[:-3], refs[-3], refs[-2], refs[-1]
+    step = pl.program_id(0)
     deep = blocks[0].shape[1]
-    total = None
-    for place, ref in enumerate(blocks):
-        rows = pl.ds(pl.multiple_of(plan_ref[place] * deep, deep), deep)
-        product = jnp.dot(ref[...], basis_ref[rows, :], preferred_element_type=jnp.float32)
-        total = product if total is None else total + product
-    out_ref[...] = total.astype(out_ref.dtype)
-
-
-def project(blocks, basis, plan):
+
+    @pl.when(step == 0)
+    def _():
+        sum_ref[...] = jnp.zeros_like(sum_ref)
+
+    for ref, (top, place) in zip(blocks, tops):
+        begin = pl.multiple_of((offsets_ref[place] * steps + step) * deep, deep)
+        sum_ref[top : top + ref.shape[0], :] += jnp.dot(
+            ref[...], basis_ref[pl.ds(begin, deep), :], preferred_element_type=jnp.float32
+        )
+
+    @pl.when(step == steps - 1)
+    def _():
+        out_ref[...] = sum_ref[...].astype(out_ref.dtype)
+
+
+def project(blocks, tops, tokens, features, basis, offsets):
+    columns = basis.shape[1]
+    deep = 256
+    steps = (blocks[0].shape[1] - features) // deep
+    tails = [pl.BlockSpec((x.shape[0], deep), lambda i: (0, features // deep + i)) for x in blocks]
     return pl.pallas_call(
-        project_kernel,
+        functools.partial(project_kernel, tops, steps),
         name="project",
-        out_shape=jax.ShapeDtypeStruct((blocks[0].shape[0], basis.shape[1]), basis.dtype),
-        in_specs=[pl.BlockSpec(memory_space=pltpu.SMEM)] + [pl.BlockSpec(memory_space=pltpu.VMEM)] * (len(blocks) + 1),
-        out_specs=pl.BlockSpec(memory_space=pltpu.VMEM),
+        out_shape=jax.ShapeDtypeStruct((tokens, columns), basis.dtype),
+        grid=(steps,),
+        in_specs=[pl.BlockSpec(memory_space=pltpu.SMEM), *tails, pl.BlockSpec(basis.shape, lambda i: (0, 0))],
+        out_specs=pl.BlockSpec((tokens, columns), lambda i: (0, 0)),
+        scratch_shapes=[pltpu.VMEM((tokens, columns), jnp.float32)],
         compiler_params=pltpu.CompilerParams(vmem_limit_bytes=VMEM_BYTES),
-    )(plan, *blocks, basis)
+    )(offsets, *blocks, basis)
 
 
 RING = [(0, 1), (1, 3), (3, 2), (2, 0)]
@@ -249,46 +264,53 @@
     features = gradients.shape[1]
 
     def crossed(chunks, place):
-        return [swap(x, "col", f"grad_{place}_cols_{i}") for i, x in enumerate(chunks)]
+        return [swap(x, "col", f"tokens_{place}_cols_{i}") for i, x in enumerate(chunks)]
 
     def fold(start, mine, theirs, place):
         return fold_block(start, mine, theirs, basis_grad, features, plan, place, jnp.float32)[0]
 
+    own = [jnp.concatenate([x[i : i + half] for x in (gradients, activations)], axis=1) for i in (0, half)]
+    slots = [(own, crossed(own, 0))]
+    start = fold_block(None, *slots[0], basis_grad, features, plan, 0, jnp.float32, 2)
+
     def piece(sums, x, place, i):
-        theirs = swap(x, "col", f"grad_{place}_cols_{i}")
+        theirs = swap(x, "col", f"tokens_{place}_cols_{i}")
         kind = jnp.bfloat16 if place == 3 else jnp.float32
-        return fold_block(sums, [x], [theirs], basis_grad, features, plan, place, kind)[0]
-
-    own = [gradients[i : i + half] for i in (0, half)]
-    sums = list(fold_block(None, own, crossed(own, 0), basis_grad, features, plan, 0, jnp.float32, 2))
-    firsts = [after(hop(x, f"grad_first_{i}"), sums[i], spans[1]) for i, x in enumerate(own)]
-    act_first = hop(after(activations, *sums), "act_first")
-    seconds = [hop(after(x, act_first) if 0 else x, f"grad_second_{i}") for i, x in enumerate(firsts)]
-    act_second = hop(act_first, "act_second")
-    act_third = hop(act_second, "act_third")
+        return theirs, fold_block(sums, [x], [theirs], basis_grad, features, plan, place, kind)[0]
+
+    owns, kept, sums = [None, None], [[], [], []], list(start)
+    firsts = [hop(x, f"tokens_first_{i}") for i, x in enumerate(own)]
+    seconds = [hop(after(x, sums[i], spans[1]), f"tokens_second_{i}") for i, x in enumerate(firsts)]
     thirds = []
     for i in range(2):
-        sums[i] = piece(sums[i], firsts[i], 1, i)
-        thirds.append(hop(after(seconds[i], sums[i], *([act_second] if i else [])), f"grad_third_{i}"))
-    sums[1] = piece(sums[1], seconds[1], 2, 1)
-    acts = (activations, act_first, act_second, act_third)
-    rotated = project([x for s in acts for x in (s, swap(s, "col", "act_cols"))], q_act, plan)
+        theirs, sums[i] = piece(sums[i], firsts[i], 1, i)
+        kept[0].append((firsts[i], theirs))
+        thirds.append(hop(after(seconds[i], sums[i]), f"tokens_third_{i}"))
+        theirs, sums[i] = piece(sums[i], seconds[i], 2, i)
+        kept[1].append((seconds[i], theirs))
+    for i in (1, 0):
+        third = after(thirds[i], sums[i])
+        theirs, owns[i] = piece(sums[i], third, 3, i)
+        kept[2].append((third, theirs))
+    kept[2] = kept[2][::-1]
+    slots += [tuple(zip(*pairs)) for pairs in kept]
+
+    first = [hop(x, f"rot_first_{i}", i == 1) for i, x in enumerate(owns)]
+    blocks = [x for mine, theirs in slots for x in (*mine, *theirs)]
+    blocks[-1] = after(blocks[-1], *owns)
+    tops = [(top, 2 * place + i) for place in range(4) for i in range(2) for top in (0, half)]
+    rotated = project(blocks, tops, tokens, features, q_act, plan)
     other = swap(rotated, "dp", "act_dp")
-    acts = [(x, swap(x, "col", "rot_act_cols")) for x in (rotated, other)]
-    owns = [None, piece(sums[1], after(thirds[1], sums[1], rotated), 3, 1)]
-    sums[0] = piece(after(sums[0], owns[1]) if 0 else sums[0], seconds[0], 2, 0)
-    owns[0] = piece(sums[0], after(thirds[0], sums[0], owns[1], *acts[1]), 3, 0)
-
-    acts = [masked_windows(plan, CORE, s, *x, window) for s, x in zip(spans, acts)]
-    first = [hop(x, f"rot_first_{i}", i == 1) for i, x in enumerate(owns)]
     second = [None, hop(after(first[1], owns[0]), "rot_second_1", True)]
-    second[0] = hop(first[0], "rot_second_0")
+    second[0] = hop(after(first[0], rotated), "rot_second_0")
     cross_first = swap(jnp.where(turn, first[0], first[1]), "dp", "rot_first_dp")
     early = [jnp.where(home, s, o) for s, o in zip(second, owns)]
     early[1] = swap(early[1], "dp", "rot_second_dp_1")
     third = [None, hop(second[1], "rot_third_1", True)]
-    third[0] = hop(after(second[0], third[1], cross_first, early[1]), "rot_third_0")
+    third[0] = hop(after(second[0], third[1], cross_first, early[1], other), "rot_third_0")
     early[0] = swap(early[0], "dp", "rot_second_dp_0")
+    acts = [(x, swap(x, "col", "rot_act_cols")) for x in (rotated, other)]
+    acts = [masked_windows(plan, CORE, s, *x, window) for s, x in zip(spans, acts)]
     cross_third = jnp.where(turn, third[1], third[0])
     cross_third = swap(after(cross_third, *early, *acts), "dp", "rot_third_dp")
 

time: 174 us -> 168 us (0.966)
  waiting for transfers between devices: 57.7 us -> 87.2 us
  Pallas kernels: 68.4 us -> 51.2 us
  starting transfers between devices: 36.4 us -> 26.9 us
  local copies, waits for them, and re-layouts: 10.3 us -> 2.42 us
    ppermute x15 -> x12, waiting for transfers between devices: 49.6 us -> 76.9 us  [hop(): return lax.ppermute(x, 'row', [hop[::-1] for hop in RING] if back else RING)]
    pallas_call x7, Pallas kernels: 41.1 us -> 31.1 us  [fold_block(): pl.pallas_call(functools.partial(fold_kernel, started, len(mine)), name=f...]
    ppermute x15 -> x12, starting transfers between devices: 25.7 us -> 16.7 us  [hop(): return lax.ppermute(x, 'row', [hop[::-1] for hop in RING] if back else RING)]
    unnamed x82 -> x2, local copies, waits for them, and re-layouts: 8.3 us -> 0.01 us
    pallas_call x2, Pallas kernels: 5.66 us -> 2.27 us  [masked_windows(): pl.pallas_call(functools.partial(mask_kernel, examples, window, place_at)...]
    pallas_call x2, Pallas kernels: 16.4 us -> 13.7 us  [squared_sums(): pl.pallas_call(functools.partial(square_kernel, chunks, examples, window,...]
    ppermute x20 -> x16, waiting for transfers between devices: 8.07 us -> 10.3 us  [swap(): return lax.ppermute(x, axis, [(0, 1), (1, 0)])]
    ppermute x20 -> x16, starting transfers between devices: 10.7 us -> 10.2 us  [swap(): return lax.ppermute(x, axis, [(0, 1), (1, 0)])]
  transfers between devices with their start and end apart: 35 -> 28, of which waited for: 16 -> 11; matrix products, arithmetic and copies ran while one was open for 0% -> 0% of each run, Pallas kernels for 35% -> 26%
where the time goes in v5:
time: 168 us
  waiting for transfers between devices  87.2 us (52%)
  Pallas kernels  51.2 us (30%)
  starting transfers between devices  26.9 us (16%)
  local copies, waits for them, and re-layouts  2.42 us (1%)
    ppermute x12, waiting for transfers between devices, hop(): return lax.ppermute(x, 'row', [hop[::-1] for hop in RING] if back else RING)  76.9 us
    pallas_call x7, Pallas kernels, fold_block(): pl.pallas_call(functools.partial(fold_kernel, started, len(mine)), name=f...  31.1 us
    ppermute x12, starting transfers between devices, hop(): return lax.ppermute(x, 'row', [hop[::-1] for hop in RING] if back else RING)  16.7 us
    pallas_call x2, Pallas kernels, squared_sums(): pl.pallas_call(functools.partial(square_kernel, chunks, examples, window,...  13.7 us
    ppermute x16, waiting for transfers between devices, swap(): return lax.ppermute(x, axis, [(0, 1), (1, 0)])  10.3 us
    ppermute x16, starting transfers between devices, swap(): return lax.ppermute(x, axis, [(0, 1), (1, 0)])  10.2 us
    pallas_call x1, Pallas kernels, project(): pl.pallas_call(functools.partial(project_kernel, tops, steps), name='proj...  4.2 us
  transfers between devices with their start and end apart: 28, of which 11 were waited for; matrix products, arithmetic and copies ran while one was open for 0% of the time, Pallas kernels for 26%

profile of v5, /device:TPU:0, one launch (start us, length us, event | category | flops | bytes accessed | tf_op | source)
XLA Modules:
  0.0 168.3 jit_solution(15359274249685037001)
XLA Ops:
  0.0 1.0 fusion.1
  1.0 1.3 fusion
  2.3 0.0 copy-start
  2.3 0.1 pad_maximum_fusion.refs_0_
  2.4 0.5 collective-permute-start.1
  3.0 0.1 collective-permute-start.2
  3.1 3.0 %collective-permute-start.4 = (bf16[160,2304]{1,0:T(8,128)(2,1)S(1)}, bf16[160,2304]{1,0:T(8,128)(2,1)}, u32[]{:S(2)}, u32[]{:S(2)}) collective-permute-start(bf16[160,2304]{1,0:T(8,128)(2,1)S(1)} %pad_maximum_fusion.1.refs_1_), channel_id=1, source_target_pairs={{0,4},{4,12},{12,8},{8,0},{1,5},{5,13},{13,9},{9,1},{2,6},{6,14},{... | collective-permute-start | bytes 2211848 | tf_op jit(solution)/shard_map/tokens_first_1/ppermute | solution.py:236
  6.1 2.6 %collective-permute-start.3 = (bf16[160,2304]{1,0:T(8,128)(2,1)S(1)}, bf16[160,2304]{1,0:T(8,128)(2,1)}, u32[]{:S(2)}, u32[]{:S(2)}) collective-permute-start(bf16[160,2304]{1,0:T(8,128)(2,1)S(1)} %pad_maximum_fusion.refs_0_), channel_id=1, source_target_pairs={{0,4},{4,12},{12,8},{8,0},{1,5},{5,13},{13,9},{9,1},{2,6},{6,14},{... | collective-permute-start | bytes 2211848 | tf_op jit(solution)/shard_map/tokens_first_0/ppermute | solution.py:236
  8.7 1.5 collective-permute-start
  10.2 0.1 stack.59.offsets_ref.plan_ref
  10.3 0.0 collective-permute-done.1.refs_2_
  10.3 5.2 %fold_0.1 = (f32[160,896]{1,0:T(8,128)S(1)}, f32[160,896]{1,0:T(8,128)S(1)}) custom-call(s32[14]{0:T(128)S(1)} %stack.59.offsets_ref.plan_ref, bf16[160,2304]{1,0:T(8,128)(2,1)S(1)} %pad_maximum_fusion.refs_0_, bf16[160,2304]{1,0:T(8,128)(2,1)S(1)} %pad_maximum_fusion.1.refs_1_, bf16[160,2304]{1,0:T(8,128)(2,1)S(1)} %collective-permute-done.1.refs_2_, ...), custom_call_target="tpu_custom_call" | custom-call | tf_op jit(solution)/shard_map/fold_0/pallas_call | solution.py:172
  15.5 0.0 collective-permute-done.lengths_ref.refs_1_
  15.6 9.0 %collective-permute-done.4.refs_1_.refs_5_ = bf16[160,2304]{1,0:T(8,128)(2,1)} collective-permute-done((bf16[160,2304]{1,0:T(8,128)(2,1)S(1)}, bf16[160,2304]{1,0:T(8,128)(2,1)}, u32[]{:S(2)}, u32[]{:S(2)}) %collective-permute-start.4) | collective-permute-done | bytes 737312 | tf_op jit(solution)/shard_map/tokens_first_1/ppermute | solution.py:236
  24.5 1.0 collective-permute-start.8
  25.6 14.7 %collective-permute-done.3.refs_1_.refs_4_ = bf16[160,2304]{1,0:T(8,128)(2,1)} collective-permute-done((bf16[160,2304]{1,0:T(8,128)(2,1)S(1)}, bf16[160,2304]{1,0:T(8,128)(2,1)}, u32[]{:S(2)}, u32[]{:S(2)}) %collective-permute-start.3) | collective-permute-done | bytes 737312 | tf_op jit(solution)/shard_map/tokens_first_0/ppermute | solution.py:236
  40.3 1.0 collective-permute-start.7
  41.4 0.0 collective-permute-done.6.refs_2_.refs_7_
  41.4 4.4 %fold_1.3.refs_0_ = f32[160,896]{1,0:T(8,128)S(1)} custom-call(s32[14]{0:T(128)S(1)} %stack.59.offsets_ref.plan_ref, f32[160,896]{1,0:T(8,128)S(1)} %get-tuple-element.20.refs_0_, bf16[160,2304]{1,0:T(8,128)(2,1)} %collective-permute-done.4.refs_1_.refs_5_, bf16[160,2304]{1,0:T(8,128)(2,1)S(1)} %collective-permute-done.6.refs_2_.refs_7_, ...), custom_call_target="tpu_custom_call" | custom-call | tf_op jit(solution)/shard_map/fold_1/pallas_call | solution.py:172
  45.8 10.2 %collective-permute-done.8.refs_1_.refs_9_ = bf16[160,2304]{1,0:T(8,128)(2,1)S(1)} collective-permute-done((bf16[160,2304]{1,0:T(8,128)(2,1)}, bf16[160,2304]{1,0:T(8,128)(2,1)S(1)}, u32[]{:S(2)}, u32[]{:S(2)}) %collective-permute-start.8) | collective-permute-done | bytes 737312 | tf_op jit(solution)/shard_map/tokens_second_1/ppermute | solution.py:236
  56.0 0.0 collective-permute-start.10
  56.0 1.3 collective-permute-start.12
  57.3 0.0 collective-permute-done.5.refs_2_.refs_6_
  57.3 4.4 %fold_1.2.refs_0_ = f32[160,896]{1,0:T(8,128)S(1)} custom-call(s32[14]{0:T(128)S(1)} %stack.59.offsets_ref.plan_ref, f32[160,896]{1,0:T(8,128)S(1)} %get-tuple-element.18.refs_0_, bf16[160,2304]{1,0:T(8,128)(2,1)} %collective-permute-done.3.refs_1_.refs_4_, bf16[160,2304]{1,0:T(8,128)(2,1)S(1)} %collective-permute-done.5.refs_2_.refs_6_, ...), custom_call_target="tpu_custom_call" | custom-call | tf_op jit(solution)/shard_map/fold_1/pallas_call | solution.py:172
  61.7 10.1 %collective-permute-done.7.refs_1_.refs_8_ = bf16[160,2304]{1,0:T(8,128)(2,1)S(1)} collective-permute-done((bf16[160,2304]{1,0:T(8,128)(2,1)}, bf16[160,2304]{1,0:T(8,128)(2,1)S(1)}, u32[]{:S(2)}, u32[]{:S(2)}) %collective-permute-start.7) | collective-permute-done | bytes 737312 | tf_op jit(solution)/shard_map/tokens_second_0/ppermute | solution.py:236
  71.8 0.0 collective-permute-start.9
  71.8 1.3 collective-permute-start.11
  73.1 0.0 collective-permute-done.10.refs_2_.refs_11_
  73.1 4.3 %fold_2.3.refs_0_ = f32[160,896]{1,0:T(8,128)S(1)} custom-call(s32[14]{0:T(128)S(1)} %stack.59.offsets_ref.plan_ref, f32[160,896]{1,0:T(8,128)S(1)} %fold_1.3.refs_0_, bf16[160,2304]{1,0:T(8,128)(2,1)S(1)} %collective-permute-done.8.refs_1_.refs_9_, bf16[160,2304]{1,0:T(8,128)(2,1)S(1)} %collective-permute-done.10.refs_2_.refs_11_, bf16[14336,896]{1,0:T(8,128)(2,1)} %bitcast.18), custom_call_target="tpu_custom_call" | custom-call | tf_op jit(solution)/shard_map/fold_2/pallas_call | solution.py:172
  77.3 10.3 %collective-permute-done.12.refs_1_.refs_13_ = bf16[160,2304]{1,0:T(8,128)(2,1)S(1)} collective-permute-done((bf16[160,2304]{1,0:T(8,128)(2,1)S(1)}, bf16[160,2304]{1,0:T(8,128)(2,1)S(1)}, u32[]{:S(2)}, u32[]{:S(2)}) %collective-permute-start.12) | collective-permute-done | bytes 737312 | tf_op jit(solution)/shard_map/tokens_third_1/ppermute | solution.py:236
  87.6 0.0 collective-permute-start.14
  87.6 0.0 collective-permute-done.9.refs_2_.refs_10_
  87.6 4.3 %fold_2.2.refs_0_ = f32[160,896]{1,0:T(8,128)S(1)} custom-call(s32[14]{0:T(128)S(1)} %stack.59.offsets_ref.plan_ref, f32[160,896]{1,0:T(8,128)S(1)} %fold_1.2.refs_0_, bf16[160,2304]{1,0:T(8,128)(2,1)S(1)} %collective-permute-done.7.refs_1_.refs_8_, bf16[160,2304]{1,0:T(8,128)(2,1)S(1)} %collective-permute-done.9.refs_2_.refs_10_, bf16[14336,896]{1,0:T(8,128)(2,1)} %bitcast.19), custom_call_target="tpu_custom_call" | custom-call | tf_op jit(solution)/shard_map/fold_2/pallas_call | solution.py:172
  91.9 11.0 %collective-permute-done.11.refs_1_.refs_12_ = bf16[160,2304]{1,0:T(8,128)(2,1)S(1)} collective-permute-done((bf16[160,2304]{1,0:T(8,128)(2,1)S(1)}, bf16[160,2304]{1,0:T(8,128)(2,1)S(1)}, u32[]{:S(2)}, u32[]{:S(2)}) %collective-permute-start.11) | collective-permute-done | bytes 737312 | tf_op jit(solution)/shard_map/tokens_third_0/ppermute | solution.py:236
  102.9 4.3 %fold_3.3.refs_6_ = bf16[160,896]{1,0:T(8,128)(2,1)S(1)} custom-call(s32[14]{0:T(128)S(1)} %stack.59.offsets_ref.plan_ref, f32[160,896]{1,0:T(8,128)S(1)} %fold_2.3.refs_0_, bf16[160,2304]{1,0:T(8,128)(2,1)S(1)} %collective-permute-done.12.refs_1_.refs_13_, bf16[160,2304]{1,0:T(8,128)(2,1)S(1)} %collective-permute-done.14.refs_2_.refs_15_, ...), custom_call_target="tpu_custom_call" | custom-call | tf_op jit(solution)/shard_map/fold_3/pallas_call | solution.py:172
  107.1 1.8 %collective-permute-start.20 = (bf16[160,896]{1,0:T(8,128)(2,1)S(1)}, bf16[160,896]{1,0:T(8,128)(2,1)S(1)}, u32[]{:S(2)}, u32[]{:S(2)}) collective-permute-start(bf16[160,896]{1,0:T(8,128)(2,1)S(1)} %fold_3.3.refs_6_), channel_id=1, source_target_pairs={{4,0},{12,4},{8,12},{0,8},{5,1},{13,5},{9,13},{1,9},{6,2},{14,6},{... | collective-permute-start | bytes 860168 | tf_op jit(solution)/shard_map/rot_first_1/ppermute | solution.py:236
  108.9 4.3 %fold_3.2.refs_4_ = bf16[160,896]{1,0:T(8,128)(2,1)S(1)} custom-call(s32[14]{0:T(128)S(1)} %stack.59.offsets_ref.plan_ref, f32[160,896]{1,0:T(8,128)S(1)} %fold_2.2.refs_0_, bf16[160,2304]{1,0:T(8,128)(2,1)S(1)} %collective-permute-done.11.refs_1_.refs_12_, bf16[160,2304]{1,0:T(8,128)(2,1)S(1)} %collective-permute-done.13.refs_2_.refs_14_, ...), custom_call_target="tpu_custom_call" | custom-call | tf_op jit(solution)/shard_map/fold_3/pallas_call | solution.py:172
  113.2 0.5 collective-permute-start.18
  113.7 2.7 %collective-permute-done.20.refs_6_ = bf16[160,896]{1,0:T(8,128)(2,1)S(1)} collective-permute-done((bf16[160,896]{1,0:T(8,128)(2,1)S(1)}, bf16[160,896]{1,0:T(8,128)(2,1)S(1)}, u32[]{:S(2)}, u32[]{:S(2)}) %collective-permute-start.20) | collective-permute-done | bytes 286752 | tf_op jit(solution)/shard_map/rot_first_1/ppermute | solution.py:236
  116.4 3.0 %collective-permute-start.21 = (bf16[160,896]{1,0:T(8,128)(2,1)S(1)}, bf16[160,896]{1,0:T(8,128)(2,1)S(1)}, u32[]{:S(2)}, u32[]{:S(2)}) collective-permute-start(bf16[160,896]{1,0:T(8,128)(2,1)S(1)} %collective-permute-done.20.refs_6_), channel_id=1, source_target_pairs={{4,0},{12,4},{8,12},{0,8},{5,1},{13,5},{9,13},{1,9},{6,2},{14,6},{... | collective-permute-start | bytes 860168 | tf_op jit(solution)/shard_map/rot_second_1/ppermute | solution.py:236
  119.4 4.2 %project.1.mine_ref = bf16[320,512]{1,0:T(8,128)(2,1)S(1)} custom-call(s32[14]{0:T(128)S(1)} %stack.59.offsets_ref.plan_ref, bf16[160,2304]{1,0:T(8,128)(2,1)S(1)} %pad_maximum_fusion.refs_0_, bf16[160,2304]{1,0:T(8,128)(2,1)S(1)} %pad_maximum_fusion.1.refs_1_, bf16[160,2304]{1,0:T(8,128)(2,1)S(1)} %collective-permute-done.1.refs_2_, ...), custom_call_target="tpu_custom_call" | custom-call | tf_op jit(solution)/shard_map/project/pallas_call | solution.py:214
  123.7 1.6 collective-permute-start.16
  125.2 0.0 collective-permute-done.18.refs_4_
  125.2 1.4 collective-permute-start.23
  126.6 0.0 collective-permute-start.19
  126.6 4.7 %collective-permute-done.21.refs_7_ = bf16[160,896]{1,0:T(8,128)(2,1)S(1)} collective-permute-done((bf16[160,896]{1,0:T(8,128)(2,1)S(1)}, bf16[160,896]{1,0:T(8,128)(2,1)S(1)}, u32[]{:S(2)}, u32[]{:S(2)}) %collective-permute-start.21) | collective-permute-done | bytes 286752 | tf_op jit(solution)/shard_map/rot_second_1/ppermute | solution.py:236
  131.4 2.5 %collective-permute-start.24 = (bf16[160,896]{1,0:T(8,128)(2,1)S(1)}, bf16[160,896]{1,0:T(8,128)(2,1)S(1)}, u32[]{:S(2)}, u32[]{:S(2)}) collective-permute-start(bf16[160,896]{1,0:T(8,128)(2,1)S(1)} %broadcast_select_fusion.1), channel_id=1, source_target_pairs={{0,1},{1,0},{2,3},{3,2},{4,5},{5,4},{6,7},{7,6},{8,9},{9,8},{10,11... | collective-permute-start | bytes 860168 | tf_op jit(solution)/shard_map/rot_second_dp_1/ppermute | solution.py:241
  133.9 0.5 collective-permute-start.22
  134.4 0.0 collective-permute-done.16.mine_ref
  134.4 0.0 collective-permute-start.15
  134.4 6.1 %collective-permute-done.23.refs_8_.refs_10_ = bf16[160,896]{1,0:T(8,128)(2,1)S(1)} collective-permute-done((bf16[160,896]{1,0:T(8,128)(2,1)S(1)}, bf16[160,896]{1,0:T(8,128)(2,1)S(1)}, u32[]{:S(2)}, u32[]{:S(2)}) %collective-permute-start.23) | collective-permute-done | bytes 286752 | tf_op jit(solution)/shard_map/rot_first_dp/ppermute | solution.py:241
  140.5 0.0 collective-permute-start.17
  140.5 0.0 collective-permute-done.19.refs_5_
  140.5 4.2 %collective-permute-done.24.refs_9_ = bf16[160,896]{1,0:T(8,128)(2,1)S(1)} collective-permute-done((bf16[160,896]{1,0:T(8,128)(2,1)S(1)}, bf16[160,896]{1,0:T(8,128)(2,1)S(1)}, u32[]{:S(2)}, u32[]{:S(2)}) %collective-permute-start.24) | collective-permute-done | bytes 286752 | tf_op jit(solution)/shard_map/rot_second_dp_1/ppermute | solution.py:241
  144.7 0.0 collective-permute-done.22.refs_7_
  144.7 0.7 collective-permute-start.25
  145.4 1.2 collective-permute-start.26
  146.6 0.0 collective-permute-done.15.theirs_ref
  146.6 1.1 masked_windows.2.refs_2_
  147.8 1.1 masked_windows.3.refs_3_
  148.9 4.1 %collective-permute-done.25.refs_5_ = bf16[160,896]{1,0:T(8,128)(2,1)S(1)} collective-permute-done((bf16[160,896]{1,0:T(8,128)(2,1)S(1)}, bf16[160,896]{1,0:T(8,128)(2,1)S(1)}, u32[]{:S(2)}, u32[]{:S(2)}) %collective-permute-start.25) | collective-permute-done | bytes 286752 | tf_op jit(solution)/shard_map/rot_third_0/ppermute | solution.py:236
  153.1 1.4 collective-permute-start.27
  154.5 6.8 %squared_sums.2.refs_12_ = f32[1024,1792]{1,0:T(8,128)} custom-call(s32[14]{0:T(128)S(1)} %stack.59.offsets_ref.plan_ref, s32[1,3]{1,0:T(1,128)S(1)} %copy-done, s32[1,3]{1,0:T(1,128)S(1)} %collective-permute-done.lengths_ref.refs_1_, bf16[3,1024,256]{2,1,0:T(8,128)(2,1)S(1)} %masked_windows.2.refs_2_, bf16[3,1024,256]{2,1,0:T(8,128)(2,1)S(1)} %masked_windows.3.refs_3_, ...), custom_call_target="tpu_custom_call" | custom-call | tf_op jit(solution)/shard_map/squared_sums/pallas_call | solution.py:126
  161.3 6.9 %squared_sums.3 = f32[1024,1792]{1,0:T(8,128)} custom-call(s32[14]{0:T(128)S(1)} %stack.59.offsets_ref.plan_ref, s32[1,3]{1,0:T(1,128)S(1)} %copy-done, s32[1,3]{1,0:T(1,128)S(1)} %collective-permute-done.lengths_ref.refs_1_, bf16[3,1024,256]{2,1,0:T(8,128)(2,1)S(1)} %masked_windows.2.refs_2_, ...), custom_call_target="tpu_custom_call", output_to_operand_aliasing={{}: (13, {})} | custom-call | tf_op jit(solution)/shard_map/squared_sums/pallas_call | solution.py:126
  (15 shorter events, 0.2 us)
Async XLA Ops:
  2.3 6.4 %copy-start = (s32[1,3]{1,0:T(1,128)S(1)}, s32[1,3]{1,0:T(1,128)}, u32[]{:S(2)}) copy-start(s32[1,3]{1,0:T(1,128)} %refs_0_.3) | copy-start | bytes 40
  2.4 7.9 %collective-permute-start.1 = (bf16[160,2304]{1,0:T(8,128)(2,1)S(1)}, bf16[160,2304]{1,0:T(8,128)(2,1)S(1)}, u32[]{:S(2)}, u32[]{:S(2)}) collective-permute-start(bf16[160,2304]{1,0:T(8,128)(2,1)S(1)} %pad_maximum_fusion.refs_0_), channel_id=1, source_target_pairs={{0,2},{2,0},{1,3},{3,1},{4,6},{6,4},{5,7},{7,5},{8,10},{10,8},{9,1... | collective-permute-start | bytes 2211848 | tf_op jit(solution)/shard_map/tokens_0_cols_0/ppermute | solution.py:241
  3.0 7.3 %collective-permute-start.2 = (bf16[160,2304]{1,0:T(8,128)(2,1)S(1)}, bf16[160,2304]{1,0:T(8,128)(2,1)S(1)}, u32[]{:S(2)}, u32[]{:S(2)}) collective-permute-start(bf16[160,2304]{1,0:T(8,128)(2,1)S(1)} %pad_maximum_fusion.1.refs_1_), channel_id=1, source_target_pairs={{0,2},{2,0},{1,3},{3,1},{4,6},{6,4},{5,7},{7,5},{8,10},{10,8},{9,1... | collective-permute-start | bytes 2211848 | tf_op jit(solution)/shard_map/tokens_0_cols_1/ppermute | solution.py:241
  3.1 21.4 %collective-permute-start.4 = (bf16[160,2304]{1,0:T(8,128)(2,1)S(1)}, bf16[160,2304]{1,0:T(8,128)(2,1)}, u32[]{:S(2)}, u32[]{:S(2)}) collective-permute-start(bf16[160,2304]{1,0:T(8,128)(2,1)S(1)} %pad_maximum_fusion.1.refs_1_), channel_id=1, source_target_pairs={{0,4},{4,12},{12,8},{8,0},{1,5},{5,13},{13,9},{9,1},{2,6},{6,14},{... | collective-permute-start | bytes 2211848 | tf_op jit(solution)/shard_map/tokens_first_1/ppermute | solution.py:236
  6.1 34.2 %collective-permute-start.3 = (bf16[160,2304]{1,0:T(8,128)(2,1)S(1)}, bf16[160,2304]{1,0:T(8,128)(2,1)}, u32[]{:S(2)}, u32[]{:S(2)}) collective-permute-start(bf16[160,2304]{1,0:T(8,128)(2,1)S(1)} %pad_maximum_fusion.refs_0_), channel_id=1, source_target_pairs={{0,4},{4,12},{12,8},{8,0},{1,5},{5,13},{13,9},{9,1},{2,6},{6,14},{... | collective-permute-start | bytes 2211848 | tf_op jit(solution)/shard_map/tokens_first_0/ppermute | solution.py:236
  8.7 6.8 %collective-permute-start = (s32[1,3]{1,0:T(1,128)S(1)}, s32[1,3]{1,0:T(1,128)S(1)}, u32[]{:S(2)}, u32[]{:S(2)}) collective-permute-start(s32[1,3]{1,0:T(1,128)S(1)} %copy-done), channel_id=1, source_target_pairs={{0,1},{1,0},{2,3},{3,2},{4,5},{5,4},{6,7},{7,6},{8,9},{9,8},{10,11... | collective-permute-start | bytes 44 | tf_op jit(solution)/shard_map/lengths_dp/ppermute | solution.py:241
  24.5 16.9 %collective-permute-start.6 = (bf16[160,2304]{1,0:T(8,128)(2,1)}, bf16[160,2304]{1,0:T(8,128)(2,1)S(1)}, u32[]{:S(2)}, u32[]{:S(2)}) collective-permute-start(bf16[160,2304]{1,0:T(8,128)(2,1)} %collective-permute-done.4.refs_1_.refs_5_), channel_id=1, source_target_pairs={{0,2},{2,0},{1,3},{3,1},{4,6},{6,4},{5,7},{7,5},{8,10},{10,8},{9,1... | collective-permute-start | bytes 2211848 | tf_op jit(solution)/shard_map/tokens_1_cols_1/ppermute | solution.py:241
  24.5 31.5 %collective-permute-start.8 = (bf16[160,2304]{1,0:T(8,128)(2,1)}, bf16[160,2304]{1,0:T(8,128)(2,1)S(1)}, u32[]{:S(2)}, u32[]{:S(2)}) collective-permute-start(bf16[160,2304]{1,0:T(8,128)(2,1)} %collective-permute-done.4.refs_1_.refs_5_), channel_id=1, source_target_pairs={{0,4},{4,12},{12,8},{8,0},{1,5},{5,13},{13,9},{9,1},{2,6},{6,14},{... | collective-permute-start | bytes 2211848 | tf_op jit(solution)/shard_map/tokens_second_1/ppermute | solution.py:236
  40.3 17.0 %collective-permute-start.5 = (bf16[160,2304]{1,0:T(8,128)(2,1)}, bf16[160,2304]{1,0:T(8,128)(2,1)S(1)}, u32[]{:S(2)}, u32[]{:S(2)}) collective-permute-start(bf16[160,2304]{1,0:T(8,128)(2,1)} %collective-permute-done.3.refs_1_.refs_4_), channel_id=1, source_target_pairs={{0,2},{2,0},{1,3},{3,1},{4,6},{6,4},{5,7},{7,5},{8,10},{10,8},{9,1... | collective-permute-start | bytes 2211848 | tf_op jit(solution)/shard_map/tokens_1_cols_0/ppermute | solution.py:241
  40.3 31.5 %collective-permute-start.7 = (bf16[160,2304]{1,0:T(8,128)(2,1)}, bf16[160,2304]{1,0:T(8,128)(2,1)S(1)}, u32[]{:S(2)}, u32[]{:S(2)}) collective-permute-start(bf16[160,2304]{1,0:T(8,128)(2,1)} %collective-permute-done.3.refs_1_.refs_4_), channel_id=1, source_target_pairs={{0,4},{4,12},{12,8},{8,0},{1,5},{5,13},{13,9},{9,1},{2,6},{6,14},{... | collective-permute-start | bytes 2211848 | tf_op jit(solution)/shard_map/tokens_second_0/ppermute | solution.py:236
  56.0 17.1 %collective-permute-start.10 = (bf16[160,2304]{1,0:T(8,128)(2,1)S(1)}, bf16[160,2304]{1,0:T(8,128)(2,1)S(1)}, u32[]{:S(2)}, u32[]{:S(2)}) collective-permute-start(bf16[160,2304]{1,0:T(8,128)(2,1)S(1)} %collective-permute-done.8.refs_1_.refs_9_), channel_id=1, source_target_pairs={{0,2},{2,0},{1,3},{3,1},{4,6},{6,4},{5,7},{7,5},{8,10},{10,8},{9,1... | collective-permute-start | bytes 2211848 | tf_op jit(solution)/shard_map/tokens_2_cols_1/ppermute | solution.py:241
  56.0 31.6 %collective-permute-start.12 = (bf16[160,2304]{1,0:T(8,128)(2,1)S(1)}, bf16[160,2304]{1,0:T(8,128)(2,1)S(1)}, u32[]{:S(2)}, u32[]{:S(2)}) collective-permute-start(bf16[160,2304]{1,0:T(8,128)(2,1)S(1)} %collective-permute-done.8.refs_1_.refs_9_), channel_id=1, source_target_pairs={{0,4},{4,12},{12,8},{8,0},{1,5},{5,13},{13,9},{9,1},{2,6},{6,14},{... | collective-permute-start | bytes 2211848 | tf_op jit(solution)/shard_map/tokens_third_1/ppermute | solution.py:236
  71.8 15.8 %collective-permute-start.9 = (bf16[160,2304]{1,0:T(8,128)(2,1)S(1)}, bf16[160,2304]{1,0:T(8,128)(2,1)S(1)}, u32[]{:S(2)}, u32[]{:S(2)}) collective-permute-start(bf16[160,2304]{1,0:T(8,128)(2,1)S(1)} %collective-permute-done.7.refs_1_.refs_8_), channel_id=1, source_target_pairs={{0,2},{2,0},{1,3},{3,1},{4,6},{6,4},{5,7},{7,5},{8,10},{10,8},{9,1... | collective-permute-start | bytes 2211848 | tf_op jit(solution)/shard_map/tokens_2_cols_0/ppermute | solution.py:241
  71.8 31.0 %collective-permute-start.11 = (bf16[160,2304]{1,0:T(8,128)(2,1)S(1)}, bf16[160,2304]{1,0:T(8,128)(2,1)S(1)}, u32[]{:S(2)}, u32[]{:S(2)}) collective-permute-start(bf16[160,2304]{1,0:T(8,128)(2,1)S(1)} %collective-permute-done.7.refs_1_.refs_8_), channel_id=1, source_target_pairs={{0,4},{4,12},{12,8},{8,0},{1,5},{5,13},{13,9},{9,1},{2,6},{6,14},{... | collective-permute-start | bytes 2211848 | tf_op jit(solution)/shard_map/tokens_third_0/ppermute | solution.py:236
  87.6 15.2 %collective-permute-start.14 = (bf16[160,2304]{1,0:T(8,128)(2,1)S(1)}, bf16[160,2304]{1,0:T(8,128)(2,1)S(1)}, u32[]{:S(2)}, u32[]{:S(2)}) collective-permute-start(bf16[160,2304]{1,0:T(8,128)(2,1)S(1)} %collective-permute-done.12.refs_1_.refs_13_), channel_id=1, source_target_pairs={{0,2},{2,0},{1,3},{3,1},{4,6},{6,4},{5,7},{7,5},{8,10},{10,8},{9,1... | collective-permute-start | bytes 2211848 | tf_op jit(solution)/shard_map/tokens_3_cols_1/ppermute | solution.py:241
  102.9 6.1 %collective-permute-start.13 = (bf16[160,2304]{1,0:T(8,128)(2,1)S(1)}, bf16[160,2304]{1,0:T(8,128)(2,1)S(1)}, u32[]{:S(2)}, u32[]{:S(2)}) collective-permute-start(bf16[160,2304]{1,0:T(8,128)(2,1)S(1)} %collective-permute-done.11.refs_1_.refs_12_), channel_id=1, source_target_pairs={{0,2},{2,0},{1,3},{3,1},{4,6},{6,4},{5,7},{7,5},{8,10},{10,8},{9,1... | collective-permute-start | bytes 2211848 | tf_op jit(solution)/shard_map/tokens_3_cols_0/ppermute | solution.py:241
  107.1 9.3 %collective-permute-start.20 = (bf16[160,896]{1,0:T(8,128)(2,1)S(1)}, bf16[160,896]{1,0:T(8,128)(2,1)S(1)}, u32[]{:S(2)}, u32[]{:S(2)}) collective-permute-start(bf16[160,896]{1,0:T(8,128)(2,1)S(1)} %fold_3.3.refs_6_), channel_id=1, source_target_pairs={{4,0},{12,4},{8,12},{0,8},{5,1},{13,5},{9,13},{1,9},{6,2},{14,6},{... | collective-permute-start | bytes 860168 | tf_op jit(solution)/shard_map/rot_first_1/ppermute | solution.py:236
  113.2 12.0 %collective-permute-start.18 = (bf16[160,896]{1,0:T(8,128)(2,1)S(1)}, bf16[160,896]{1,0:T(8,128)(2,1)S(1)}, u32[]{:S(2)}, u32[]{:S(2)}) collective-permute-start(bf16[160,896]{1,0:T(8,128)(2,1)S(1)} %fold_3.2.refs_4_), channel_id=1, source_target_pairs={{0,4},{4,12},{12,8},{8,0},{1,5},{5,13},{13,9},{9,1},{2,6},{6,14},{... | collective-permute-start | bytes 860168 | tf_op jit(solution)/shard_map/rot_first_0/ppermute | solution.py:236
  116.4 15.0 %collective-permute-start.21 = (bf16[160,896]{1,0:T(8,128)(2,1)S(1)}, bf16[160,896]{1,0:T(8,128)(2,1)S(1)}, u32[]{:S(2)}, u32[]{:S(2)}) collective-permute-start(bf16[160,896]{1,0:T(8,128)(2,1)S(1)} %collective-permute-done.20.refs_6_), channel_id=1, source_target_pairs={{4,0},{12,4},{8,12},{0,8},{5,1},{13,5},{9,13},{1,9},{6,2},{14,6},{... | collective-permute-start | bytes 860168 | tf_op jit(solution)/shard_map/rot_second_1/ppermute | solution.py:236
  123.7 10.8 %collective-permute-start.16 = (bf16[320,512]{1,0:T(8,128)(2,1)S(1)}, bf16[320,512]{1,0:T(8,128)(2,1)S(1)}, u32[]{:S(2)}, u32[]{:S(2)}) collective-permute-start(bf16[320,512]{1,0:T(8,128)(2,1)S(1)} %project.1.mine_ref), channel_id=1, source_target_pairs={{0,1},{1,0},{2,3},{3,2},{4,5},{5,4},{6,7},{7,6},{8,9},{9,8},{10,11... | collective-permute-start | bytes 983048 | tf_op jit(solution)/shard_map/act_dp/ppermute | solution.py:241
  125.2 15.3 %collective-permute-start.23 = (bf16[160,896]{1,0:T(8,128)(2,1)S(1)}, bf16[160,896]{1,0:T(8,128)(2,1)S(1)}, u32[]{:S(2)}, u32[]{:S(2)}) collective-permute-start(bf16[160,896]{1,0:T(8,128)(2,1)S(1)} %broadcast_select_fusion.3), channel_id=1, source_target_pairs={{0,1},{1,0},{2,3},{3,2},{4,5},{5,4},{6,7},{7,6},{8,9},{9,8},{10,11... | collective-permute-start | bytes 860168 | tf_op jit(solution)/shard_map/rot_first_dp/ppermute | solution.py:241
  126.6 13.9 %collective-permute-start.19 = (bf16[160,896]{1,0:T(8,128)(2,1)S(1)}, bf16[160,896]{1,0:T(8,128)(2,1)S(1)}, u32[]{:S(2)}, u32[]{:S(2)}) collective-permute-start(bf16[160,896]{1,0:T(8,128)(2,1)S(1)} %collective-permute-done.18.refs_4_), channel_id=1, source_target_pairs={{0,4},{4,12},{12,8},{8,0},{1,5},{5,13},{13,9},{9,1},{2,6},{6,14},{... | collective-permute-start | bytes 860168 | tf_op jit(solution)/shard_map/rot_second_0/ppermute | solution.py:236
  131.4 13.3 %collective-permute-start.24 = (bf16[160,896]{1,0:T(8,128)(2,1)S(1)}, bf16[160,896]{1,0:T(8,128)(2,1)S(1)}, u32[]{:S(2)}, u32[]{:S(2)}) collective-permute-start(bf16[160,896]{1,0:T(8,128)(2,1)S(1)} %broadcast_select_fusion.1), channel_id=1, source_target_pairs={{0,1},{1,0},{2,3},{3,2},{4,5},{5,4},{6,7},{7,6},{8,9},{9,8},{10,11... | collective-permute-start | bytes 860168 | tf_op jit(solution)/shard_map/rot_second_dp_1/ppermute | solution.py:241
  133.9 10.8 %collective-permute-start.22 = (bf16[160,896]{1,0:T(8,128)(2,1)S(1)}, bf16[160,896]{1,0:T(8,128)(2,1)S(1)}, u32[]{:S(2)}, u32[]{:S(2)}) collective-permute-start(bf16[160,896]{1,0:T(8,128)(2,1)S(1)} %collective-permute-done.21.refs_7_), channel_id=1, source_target_pairs={{4,0},{12,4},{8,12},{0,8},{5,1},{13,5},{9,13},{1,9},{6,2},{14,6},{... | collective-permute-start | bytes 860168 | tf_op jit(solution)/shard_map/rot_third_1/ppermute | solution.py:236
  134.4 12.2 %collective-permute-start.15 = (bf16[320,512]{1,0:T(8,128)(2,1)S(1)}, bf16[320,512]{1,0:T(8,128)(2,1)S(1)}, u32[]{:S(2)}, u32[]{:S(2)}) collective-permute-start(bf16[320,512]{1,0:T(8,128)(2,1)S(1)} %project.1.mine_ref), channel_id=1, source_target_pairs={{0,2},{2,0},{1,3},{3,1},{4,6},{6,4},{5,7},{7,5},{8,10},{10,8},{9,1... | collective-permute-start | bytes 983048 | tf_op jit(solution)/shard_map/rot_act_cols/ppermute | solution.py:241
  140.5 7.2 %collective-permute-start.17 = (bf16[320,512]{1,0:T(8,128)(2,1)S(1)}, bf16[320,512]{1,0:T(8,128)(2,1)S(1)}, u32[]{:S(2)}, u32[]{:S(2)}) collective-permute-start(bf16[320,512]{1,0:T(8,128)(2,1)S(1)} %collective-permute-done.16.mine_ref), channel_id=1, source_target_pairs={{0,2},{2,0},{1,3},{3,1},{4,6},{6,4},{5,7},{7,5},{8,10},{10,8},{9,1... | collective-permute-start | bytes 983048 | tf_op jit(solution)/shard_map/rot_act_cols/ppermute | solution.py:241
  144.7 8.3 %collective-permute-start.25 = (bf16[160,896]{1,0:T(8,128)(2,1)S(1)}, bf16[160,896]{1,0:T(8,128)(2,1)S(1)}, u32[]{:S(2)}, u32[]{:S(2)}) collective-permute-start(bf16[160,896]{1,0:T(8,128)(2,1)S(1)} %collective-permute-done.19.refs_5_), channel_id=1, source_target_pairs={{0,4},{4,12},{12,8},{8,0},{1,5},{5,13},{13,9},{9,1},{2,6},{6,14},{... | collective-permute-start | bytes 860168 | tf_op jit(solution)/shard_map/rot_third_0/ppermute | solution.py:236
  145.4 7.7 %collective-permute-start.26 = (bf16[160,896]{1,0:T(8,128)(2,1)S(1)}, bf16[160,896]{1,0:T(8,128)(2,1)S(1)}, u32[]{:S(2)}, u32[]{:S(2)}) collective-permute-start(bf16[160,896]{1,0:T(8,128)(2,1)S(1)} %broadcast_select_fusion), channel_id=1, source_target_pairs={{0,1},{1,0},{2,3},{3,2},{4,5},{5,4},{6,7},{7,6},{8,9},{9,8},{10,11... | collective-permute-start | bytes 860168 | tf_op jit(solution)/shard_map/rot_second_dp_0/ppermute | solution.py:241
  153.1 8.2 %collective-permute-start.27 = (bf16[160,896]{1,0:T(8,128)(2,1)S(1)}, bf16[160,896]{1,0:T(8,128)(2,1)S(1)}, u32[]{:S(2)}, u32[]{:S(2)}) collective-permute-start(bf16[160,896]{1,0:T(8,128)(2,1)S(1)} %broadcast_select_fusion.2), channel_id=1, source_target_pairs={{0,1},{1,0},{2,3},{3,2},{4,5},{5,4},{6,7},{7,6},{8,9},{9,8},{10,11... | collective-permute-start | bytes 860168 | tf_op jit(solution)/shard_map/rot_third_dp/ppermute | solution.py:241
